TPU v7x, 32 devices: a whole 2x2x4 slice. The times are simulated.
32 devices in a mesh: fsdp: 8 (over z, x), dp: 4 (over y, core).
Axes of the slice: x: 2, y: 2, z: 4, core: 2. Of those that a mesh axis runs over, the one named last changes fastest.
Arguments:
- tokens: bfloat16 [16384, 768], P(('fsdp', 'dp')), may hold values from -6 to 6
- cotangent: bfloat16 [16384, 768], P(('fsdp', 'dp')), may hold values from -6 to 6
- seq_lens: int32 [32, 4], P(('fsdp', 'dp')), may hold values from 0 to 512, as said below
- routes: int32 [16384, 1], P(('fsdp', 'dp')), may hold values from 0 to 7; in each aligned block of 512 rows (0 to 511, 512 to 1023, ...) at most 128 rows name the same one
- norm_gains: bfloat16 [2, 768], P(None, ('fsdp', 'dp')), may hold values from 0.5 to 1.5
- qkv_weight: bfloat16 [768, 2304], P(('fsdp', 'dp')), may hold values from -0.21875 to 0.21875
- out_weight: bfloat16 [768, 768], P(('fsdp', 'dp')), may hold values from -0.875 to 0.875
- router_weight: bfloat16 [768, 8], P(('fsdp', 'dp')), may hold values from -0.15625 to 0.15625
- rel_bias: float32 [32, 12], replicated, may hold values from -4 to 4
- expert_in: bfloat16 [8, 768, 3072], P('dp', None, 'fsdp'), may hold values from -0.21875 to 0.21875
- expert_out: bfloat16 [8, 3072, 768], P('dp', 'fsdp'), may hold values from -0.875 to 0.875
Outputs:
- mixed: bfloat16 [16384, 768], P(('fsdp', 'dp'))
- tokens_grad: float32 [16384, 768], P(('fsdp', 'dp'))
- gains_grad: float32 [2, 768], P(None, ('fsdp', 'dp'))
- qkv_grad: float32 [768, 2304], P(('fsdp', 'dp'))
- out_grad: float32 [768, 768], P(('fsdp', 'dp'))
- router_grad: float32 [768, 8], P(('fsdp', 'dp'))
- bias_grad: float32 [32, 12], replicated
- expert_in_grad: float32 [8, 768, 3072], P('dp', None, 'fsdp')
- expert_out_grad: float32 [8, 3072, 768], P('dp', 'fsdp')
Inputs may be any that keep to these rules, and one draw needn't show every extreme that they name: `seq_lens`: row b lists the sequences of block b in order from its first slot; a row sums to 256 or more and to 512 or less; some row is one sequence of 512. `routes`: among the 512 rows of one device no expert is named more than 128 times.
All inputs are finite; a program needn't handle non-finite values.
Results may differ from a plain program's by a relative error of at most 0.015.
Values may be sent and summed in bfloat16 or wider, within the bound.
No kernel may reach another device: no remote copies, remote signals or barrier semaphores. Data moves between devices by JAX's collectives and lax.ppermute only.
A program may use at most 192 MiB of HBM per device.

v0:
```python
from functools import reduce

import jax
import jax.numpy as jnp
from jax import lax
from jax.sharding import PartitionSpec as P

HEADS = 12
HEAD_DIM = 64


EPS = 1e-06
LIMITS = (12, 16, 23, 32, 46, 64, 91)
SCALE = 0.125
HIGH = lax.Precision.HIGHEST
LOW = jnp.bfloat16
FULL = jnp.float32


def bucket_index(relative):
    distance = jnp.abs(relative)
    far_bucket = reduce(
        lambda counted, boundary: counted + (distance >= boundary).astype(jnp.int32),
        LIMITS,
        jnp.full_like(distance, 8),
    )
    return jnp.where(distance < 8, distance, far_bucket) + 16 * (relative > 0).astype(jnp.int32)


def segment_ids(lengths, slots):
    ending = jnp.cumsum(lengths)
    places = jnp.arange(slots, dtype=jnp.int32)
    return jnp.sum((places[:, None] >= ending[None, :]).astype(jnp.int32), axis=1)


def rms_parts(values, gain):
    inverse = lax.rsqrt(jnp.mean(values * values, axis=-1, keepdims=True) + EPS)
    return (values * inverse * gain, inverse)


def norm_back(values, inverse, gain, upstream):
    scaled = upstream * gain
    grad_values = inverse * scaled - values * inverse * inverse * inverse * jnp.mean(
        values * scaled, axis=-1, keepdims=True
    )
    return (grad_values, jnp.sum(upstream * values * inverse, axis=0))


def gelu_slope(values):
    normal_cdf = 0.5 * (1.0 + lax.erf(values * 0.7071067811865476))
    return normal_cdf + values * jnp.exp(-0.5 * values * values) * 0.3989422804014327


def softmax_rows(scores):
    highest = jnp.max(scores, axis=-1, keepdims=True)
    raised = jnp.exp(scores - highest)
    return raised / jnp.sum(raised, axis=-1, keepdims=True)


def pair_scores(queries, keys_in, bias_pair, allowed):
    scores = (
        jnp.einsum("qgd,kgd->gqk", queries, keys_in, preferred_element_type=FULL) * SCALE
        + bias_pair
    )
    return jnp.where(allowed[None], scores, -1e30)


def attend_forward(queries, keys_in, values_in, bias_pairs, allowed):

    def one_pair(parts):
        query_pair, key_pair, value_pair, bias_pair = parts
        scores = pair_scores(query_pair, key_pair, bias_pair, allowed)
        highest = jnp.max(scores, axis=-1, keepdims=True)
        raised = jnp.exp(scores - highest)
        summed = jnp.sum(raised, axis=-1, keepdims=True)
        soft_low = (raised / summed).astype(LOW)
        result = jnp.einsum("gqk,kgd->qgd", soft_low, value_pair, preferred_element_type=FULL)
        return (result.astype(LOW), (highest + jnp.log(summed))[..., 0])

    return lax.map(one_pair, (queries, keys_in, values_in, bias_pairs))


def attend_back(queries, keys_in, values_in, grad_heads, log_totals, bias_pairs, allowed):

    def one_pair(parts):
        query_pair, key_pair, value_pair, grad_pair, total_pair, bias_pair = parts
        scores = pair_scores(query_pair, key_pair, bias_pair, allowed)
        soft = jnp.exp(scores - total_pair[..., None])
        soft_low = soft.astype(LOW)
        grad_value = jnp.einsum("gqk,qgd->kgd", soft_low, grad_pair, preferred_element_type=FULL)
        grad_soft = jnp.einsum("qgd,kgd->gqk", grad_pair, value_pair, preferred_element_type=FULL)
        grad_scores = soft * (grad_soft - jnp.sum(grad_soft * soft, axis=-1, keepdims=True))
        scores_low = grad_scores.astype(LOW)
        grad_query = (
            jnp.einsum("gqk,kgd->qgd", scores_low, key_pair, preferred_element_type=FULL) * SCALE
        )
        grad_key = (
            jnp.einsum("gqk,qgd->kgd", scores_low, query_pair, preferred_element_type=FULL) * SCALE
        )
        return (grad_query, grad_key, grad_value, scores_low)

    return lax.map(one_pair, (queries, keys_in, values_in, grad_heads, log_totals, bias_pairs))


def expert_forward(parts):
    expert_rows, w_first, w_second = parts
    pre_act = jnp.dot(expert_rows, w_first, preferred_element_type=FULL)
    hidden = jax.nn.gelu(pre_act, approximate=False).astype(LOW)
    return jnp.dot(hidden, w_second, preferred_element_type=FULL).astype(LOW)


def expert_backward(parts):
    expert_rows, grad_out_rows, w_first, w_second = parts
    pre_act = jnp.dot(expert_rows, w_first, preferred_element_type=FULL)
    hidden = jax.nn.gelu(pre_act, approximate=False).astype(LOW)
    grad_hidden = jnp.einsum("rd,fd->rf", grad_out_rows, w_second, preferred_element_type=FULL)
    grad_second = jnp.einsum("rf,rd->fd", hidden, grad_out_rows, preferred_element_type=FULL)
    grad_pre = (grad_hidden * gelu_slope(pre_act)).astype(LOW)
    grad_first = jnp.einsum("rd,rf->df", expert_rows, grad_pre, preferred_element_type=FULL)
    grad_rows = jnp.einsum("rf,df->rd", grad_pre, w_first, preferred_element_type=FULL).astype(LOW)
    first_shard, second_shard = (
        lax.psum_scatter(
            grad_first.astype(jnp.bfloat16), "fsdp", scatter_dimension=1, tiled=True
        ).astype(jnp.float32),
        lax.psum_scatter(
            grad_second.astype(jnp.bfloat16), "fsdp", scatter_dimension=0, tiled=True
        ).astype(jnp.float32),
    )
    return (grad_rows, first_shard, second_shard)


def body(
    tokens,
    cotangent,
    seq_lens,
    routes,
    norm_gains,
    qkv_weight,
    out_weight,
    router_weight,
    rel_bias,
    expert_in,
    expert_out,
):
    tok_count = tokens.shape[0]
    model_width = tokens.shape[1]
    bucket_count = rel_bias.shape[0]
    dense_full = (
        lax.all_gather(qkv_weight, ("fsdp", "dp"), axis=0, tiled=True),
        lax.all_gather(out_weight, ("fsdp", "dp"), axis=0, tiled=True),
        lax.all_gather(router_weight, ("fsdp", "dp"), axis=0, tiled=True),
        lax.all_gather(norm_gains, ("fsdp", "dp"), axis=1, tiled=True),
    )
    qkv_full, out_full, router_full, gains_full = dense_full
    gains_float = gains_full.astype(FULL)
    inputs = tokens.astype(FULL)
    normed_one, inverse_one = rms_parts(inputs, gains_float[0])
    normed_low = normed_one.astype(LOW)
    projected = jnp.dot(normed_low, qkv_full, preferred_element_type=FULL).astype(LOW)
    split_heads = projected.reshape(tok_count, 3, HEADS // 2, 2, HEAD_DIM).transpose(1, 2, 0, 3, 4)
    queries, keys_in, values_in = (split_heads[0], split_heads[1], split_heads[2])
    segment = segment_ids(seq_lens[0], tok_count)
    allowed = segment[:, None] == segment[None, :]
    places = jnp.arange(tok_count, dtype=jnp.int32)
    bucket_map = bucket_index(places[None, :] - places[:, None])
    bias_table = rel_bias.T
    zero_bias = jnp.zeros((rel_bias.shape[1], tok_count, tok_count), FULL)
    bias_all = reduce(
        lambda total, number: total
        + jnp.where(bucket_map[None] == number, bias_table[:, number][:, None, None], 0.0),
        range(bucket_count),
        zero_bias,
    )
    bias_pairs = bias_all.reshape(HEADS // 2, 2, tok_count, tok_count)
    attended, log_totals = attend_forward(queries, keys_in, values_in, bias_pairs, allowed)
    attended_flat = attended.transpose(1, 0, 2, 3).reshape(tok_count, model_width)
    hidden_one = inputs + jnp.dot(attended_flat, out_full, preferred_element_type=FULL)
    normed_two, inverse_two = rms_parts(hidden_one, gains_float[1])
    normed_two_low = normed_two.astype(LOW)
    router_soft = softmax_rows(jnp.dot(normed_two_low, router_full, preferred_element_type=FULL))
    experts_all = router_full.shape[1]
    chosen = routes[:, 0]
    chosen_hot = chosen[:, None] == jnp.arange(experts_all, dtype=jnp.int32)[None, :]
    gate_value = jnp.sum(jnp.where(chosen_hot, router_soft, 0.0), axis=1)
    capacity = 2 * tok_count // experts_all
    ranked = chosen_hot.astype(jnp.int32)
    rank_in = jnp.sum((jnp.cumsum(ranked, axis=0) - ranked) * ranked, axis=1)
    slot_index = chosen * capacity + rank_in
    peer_count = lax.axis_size("dp")
    local_experts = experts_all // peer_count

    def to_buffer(values):
        flat = jnp.zeros((experts_all * capacity, model_width), LOW).at[slot_index].set(values)
        return flat.reshape(peer_count, local_experts, capacity, model_width)

    def to_rows(buffer):
        return buffer.transpose(1, 0, 2, 3).reshape(
            local_experts, peer_count * capacity, model_width
        )

    def from_rows(expert_values):
        return expert_values.reshape(local_experts, peer_count, capacity, model_width).transpose(
            1, 0, 2, 3
        )

    def from_buffer(buffer):
        return buffer.reshape(experts_all * capacity, model_width)[slot_index]

    received = lax.all_to_all(
        to_buffer(normed_two_low), "dp", split_axis=0, concat_axis=0, tiled=True
    )
    expert_full = (
        lax.all_gather(expert_in, "fsdp", axis=2, tiled=True),
        lax.all_gather(expert_out, "fsdp", axis=1, tiled=True),
    )
    expert_rows = to_rows(received)
    expert_y = lax.map(expert_forward, (expert_rows, expert_full[0], expert_full[1]))
    returned = lax.all_to_all(from_rows(expert_y), "dp", split_axis=0, concat_axis=0, tiled=True)
    token_y = from_buffer(returned).astype(FULL)
    mixed = (hidden_one + gate_value[:, None] * token_y).astype(LOW)
    upstream = cotangent.astype(FULL)
    grad_y = (gate_value[:, None] * upstream).astype(LOW)
    grad_gate = jnp.sum(upstream * token_y, axis=1)
    grad_logits = router_soft * (
        jnp.where(chosen_hot, grad_gate[:, None], 0.0) - (gate_value * grad_gate)[:, None]
    )
    router_local = jnp.dot(normed_two_low.astype(FULL).T, grad_logits, precision=HIGH)
    dense_back = (
        lax.all_gather(qkv_weight, ("fsdp", "dp"), axis=0, tiled=True),
        lax.all_gather(out_weight, ("fsdp", "dp"), axis=0, tiled=True),
        lax.all_gather(router_weight, ("fsdp", "dp"), axis=0, tiled=True),
        lax.all_gather(norm_gains, ("fsdp", "dp"), axis=1, tiled=True),
    )
    expert_back = (
        lax.all_gather(expert_in, "fsdp", axis=2, tiled=True),
        lax.all_gather(expert_out, "fsdp", axis=1, tiled=True),
    )
    qkv_back, out_back, router_back, gains_back = dense_back
    grad_received = lax.all_to_all(to_buffer(grad_y), "dp", split_axis=0, concat_axis=0, tiled=True)
    grad_rows, in_grad, out_expert_grad = lax.map(
        expert_backward, (expert_rows, to_rows(grad_received), expert_back[0], expert_back[1])
    )
    grad_returned = lax.all_to_all(
        from_rows(grad_rows), "dp", split_axis=0, concat_axis=0, tiled=True
    )
    grad_normed_two = from_buffer(grad_returned).astype(FULL) + jnp.dot(
        grad_logits, router_back.astype(FULL).T, precision=HIGH
    )
    gains_back_float = gains_back.astype(FULL)
    grad_from_two, gain_grad_two = norm_back(
        hidden_one, inverse_two, gains_back_float[1], grad_normed_two
    )
    grad_hidden_one = upstream + grad_from_two
    grad_attn_low = grad_hidden_one.astype(LOW)
    out_local = jnp.einsum("td,te->de", attended_flat, grad_attn_low, preferred_element_type=FULL)
    grad_attended = jnp.dot(grad_attn_low, out_back.T, preferred_element_type=FULL).astype(LOW)
    grad_heads = grad_attended.reshape(tok_count, HEADS // 2, 2, HEAD_DIM).transpose(1, 0, 2, 3)
    grad_query, grad_key, grad_value, grad_score_pairs = attend_back(
        queries, keys_in, values_in, grad_heads, log_totals, bias_pairs, allowed
    )
    grad_projected = (
        jnp.stack((grad_query, grad_key, grad_value))
        .transpose(2, 0, 1, 3, 4)
        .reshape(tok_count, 3 * model_width)
        .astype(LOW)
    )
    qkv_local = jnp.einsum("td,te->de", normed_low, grad_projected, preferred_element_type=FULL)
    grad_normed_one = jnp.dot(grad_projected, qkv_back.T, preferred_element_type=FULL)
    grad_from_one, gain_grad_one = norm_back(
        inputs, inverse_one, gains_back_float[0], grad_normed_one
    )
    tokens_grad = grad_hidden_one + grad_from_one
    bucket_hot = (
        bucket_map[:, :, None] == jnp.arange(bucket_count, dtype=jnp.int32)[None, None, :]
    ).astype(LOW)
    grad_score_all = grad_score_pairs.reshape(HEADS, tok_count, tok_count)
    bias_local = jnp.einsum("hqk,qkb->bh", grad_score_all, bucket_hot, preferred_element_type=FULL)
    gains_local = jnp.stack((gain_grad_one, gain_grad_two))
    gains_grad, qkv_grad, out_grad, router_grad = (
        lax.psum_scatter(gains_local, ("fsdp", "dp"), scatter_dimension=1, tiled=True),
        lax.psum_scatter(qkv_local, ("fsdp", "dp"), scatter_dimension=0, tiled=True),
        lax.psum_scatter(out_local, ("fsdp", "dp"), scatter_dimension=0, tiled=True),
        lax.psum_scatter(router_local, ("fsdp", "dp"), scatter_dimension=0, tiled=True),
    )
    bias_grad = lax.psum(bias_local, ("fsdp", "dp"))
    return (
        mixed,
        tokens_grad,
        gains_grad,
        qkv_grad,
        out_grad,
        router_grad,
        bias_grad,
        in_grad,
        out_expert_grad,
    )


def solution(mesh):
    placed = (
        P(("fsdp", "dp"), None),
        P(("fsdp", "dp"), None),
        P(("fsdp", "dp"), None),
        P(("fsdp", "dp"), None),
        P(None, ("fsdp", "dp")),
        P(("fsdp", "dp"), None),
        P(("fsdp", "dp"), None),
        P(("fsdp", "dp"), None),
        P(),
        P("dp", None, "fsdp"),
        P("dp", "fsdp", None),
    )
    return jax.shard_map(
        body,
        mesh=mesh,
        in_specs=placed,
        out_specs=(
            P(("fsdp", "dp"), None),
            P(("fsdp", "dp"), None),
            P(None, ("fsdp", "dp")),
            P(("fsdp", "dp"), None),
            P(("fsdp", "dp"), None),
            P(("fsdp", "dp"), None),
            P(),
            P("dp", None, "fsdp"),
            P("dp", "fsdp", None),
        ),
        check_vma=False,
    )
```

profile of v0, /device:TPU:0, one launch (start us, length us, event | category | flops | bytes accessed | tf_op | source)
XLA Modules:
  0.0 1171.6 jit_solution(8290868526856896158)
XLA Ops:
  32.1 43.3 %all-gather = bf16[32,24,2]{1,2,0:T(2,128)(2,1)S(1)} all-gather(bf16[1,24,2]{1,2,0:T(2,128)(2,1)S(1)} %bitcast.339), channel_id=1, replica_groups=mesh['fsdp'=8,'dp'=4] {'fsdp','dp'}, dimensions={0}, use_global_device_ids=true | all-gather | bytes 3168 | tf_op jit(solution)/shard_map/all_gather | solution.py:152
  92.1 48.6 %select_add_fusion = f32[6,2,512,512]{2,3,1,0:T(8,128)} fusion(f32[6,2]{1,0:T(8,128)S(1)} %broadcast_in_dim.673, f32[6,2]{1,0:T(8,128)S(1)} %broadcast_in_dim.670, f32[6,2]{1,0:T(8,128)S(1)} %broadcast_in_dim.667, f32[6,2]{1,0:T(8,128)S(1)} %broadcast_in_dim.664, f32[6,2]{1,0:T(8,128)S(1)} %broadcast_in_dim.661, f32[6,2]{1,0:T(8,128)S(1)} %broadcast_in_dim.658, ...), kind=kLoop, calls=%fused_computation.239 | loop fusion | flops 198180864 | bytes 20973056 | tf_op jit(solution)/shard_map/add | solution.py:169
  149.2 27.5 %while.56 = (s32[]{:T(128)}, bf16[6,512,2,64]{1,3,2,0:T(8,128)(2,1)}, f32[6,2,512]{2,1,0:T(2,128)}, bf16[6,512,2,64]{1,3,2,0:T(8,128)(2,1)S(1)}, bf16[6,512,2,64...) while((s32[]{:T(128)}, ...), condition=%wide.region_6.7_spmd.clone, body=%wide.region_3.6_spmd.clone.sunk | while | flops 139262976 | bytes 9474665 | solution.py:80
  188.9 50.0 %all-gather.1 = bf16[32,24,8]{1,2,0:T(8,128)(2,1)S(1)} all-gather(bf16[1,24,8]{1,2,0:T(8,128)(2,1)S(1)} %bitcast.338), channel_id=1, replica_groups=mesh['fsdp'=8,'dp'=4] {'fsdp','dp'}, dimensions={0}, use_global_device_ids=true | all-gather | bytes 12672 | tf_op jit(solution)/shard_map/all_gather | solution.py:151
  250.8 17.4 %all-to-all-done.2 = bf16[4,2,128,768]{3,2,1,0:T(8,128)(2,1)S(1)} async-done(((bf16[4,2,128,768]{3,2,1,0:T(8,128)(2,1)}), bf16[4,2,128,768]{3,2,1,0:T(8,128)(2,1)S(1)}, u32[]{:S(2)}, u32[]{:S(2)}) %all-to-all-start.2) | async-done | bytes 1572896 | tf_op jit(solution)/shard_map/all_to_all | solution.py:239
  269.5 138.1 %all-gather.13.cloned.1.call-done = bf16[2,3072,768]{2,1,0:T(8,128)(2,1)} async-done(((bf16[2,384,768]{2,1,0:T(8,128)(2,1)}), bf16[2,3072,768]{2,1,0:T(8,128)(2,1)}) %all-gather.13.cloned.1.call-update) | async-done | bytes 9437200 | tf_op jit(solution)/shard_map/all_gather | solution.py:214
  407.8 53.5 %while.54 = (s32[]{:T(128)}, bf16[2,512,768]{2,1,0:T(8,128)(2,1)S(1)}, bf16[2,512,768]{2,1,0:T(8,128)(2,1)}, bf16[2,768,3072]{2,1,0:T(8,128)(2,1)}, bf16[2,3072,768]{2,1,0:T(8,128)(2,1)}, /*index=5*/s32[]{:T(128)}) while((s32[]{:T(128)}, bf16[2,512,768]{2,1,0:T(8,128)(2,1)S(1)}, bf16[2,512,768]{2,1,0:T(8,128)(2,1)}, ...), condition=%wide.region_16.17_spmd, body=%wide.region_15.16_spmd.sunk | while | flops 4934467584 | bytes 11012173 | solution.py:217
  419.4 20.7 %fusion.344 = bf16[2,512,768]{2,1,0:T(8,128)(2,1)S(1)} fusion(bf16[2,512,768]{2,1,0:T(8,128)(2,1)S(1)} %get-tuple-element.648, s32[]{:T(128)S(6)} %copy.136, bf16[2,3072,768]{2,1,0:T(8,128)(2,1)} %get-tuple-element.657, bf16[2,768,3072]{2,1,0:T(8,128)(2,1)} %get-tuple-element.656, bf16[2,512,768]{2,1,0:T(8,128)(2,1)} %get-tuple-element.655), kind=kOutput, calls=%fused_computation.62.clone.1 | convolution fusion | flops 4934467584 | bytes 11012096 | tf_op jit(solution)/shard_map/while/body/eval_jaxpr/dot_general | solution.py:109
  440.1 20.7 %fusion.344 = bf16[2,512,768]{2,1,0:T(8,128)(2,1)S(1)} fusion(bf16[2,512,768]{2,1,0:T(8,128)(2,1)S(1)} %get-tuple-element.648, s32[]{:T(128)S(6)} %copy.136, bf16[2,3072,768]{2,1,0:T(8,128)(2,1)} %get-tuple-element.657, bf16[2,768,3072]{2,1,0:T(8,128)(2,1)} %get-tuple-element.656, bf16[2,512,768]{2,1,0:T(8,128)(2,1)} %get-tuple-element.655), kind=kOutput, calls=%fused_computation.62.clone.1 | convolution fusion | flops 4934467584 | bytes 11012096 | tf_op jit(solution)/shard_map/while/body/eval_jaxpr/dot_general | solution.py:109
  467.0 436.6 %while.55 = (s32[]{:T(128)}, bf16[2,512,768]{2,1,0:T(8,128)(2,1)S(1)}, f32[2,768,384]{2,1,0:T(8,128)}, f32[2,384,768]{2,1,0:T(8,128)}, bf16[2,512,768]{2,1,0:T(8...) while((s32[]{:T(128)}, ...), condition=%wide.region_21.22_spmd, body=%wide.region_18.21_spmd.sunk | while | flops 12203261952 | bytes 189926768 | solution.py:240
  467.0 4.8 fusion.355
  478.8 4.4 convolution_convert_fusion.7
  483.2 6.7 copy.113
  489.9 18.6 %convolution_convert_fusion.8 = bf16[3072,768]{1,0:T(8,128)(2,1)} fusion(f32[512,3072]{1,0:T(8,128)} %copy-done.41, bf16[2,512,768]{2,1,0:T(8,128)(2,1)} %get-tuple-element.681, s32[]{:T(128)S(6)} %copy.144), kind=kOutput, calls=%fused_computation.122.clone.1 | convolution fusion | flops 2520514560 | bytes 11796484 | tf_op jit(solution)/shard_map/while/body/eval_jaxpr/rf,rd->fd/dot_general | solution.py:117
  508.5 6.0 fusion.357
  514.5 69.4 %reduce-scatter.15.cloned.1.call-done = bf16[384,768]{1,0:T(8,128)(2,1)} async-done(((bf16[3072,768]{1,0:T(8,128)(2,1)}), bf16[384,768]{1,0:T(8,128)(2,1)}) %reduce-scatter.15.cloned.1.call-update) | async-done | bytes 589840 | tf_op jit(solution)/shard_map/while
  586.4 96.1 %reduce-scatter.17.cloned.1.call-done = bf16[384,768]{1,0:T(8,128)(2,1)} async-done(((bf16[3072,768]{1,0:T(8,128)(2,1)}), bf16[384,768]{1,0:T(8,128)(2,1)}) %reduce-scatter.17.cloned.1.call-update) | async-done | bytes 589840 | tf_op jit(solution)/shard_map/while/body/eval_jaxpr/reduce_scatter | solution.py:125
  684.6 4.8 fusion.355
  696.4 4.4 convolution_convert_fusion.7
  700.8 6.7 copy.113
  707.5 18.6 %convolution_convert_fusion.8 = bf16[3072,768]{1,0:T(8,128)(2,1)} fusion(f32[512,3072]{1,0:T(8,128)} %copy-done.41, bf16[2,512,768]{2,1,0:T(8,128)(2,1)} %get-tuple-element.681, s32[]{:T(128)S(6)} %copy.144), kind=kOutput, calls=%fused_computation.122.clone.1 | convolution fusion | flops 2520514560 | bytes 11796484 | tf_op jit(solution)/shard_map/while/body/eval_jaxpr/rf,rd->fd/dot_general | solution.py:117
  726.1 6.0 fusion.357
  732.1 70.7 %reduce-scatter.15.cloned.1.call-done = bf16[384,768]{1,0:T(8,128)(2,1)} async-done(((bf16[3072,768]{1,0:T(8,128)(2,1)}), bf16[384,768]{1,0:T(8,128)(2,1)}) %reduce-scatter.15.cloned.1.call-update) | async-done | bytes 589840 | tf_op jit(solution)/shard_map/while
  805.2 96.2 %reduce-scatter.17.cloned.1.call-done = bf16[384,768]{1,0:T(8,128)(2,1)} async-done(((bf16[3072,768]{1,0:T(8,128)(2,1)}), bf16[384,768]{1,0:T(8,128)(2,1)}) %reduce-scatter.17.cloned.1.call-update) | async-done | bytes 589840 | tf_op jit(solution)/shard_map/while/body/eval_jaxpr/reduce_scatter | solution.py:125
  908.8 5.0 gather_fusion
  915.4 13.2 %all-to-all-done.3 = bf16[4,2,128,768]{3,2,1,0:T(8,128)(2,1)S(1)} async-done(((bf16[4,2,128,768]{3,2,1,0:T(8,128)(2,1)}), bf16[4,2,128,768]{3,2,1,0:T(8,128)(2,1)S(1)}, u32[]{:S(2)}, u32[]{:S(2)}) %all-to-all-start.3) | async-done | bytes 1572896 | tf_op jit(solution)/shard_map/all_to_all | solution.py:243
  941.5 68.8 %while.57 = (s32[]{:T(128)}, bf16[6,512,2,64]{1,3,2,0:T(8,128)(2,1)}, bf16[6,512,2,64]{1,3,2,0:T(8,128)(2,1)}, bf16[6,512,2,64]{1,3,2,0:T(8,128)(2,1)}, bf16[6,2...) while((s32[]{:T(128)}, ...), condition=%wide.region_26.27_spmd.clone, body=%wide.region_24.26_spmd.clone.sunk | while | flops 341179392 | bytes 21130892 | solution.py:102
  1013.6 5.2 fusion.267
  1019.2 6.3 fusion.244
  1026.0 8.1 fusion.245
  1034.1 40.6 %all-reduce.2 = (f32[2,768]{1,0:T(2,128)S(1)}, f32[768,8]{0,1:T(8,128)S(1)}, f32[32,12]{0,1:T(8,128)}) all-reduce(f32[2,768]{1,0:T(2,128)S(1)} %pad_maximum_fusion.1, f32[768,8]{0,1:T(8,128)S(1)} %fusion.275, f32[32,12]{0,1:T(8,128)S(1)} %fusion.245), channel_id=4, replica_groups=mesh['fsdp'=8,'dp'=4] {'fsdp','dp'}, use_global_device_ids=true, to_apply=%region_30.31.clone | all-reduce | flops 8064 | bytes 64512
  1079.2 85.4 %reduce-scatter.11.cloned.1.call-done = f32[24,2304]{1,0:T(8,128)} async-done(((f32[768,2304]{1,0:T(8,128)}), f32[24,2304]{1,0:T(8,128)}) %reduce-scatter.11.cloned.1.call-update) | async-done | bytes 221200 | tf_op jit(solution)/shard_map/reduce_scatter | solution.py:281
  (329 shorter events, 228.2 us)
Async XLA Ops:
  7.2 24.9 %copy-start.39 = (bf16[2,24]{1,0:T(2,128)(2,1)S(1)}, bf16[2,24]{1,0:T(2,128)(2,1)}, u32[]{:S(2)}) copy-start(bf16[2,24]{1,0:T(2,128)(2,1)} %param.23) | copy-start | bytes 292
  7.2 68.5 %copy-start.8 = (bf16[512,768]{1,0:T(8,128)(2,1)S(1)}, bf16[512,768]{1,0:T(8,128)(2,1)}, u32[]{:S(2)}) copy-start(bf16[512,768]{1,0:T(8,128)(2,1)} %param.19) | copy-start | bytes 2359300
  7.2 83.4 %copy-start.24 = (s32[512,1]{0,1:T(1,128)S(1)}, s32[512,1]{0,1:T(1,128)}, u32[]{:S(2)}) copy-start(s32[512,1]{0,1:T(1,128)} %param.22) | copy-start | bytes 6148
  7.2 133.5 %all-gather.7.cloned.1.call-start = ((), (), s32[]{:S(2)}) async-start(), calls=%async_computation.8 | async-start | bytes 3649536 | tf_op jit(solution)/shard_map/all_gather | solution.py:149
  7.9 168.8 %all-gather.9.cloned.1.call-start = ((), (), s32[]{:S(2)}) async-start(), calls=%async_computation.9 | async-start | bytes 1216512 | tf_op jit(solution)/shard_map/all_gather | solution.py:150
  8.7 260.8 %all-gather.11.cloned.1.call-start = ((), (), s32[]{:S(2)}) async-start(), calls=%async_computation.10 | async-start | bytes 10616832 | tf_op jit(solution)/shard_map/all_gather | solution.py:213
  9.4 398.2 %all-gather.13.cloned.1.call-start = ((), (), s32[]{:S(2)}) async-start(), calls=%async_computation.11 | async-start | bytes 10616832 | tf_op jit(solution)/shard_map/all_gather | solution.py:214
  75.7 65.0 %copy-start.18 = (f32[768]{0:T(1024)}, f32[768]{0:T(1024)S(1)}, u32[]{:S(2)}) copy-start(f32[768]{0:T(1024)S(1)} %get-tuple-element.281) | copy-start | bytes 9220
  75.7 163.3 %copy-start.22 = (f32[768]{0:T(1024)}, f32[768]{0:T(1024)S(1)}, u32[]{:S(2)}) copy-start(f32[768]{0:T(1024)S(1)} %get-tuple-element.280) | copy-start | bytes 9220
  76.0 64.7 %copy-start.32 = (f32[512]{0:T(512)}, f32[512]{0:T(512)S(1)}, u32[]{:S(2)}) copy-start(f32[512]{0:T(512)S(1)} %add_rsqrt_fusion.1) | copy-start | bytes 6148
  92.1 148.5 %copy-start.36 = (s32[512,1]{0,1:T(1,128)}, s32[512,1]{0,1:T(1,128)S(1)}, u32[]{:S(2)}) copy-start(s32[512,1]{0,1:T(1,128)S(1)} %compare_select_fusion.1) | copy-start | bytes 6148
  176.7 62.6 %copy-start.13 = (s32[512]{0:T(512)}, s32[512]{0:T(512)S(1)}, u32[]{:S(2)}) copy-start(s32[512]{0:T(512)S(1)} %get-tuple-element.758) | copy-start | bytes 6148
  178.1 62.5 %copy-start.5 = (bf16[512,768]{1,0:T(8,128)(2,1)S(1)}, bf16[512,768]{1,0:T(8,128)(2,1)}, u32[]{:S(2)}) copy-start(bf16[512,768]{1,0:T(8,128)(2,1)} %param.20) | copy-start | bytes 2359300
  180.6 63.9 %copy-start = (f32[512,768]{1,0:T(8,128)}, f32[512,768]{1,0:T(8,128)S(1)}, u32[]{:S(2)}) copy-start(f32[512,768]{1,0:T(8,128)S(1)} %get-tuple-element.363) | copy-start | bytes 4718596
  180.6 63.9 %copy-start.28 = (f32[512]{0:T(512)}, f32[512]{0:T(512)S(1)}, u32[]{:S(2)}) copy-start(f32[512]{0:T(512)S(1)} %add_rsqrt_fusion) | copy-start | bytes 6148
  184.5 60.0 %all-to-all-start = ((bf16[4,2,128,768]{3,2,1,0:T(8,128)(2,1)}), bf16[4,2,128,768]{3,2,1,0:T(8,128)(2,1)}, u32[]{:S(2)}, u32[]{:S(2)}) async-start(bf16[4,2,128,768]{3,2,1,0:T(8,128)(2,1)} %bitcast.315), calls=%async_computation.2 | async-start | bytes 3145728 | tf_op jit(solution)/shard_map/all_to_all | solution.py:209
  240.5 167.2 %copy-start.26 = (f32[512]{0:T(512)}, f32[512]{0:T(512)S(1)}, u32[]{:S(2)}) copy-start(f32[512]{0:T(512)S(1)} %get-tuple-element.364) | copy-start | bytes 6148
  240.5 167.2 %copy-start.30 = (f32[512]{0:T(512)}, f32[512]{0:T(512)S(1)}, u32[]{:S(2)}) copy-start(f32[512]{0:T(512)S(1)} %fusion.274) | copy-start | bytes 6148
  240.6 167.2 %copy-start.34 = (f32[512]{0:T(512)}, f32[512]{0:T(512)S(1)}, u32[]{:S(2)}) copy-start(f32[512]{0:T(512)S(1)} %select_reduce_fusion) | copy-start | bytes 6148
  244.6 23.6 %all-to-all-start.2 = ((bf16[4,2,128,768]{3,2,1,0:T(8,128)(2,1)}), bf16[4,2,128,768]{3,2,1,0:T(8,128)(2,1)S(1)}, u32[]{:S(2)}, u32[]{:S(2)}) async-start(bf16[4,2,128,768]{3,2,1,0:T(8,128)(2,1)} %bitcast.316), calls=%async_computation.4 | async-start | bytes 3145728 | tf_op jit(solution)/shard_map/all_to_all | solution.py:239
  462.5 442.4 %all-to-all-start.1 = ((bf16[4,2,128,768]{3,2,1,0:T(8,128)(2,1)}), bf16[4,2,128,768]{3,2,1,0:T(8,128)(2,1)}, u32[]{:S(2)}, u32[]{:S(2)}) async-start(bf16[4,2,128,768]{3,2,1,0:T(8,128)(2,1)} %bitcast.230), calls=%async_computation.3 | async-start | bytes 3145728 | tf_op jit(solution)/shard_map/all_to_all | solution.py:218
  467.0 116.9 %reduce-scatter.15.cloned.1.call-start = ((), (), s32[]{:S(2)}) async-start(), calls=%async_computation.14 | async-start | bytes 5308416 | tf_op jit(solution)/shard_map/while
  489.8 192.6 %reduce-scatter.17.cloned.1.call-start = ((), (), s32[]{:S(2)}) async-start(), calls=%async_computation.15 | async-start | bytes 5308416 | tf_op jit(solution)/shard_map/while/body/eval_jaxpr/reduce_scatter | solution.py:125
  684.6 118.2 %reduce-scatter.15.cloned.1.call-start = ((), (), s32[]{:S(2)}) async-start(), calls=%async_computation.14 | async-start | bytes 5308416 | tf_op jit(solution)/shard_map/while
  707.4 194.0 %reduce-scatter.17.cloned.1.call-start = ((), (), s32[]{:S(2)}) async-start(), calls=%async_computation.15 | async-start | bytes 5308416 | tf_op jit(solution)/shard_map/while/body/eval_jaxpr/reduce_scatter | solution.py:125
  904.8 23.7 %all-to-all-start.3 = ((bf16[4,2,128,768]{3,2,1,0:T(8,128)(2,1)}), bf16[4,2,128,768]{3,2,1,0:T(8,128)(2,1)S(1)}, u32[]{:S(2)}, u32[]{:S(2)}) async-start(bf16[4,2,128,768]{3,2,1,0:T(8,128)(2,1)} %bitcast.229), calls=%async_computation.5 | async-start | bytes 3145728 | tf_op jit(solution)/shard_map/all_to_all | solution.py:243
  908.5 170.6 %reduce-scatter.13.cloned.1.call-start = ((), (), s32[]{:S(2)}) async-start(), calls=%async_computation.13 | async-start | bytes 2433024 | tf_op jit(solution)/shard_map/reduce_scatter | solution.py:282
  908.7 22.7 %copy-start.1 = (f32[512,768]{1,0:T(8,128)S(1)}, f32[512,768]{1,0:T(8,128)}, u32[]{:S(2)}) copy-start(f32[512,768]{1,0:T(8,128)} %copy-done) | copy-start | bytes 4718596
  941.4 223.2 %reduce-scatter.11.cloned.1.call-start = ((), (), s32[]{:S(2)}) async-start(), calls=%async_computation.12 | async-start | bytes 7299072 | tf_op jit(solution)/shard_map/reduce_scatter | solution.py:281
  941.4 72.1 %copy-start.9 = (bf16[512,768]{1,0:T(8,128)(2,1)S(1)}, bf16[512,768]{1,0:T(8,128)(2,1)}, u32[]{:S(2)}) copy-start(bf16[512,768]{1,0:T(8,128)(2,1)} %param.19) | copy-start | bytes 2359300
  941.4 72.1 %copy-start.19 = (f32[768]{0:T(1024)S(1)}, f32[768]{0:T(1024)}, u32[]{:S(2)}) copy-start(f32[768]{0:T(1024)} %copy-done.18) | copy-start | bytes 9220
  941.4 72.1 %copy-start.33 = (f32[512]{0:T(512)S(1)}, f32[512]{0:T(512)}, u32[]{:S(2)}) copy-start(f32[512]{0:T(512)} %copy-done.32) | copy-start | bytes 6148
  (32 other events, 279.2 us)
Sparse Core Ops, SparseCore 0:
  11.0 62.8 all-gather.6
  76.8 52.9 all-gather.8
  131.8 137.3 all-gather.10
  271.3 136.2 all-gather.12
  490.0 93.9 reduce-scatter.14
  587.4 95.0 reduce-scatter.16
  707.6 95.1 reduce-scatter.14
  806.4 94.9 reduce-scatter.16
  941.5 97.9 reduce-scatter.12
  1046.5 118.0 reduce-scatter.10
where the time goes:
time: 1180 us; the launch traced here: 1170 us
  waiting for transfers between devices  589 us (50%)
  matrix products  226 us (19%)
  blocking collectives  134 us (11%)
  other arithmetic  111 us (9%)
  local copies, waits for them, and re-layouts  67.9 us (6%)
  starting transfers between devices  16.4 us (1%)
  between operations  15.1 us (1%)
  loops' own time  12.6 us (1%)
    reduce_scatter x2, waiting for transfers between devices, expert_backward(): lax.psum_scatter(grad_second.astype(jnp.bfloat16), 'fsdp', scatter_dimens...  192 us
    while x6, waiting for transfers between devices  140 us
    all_gather x1, waiting for transfers between devices, body(): lax.all_gather(expert_out, 'fsdp', axis=1, tiled=True)  138 us
    reduce_scatter x1, waiting for transfers between devices, body(): lax.psum_scatter(qkv_local, ('fsdp', 'dp'), scatter_dimension=0, tiled=True)  85.4 us
    all_gather x1, blocking collectives, body(): lax.all_gather(router_weight, ('fsdp', 'dp'), axis=0, tiled=True)  50 us
    add x1, other arithmetic, body(): total + jnp.where(bucket_map[None] == number, bias_table[:, number][:, No...  48.6 us
    all_gather x1, blocking collectives, body(): lax.all_gather(norm_gains, ('fsdp', 'dp'), axis=1, tiled=True)  43.3 us
    dot_general x2, matrix products, expert_forward(): return jnp.dot(hidden, w_second, preferred_element_type=FULL).astype(LOW)  41.4 us
  transfers between devices with their start and end apart: 14, of which 8 were waited for; matrix products, arithmetic and copies ran while one was open for 29% of the time, Pallas kernels for 0%

commit v1 on v0

v1 whole, which is shorter than its diff:
```python
from functools import partial, reduce

import jax
import jax.numpy as jnp
from jax import lax
from jax.experimental import pallas as pl
from jax.experimental.pallas import tpu as pltpu
from jax.sharding import PartitionSpec as P

HEADS = 12
HEAD_DIM = 64
EPS = 1e-06
LIMITS = (12, 16, 23, 32, 46, 64, 91)
SCALE = 0.125
HIGH = lax.Precision.HIGHEST
LOW = jnp.bfloat16
FULL = jnp.float32
ROWS = 128
VMEM_BYTES = 52 * 1024 * 1024


def bucket_index(relative):
    distance = jnp.abs(relative)
    far_bucket = reduce(
        lambda counted, boundary: counted + (distance >= boundary).astype(jnp.int32),
        LIMITS,
        jnp.full_like(distance, 8),
    )
    return jnp.where(distance < 8, distance, far_bucket) + 16 * (relative > 0).astype(jnp.int32)


def segment_ids(lengths, slots):
    ending = jnp.cumsum(lengths)
    places = jnp.arange(slots, dtype=jnp.int32)
    return jnp.sum((places[:, None] >= ending[None, :]).astype(jnp.int32), axis=1)


def rms_parts(values, gain):
    inverse = lax.rsqrt(jnp.mean(values * values, axis=-1, keepdims=True) + EPS)
    return (values * inverse * gain, inverse)


def norm_back(values, inverse, gain, upstream):
    scaled = upstream * gain
    grad_values = inverse * scaled - values * inverse * inverse * inverse * jnp.mean(
        values * scaled, axis=-1, keepdims=True
    )
    return (grad_values, jnp.sum(upstream * values * inverse, axis=0))


def softmax_rows(scores):
    highest = jnp.max(scores, axis=-1, keepdims=True)
    raised = jnp.exp(scores - highest)
    return raised / jnp.sum(raised, axis=-1, keepdims=True)


def mm(left, right, contract, out=FULL):
    return lax.dot_general(left, right, (contract, ((), ())), preferred_element_type=FULL).astype(
        out
    )


def swap(value, dim):
    axis, mask = dim
    count = lax.axis_size(axis)
    return lax.ppermute(value, axis, [(i, i ^ mask) for i in range(count)])


def bit_of(dim):
    axis, mask = dim
    return (lax.axis_index(axis) & mask) != 0


def stage_pair(value, dim):
    other = swap(value, dim)
    return jnp.where(bit_of(dim), jnp.stack((other, value)), jnp.stack((value, other)))


def line_shift(value, places, first, last, by):
    pairs = []
    for place in range(first, last + 1):
        if 0 <= place + by < places:
            pairs += [(2 * place, 2 * (place + by)), (2 * place + 1, 2 * (place + by) + 1)]
    return lax.ppermute(value, "fsdp", pairs)


def ring_shift(value, places, by):
    count = 2 * places
    return lax.ppermute(value, "fsdp", [(i, (i - 2 * by) % count) for i in range(count)])


def z_gather(value, places, place):
    parts = jnp.stack([value] + [ring_shift(value, places, by) for by in range(1, places)])
    return lax.dynamic_slice_in_dim(
        jnp.concatenate((parts, parts)), lax.rem(places - place, places), places, 0
    )


def line_gather(value, places, place):
    ahead, behind = [value], [value]
    for step in range(1, places):
        ahead.append(line_shift(ahead[-1], places, 1, places - step, -1))
        behind.append(line_shift(behind[-1], places, step - 1, places - 2, 1))
    return [value] + [
        jnp.where(place + step < places, ahead[step], behind[places - step])
        for step in range(1, places)
    ]


def line_scatter(parts, places):
    up = down = None
    for far in range(places - 1, 0, -1):
        send_up, send_down = parts[far], parts[places - far]
        if up is not None:
            send_up = (send_up.astype(FULL) + up.astype(FULL)).astype(LOW)
            send_down = (send_down.astype(FULL) + down.astype(FULL)).astype(LOW)
        up = line_shift(send_up, places, 0, places - 1 - far, 1)
        down = line_shift(send_down, places, far, places - 1, -1)
    return parts[0].astype(FULL) + up.astype(FULL) + down.astype(FULL)


def gather_blocks(value, dims):
    held = {(): value}
    for dim in dims:
        keys = list(held)
        arrived = swap(jnp.stack([held[key] for key in keys]) if len(keys) > 1 else value, dim)
        for number, key in enumerate(keys):
            new_key = tuple(sorted(key + (dim,)))
            held[new_key] = arrived[number] if len(keys) > 1 else arrived
    return held


def scatter_blocks(held, dims):
    for dim in dims:
        stay = [key for key in held if dim not in key]
        leave = [tuple(sorted(key + (dim,))) for key in stay]
        sent = jnp.stack([held[key].astype(LOW) for key in leave])
        arrived = swap(sent, dim)
        held = {
            key: held[key].astype(FULL) + arrived[number].astype(FULL)
            for number, key in enumerate(stay)
        }
    return held[()]


def dense_gather(value, places, place, dims, core):
    rows, columns = value.shape
    half = (columns // 256) * 128
    first = z_gather(value[:, :half], places, place)
    for dim in dims:
        first = stage_pair(first, dim)
    second = value[:, half:]
    for dim in reversed(dims):
        second = stage_pair(second, dim)
    second = z_gather(second, places, place)
    first, second = (stage_pair(part, core) for part in (first, second))
    count = len(dims)
    axes = ("core",) + tuple(reversed(dims)) + ("z", "rows", "columns")
    axes_second = ("core", "z") + tuple(dims) + ("rows", "columns")
    wanted = ("z", dims[0]) + tuple(sorted(dims[1:], reverse=True)) + ("core", "rows", "columns")
    assert count + 4 == len(wanted)
    first = first.transpose([axes.index(name) for name in wanted]).reshape(-1, half)
    second = second.transpose([axes_second.index(name) for name in wanted]).reshape(
        -1, columns - half
    )
    return jnp.concatenate((first, second), axis=1)


def dense_scatter(value, places, place, dims, core, rows):
    columns = value.shape[1]
    half = (columns // 256) * 128
    names = ["z", dims[0]] + sorted(dims[1:], reverse=True) + [core]
    shaped = value.reshape((places,) + (2,) * (len(names) - 1) + (rows, columns))

    def halve(part, part_names, dim):
        spot = part_names.index(dim)
        own = bit_of(dim).astype(jnp.int32)
        keep = lax.dynamic_index_in_dim(part, own, spot, keepdims=False)
        send = lax.dynamic_index_in_dim(part, 1 - own, spot, keepdims=False)
        total = keep.astype(FULL) + swap(send, dim).astype(FULL)
        return (total, part_names[:spot] + part_names[spot + 1 :])

    def run(part, order):
        part_names = names
        for dim in order:
            total, part_names = halve(part, part_names, dim)
            part = total.astype(LOW)
        total = total if places == 1 else lax.dynamic_index_in_dim(total, place, 0, keepdims=False)
        for by in range(1, places):
            send = lax.dynamic_index_in_dim(part, lax.rem(place + by, places), 0, keepdims=False)
            total = total + ring_shift(send, places, places - by).astype(FULL)
        return total

    first = run(shaped[..., :half], [core] + list(dims))
    second = run(shaped[..., half:], [core] + list(reversed(dims)))
    return jnp.concatenate((first, second), axis=1)


def sum_everywhere(value):
    for axis in ("dp", "fsdp"):
        mask = 1
        while mask < lax.axis_size(axis):
            value = value + swap(value, (axis, mask))
            mask *= 2
    return value


def diagonal_hot(slots, bucket_count):
    width = 2 * slots
    lanes = jnp.arange(width, dtype=jnp.int32)[None, :]
    rows = jnp.arange(8, dtype=jnp.int32)[:, None]
    diagonal = (lanes - rows + (ROWS - 1)) % width
    bucket = jnp.where(diagonal < width - 1, bucket_index(diagonal - (slots - 1)), -1)
    return (bucket[:, :, None] == jnp.arange(bucket_count, dtype=jnp.int32)).astype(FULL)


def attend_kernel(query, key, value, base, seg_col, seg_row, out, probs, toeplitz):
    slots = query.shape[0]
    lanes = lax.broadcasted_iota(jnp.int32, (1, 2 * HEAD_DIM), 1)
    total = [None] * (slots // ROWS)
    for head in range(2):
        mine = (lanes >= head * HEAD_DIM) & (lanes < (head + 1) * HEAD_DIM)
        table = base[head]
        size = 8
        while size < ROWS:
            table = jnp.concatenate((table, pltpu.roll(table, size, 1)), axis=0)
            size *= 2
        toeplitz[...] = table
        value_head = jnp.where(mine, value[...], 0).astype(LOW)
        for block in range(slots // ROWS):
            rows = pl.ds(block * ROWS, ROWS)
            query_head = jnp.where(mine, query[rows, :], 0).astype(LOW)
            shift = slots - ROWS - block * ROWS
            scores = mm(query_head, key[...], ((1,), (1,))) * SCALE
            scores = scores + toeplitz[:, shift : shift + slots]
            scores = jnp.where(seg_col[rows, :] == seg_row[...], scores, -1e30)
            highest = jnp.max(scores, axis=-1, keepdims=True)
            raised = jnp.exp(scores - highest)
            low = (raised / jnp.sum(raised, axis=-1, keepdims=True)).astype(LOW)
            probs[head, rows, :] = low
            part = mm(low, value_head, ((1,), (0,)))
            total[block] = part if head == 0 else total[block] + part
    for block in range(slots // ROWS):
        out[pl.ds(block * ROWS, ROWS), :] = total[block].astype(LOW)


def attend_forward(projected, base, seg_col, seg_row):
    slots = projected.shape[0]
    width = projected.shape[1] // 3
    pairs = HEADS // 2
    lanes = 2 * HEAD_DIM
    return pl.pallas_call(
        attend_kernel,
        grid=(pairs,),
        in_specs=[
            pl.BlockSpec((slots, lanes), lambda p: (0, p)),
            pl.BlockSpec((slots, lanes), lambda p: (0, p + pairs)),
            pl.BlockSpec((slots, lanes), lambda p: (0, p + 2 * pairs)),
            pl.BlockSpec((2, 8, 2 * slots), lambda p: (p, 0, 0)),
            pl.BlockSpec((slots, 1), lambda p: (0, 0)),
            pl.BlockSpec((1, slots), lambda p: (0, 0)),
        ],
        out_specs=[
            pl.BlockSpec((slots, lanes), lambda p: (0, p)),
            pl.BlockSpec((2, slots, slots), lambda p: (p, 0, 0)),
        ],
        out_shape=[
            jax.ShapeDtypeStruct((slots, width), LOW),
            jax.ShapeDtypeStruct((HEADS, slots, slots), LOW),
        ],
        scratch_shapes=[pltpu.VMEM((ROWS, 2 * slots), FULL)],
        compiler_params=pltpu.CompilerParams(vmem_limit_bytes=VMEM_BYTES),
        cost_estimate=pl.CostEstimate(
            flops=HEADS * slots * slots * HEAD_DIM * 16,
            bytes_accessed=HEADS * slots * slots * 2 + 8 * slots * width,
            transcendentals=HEADS * slots * slots,
        ),
        name="attend_forward",
    )(projected, projected, projected, base, seg_col, seg_row)


def attend_back_kernel(
    query, key, value, grad, probs, out_query, out_key, out_value, diagonals, lined, scores_low
):
    slots = query.shape[0]
    lanes = lax.broadcasted_iota(jnp.int32, (1, 2 * HEAD_DIM), 1)
    query_total = [None] * (slots // ROWS)
    key_total = value_total = None
    for head in range(2):
        mine = (lanes >= head * HEAD_DIM) & (lanes < (head + 1) * HEAD_DIM)
        key_head = jnp.where(mine, key[...], 0).astype(LOW)
        grad_head = jnp.where(mine, grad[...], 0).astype(LOW)
        query_head = jnp.where(mine, query[...], 0).astype(LOW)
        lined[...] = jnp.zeros_like(lined)
        for block in range(slots // ROWS):
            rows = pl.ds(block * ROWS, ROWS)
            soft = probs[head, rows, :].astype(FULL)
            grad_rows = jnp.where(mine, grad[rows, :], 0).astype(LOW)
            weighted = soft * mm(grad_rows, value[...], ((1,), (1,)))
            back = weighted - soft * jnp.sum(weighted, axis=-1, keepdims=True)
            low = back.astype(LOW)
            scores_low[rows, :] = low
            shift = slots - ROWS - block * ROWS
            lined[:, shift : shift + slots] += low.astype(FULL)
            part = mm(low, key_head, ((1,), (0,)))
            query_total[block] = part if head == 0 else query_total[block] + part
        key_part = mm(scores_low[...], query_head, ((0,), (0,)))
        value_part = mm(probs[head], grad_head, ((0,), (0,)))
        key_total = key_part if head == 0 else key_total + key_part
        value_total = value_part if head == 0 else value_total + value_part
        table = lined[...]
        size = ROWS
        while size > 8:
            size //= 2
            table = table[:size] + pltpu.roll(table[size:], 2 * slots - size, 1)
        diagonals[head] = table
    out_key[...] = (key_total * SCALE).astype(LOW)
    out_value[...] = value_total.astype(LOW)
    for block in range(slots // ROWS):
        out_query[pl.ds(block * ROWS, ROWS), :] = (query_total[block] * SCALE).astype(LOW)


def attend_back(projected, grad_attended, probs):
    slots = projected.shape[0]
    width = projected.shape[1] // 3
    pairs = HEADS // 2
    lanes = 2 * HEAD_DIM
    column = pl.BlockSpec((slots, lanes), lambda p: (0, p))
    return pl.pallas_call(
        attend_back_kernel,
        grid=(pairs,),
        in_specs=[
            column,
            pl.BlockSpec((slots, lanes), lambda p: (0, p + pairs)),
            pl.BlockSpec((slots, lanes), lambda p: (0, p + 2 * pairs)),
            column,
            pl.BlockSpec((2, slots, slots), lambda p: (p, 0, 0)),
        ],
        out_specs=[
            column,
            column,
            column,
            pl.BlockSpec((2, 8, 2 * slots), lambda p: (p, 0, 0)),
        ],
        out_shape=[jax.ShapeDtypeStruct((slots, width), LOW)] * 3
        + [jax.ShapeDtypeStruct((HEADS, 8, 2 * slots), FULL)],
        scratch_shapes=[pltpu.VMEM((ROWS, 2 * slots), FULL), pltpu.VMEM((slots, slots), LOW)],
        compiler_params=pltpu.CompilerParams(vmem_limit_bytes=VMEM_BYTES),
        cost_estimate=pl.CostEstimate(
            flops=HEADS * slots * slots * HEAD_DIM * 32,
            bytes_accessed=HEADS * slots * slots * 2 + 14 * slots * width,
            transcendentals=0,
        ),
        name="attend_back",
    )(projected, projected, projected, grad_attended, probs)


def expert_kernel(chunks, started, *refs):
    refs = list(refs)
    rows, grads = refs[0], refs[1]
    first = refs[2 : 2 + chunks]
    second = refs[2 + chunks : 2 + 2 * chunks]
    at = 2 + 2 * chunks
    if started:
        old_y, old_back = refs[at], refs[at + 1]
        at += 2
    y_out, back_out = refs[at], refs[at + 1]
    first_out = refs[at + 2 : at + 2 + chunks]
    second_out = refs[at + 2 + chunks : at + 2 + 2 * chunks]
    y_sum, back_sum, hidden_low, pre_low = refs[at + 2 + 2 * chunks :]
    count = rows.shape[1]
    step = min(256, count)
    for chunk in range(chunks):
        w_first, w_second = first[chunk], second[chunk]
        for block in range(count // step):
            some = pl.ds(block * step, step)
            pre = mm(rows[0, some, :], w_first[0], ((1,), (0,)))
            grad_hidden = mm(grads[0, some, :], w_second[0], ((1,), (1,)))
            normal_cdf = 0.5 + 0.5 * lax.erf(pre * 0.7071067811865476)
            slope = normal_cdf + pre * jnp.exp(-0.5 * pre * pre) * 0.3989422804014327
            hidden = (pre * normal_cdf).astype(LOW)
            grad_pre = (grad_hidden * slope).astype(LOW)
            hidden_low[some, :] = hidden
            pre_low[some, :] = grad_pre
            y_part = mm(hidden, w_second[0], ((1,), (0,)))
            back_part = mm(grad_pre, w_first[0], ((1,), (1,)))
            if chunk > 0:
                y_part = y_part + y_sum[some, :]
                back_part = back_part + back_sum[some, :]
            elif started:
                y_part = y_part + old_y[0, some, :].astype(FULL)
                back_part = back_part + old_back[0, some, :].astype(FULL)
            if chunk < chunks - 1:
                y_sum[some, :] = y_part
                back_sum[some, :] = back_part
            else:
                y_out[0, some, :] = y_part.astype(LOW)
                back_out[0, some, :] = back_part.astype(LOW)
        first_out[chunk][0] = mm(rows[0], pre_low[...], ((0,), (0,)), LOW)
        second_out[chunk][0] = mm(hidden_low[...], grads[0], ((0,), (0,)), LOW)


def run_experts(rows, grads, first, second, old=()):
    chunks = len(first)
    experts, count, width = rows.shape
    units = first[0].shape[2]

    def whole(*shape):
        return pl.BlockSpec((1,) + shape, lambda e: (e, 0, 0))

    row_spec, first_spec, second_spec = whole(count, width), whole(width, units), whole(units, width)
    outs = pl.pallas_call(
        partial(expert_kernel, chunks, len(old) > 0),
        grid=(experts,),
        in_specs=[row_spec] * 2
        + [first_spec] * chunks
        + [second_spec] * chunks
        + [row_spec] * len(old),
        out_specs=[row_spec] * 2 + [first_spec] * chunks + [second_spec] * chunks,
        out_shape=[jax.ShapeDtypeStruct(rows.shape, LOW)] * 2
        + [jax.ShapeDtypeStruct((experts, width, units), LOW)] * chunks
        + [jax.ShapeDtypeStruct((experts, units, width), LOW)] * chunks,
        scratch_shapes=[
            pltpu.VMEM((count, width), FULL),
            pltpu.VMEM((count, width), FULL),
            pltpu.VMEM((count, units), LOW),
            pltpu.VMEM((count, units), LOW),
        ],
        compiler_params=pltpu.CompilerParams(vmem_limit_bytes=VMEM_BYTES),
        cost_estimate=pl.CostEstimate(
            flops=experts * chunks * 12 * count * width * units,
            bytes_accessed=experts * (8 * count * width + 8 * chunks * width * units),
            transcendentals=2 * experts * chunks * count * units,
        ),
        name="expert_pass",
    )(rows, grads, *first, *second, *old)
    return (outs[0], outs[1], outs[2 : 2 + chunks], outs[2 + chunks :])


def body(
    tokens,
    cotangent,
    seq_lens,
    routes,
    norm_gains,
    qkv_weight,
    out_weight,
    router_weight,
    rel_bias,
    expert_in,
    expert_out,
):
    tok_count, width = tokens.shape
    bucket_count = rel_bias.shape[0]
    shard_rows = qkv_weight.shape[0]
    experts_all = router_weight.shape[1]
    local_experts = expert_in.shape[0]
    capacity = 2 * tok_count // experts_all
    places = lax.axis_size("fsdp") // 2
    place = lax.axis_index("fsdp") // 2
    peer = lax.axis_index("dp")
    peer_count = lax.axis_size("dp")
    core = ("dp", 1)
    dims = [("fsdp", 1)]
    mask = 2
    while mask < peer_count:
        dims.append(("dp", mask))
        mask *= 2

    spare = -(4 * width + experts_all + 2) % 128
    packed = jnp.concatenate(
        (
            qkv_weight,
            out_weight,
            router_weight,
            norm_gains.T,
            jnp.zeros((shard_rows, spare), LOW),
        ),
        axis=1,
    )
    dense = dense_gather(packed, places, place, dims, core)
    qkv_full = dense[:, : 3 * width]
    out_full = dense[:, 3 * width : 4 * width]
    router_full = dense[:, 4 * width : 4 * width + experts_all]
    gains_float = dense[:, 4 * width + experts_all : 4 * width + experts_all + 2].T.astype(FULL)

    first_all = line_gather(expert_in, places, place)
    second_all = line_gather(expert_out, places, place)

    chosen = routes[:, 0]
    chosen_hot = chosen[:, None] == jnp.arange(experts_all, dtype=jnp.int32)[None, :]
    order = jnp.arange(tok_count, dtype=jnp.int32)
    earlier = (order[:, None] > order[None, :]).astype(LOW)
    rank_all = jnp.dot(earlier, chosen_hot.astype(LOW), preferred_element_type=FULL)
    rank_in = jnp.sum(jnp.where(chosen_hot, rank_all, 0.0), axis=1).astype(jnp.int32)
    slots_of = gather_blocks((chosen * capacity + rank_in)[None, :], dims)
    keys = sorted(slots_of)
    slots_near = jnp.stack([slots_of[key][0] for key in keys])
    local_slots = local_experts * capacity
    slot_ids = jnp.arange(local_slots, dtype=jnp.int32).reshape(local_experts, capacity)

    def hot_of(owner):
        wanted = owner * local_slots + slot_ids
        return (slots_near[:, None, None, :] == wanted[None, :, :, None]).astype(LOW)

    hot_own, hot_other = hot_of(peer), hot_of(peer ^ 1)
    segment = segment_ids(seq_lens[0], tok_count)
    bucket_hot = diagonal_hot(tok_count, bucket_count)
    base = jnp.einsum("rjb,bh->hrj", bucket_hot, rel_bias, precision=HIGH)

    inputs = tokens.astype(FULL)
    normed_one, inverse_one = rms_parts(inputs, gains_float[0])
    normed_low = normed_one.astype(LOW)
    projected = jnp.dot(normed_low, qkv_full, preferred_element_type=FULL).astype(LOW)
    attended, probs = attend_forward(projected, base, segment[:, None], segment[None, :])
    hidden_one = inputs + jnp.dot(attended, out_full, preferred_element_type=FULL)
    normed_two, inverse_two = rms_parts(hidden_one, gains_float[1])
    normed_two_low = normed_two.astype(LOW)
    router_soft = softmax_rows(jnp.dot(normed_two_low, router_full, preferred_element_type=FULL))
    gate_value = jnp.sum(jnp.where(chosen_hot, router_soft, 0.0), axis=1)
    upstream = cotangent.astype(FULL)
    grad_y = (gate_value[:, None] * upstream).astype(LOW)

    def dispatch(value, dims_in_order):
        held = gather_blocks(value, dims_in_order)
        blocks = jnp.stack([held[key] for key in keys])

        def pick(hot):
            return jnp.einsum("bjst,btd->jbsd", hot, blocks, preferred_element_type=FULL).astype(LOW)

        both = jnp.stack((pick(hot_own), swap(pick(hot_other), core)), axis=1)
        return both.reshape(local_experts, -1, width)

    rows = dispatch(normed_two_low, dims)
    grads = dispatch(grad_y, list(reversed(dims)))

    odd = [part for part in range(places) if part % 2 == 1]
    even = [part for part in range(places) if part % 2 == 0]
    first_grads, second_grads = [None] * places, [None] * places
    old = ()
    todo = sorted(range(places), key=lambda part: (-abs(2 * part - places), -part))
    todo = [part for part in todo if part != 0] + [0]
    for number in range(0, places, 2):
        group = todo[number : number + 2]
        y_rows, back_rows, in_parts, out_parts = run_experts(
            rows,
            grads,
            [first_all[part] for part in group],
            [second_all[part] for part in group],
            old,
        )
        old = (y_rows, back_rows)
        for part, in_part, out_part in zip(group, in_parts, out_parts):
            first_grads[part], second_grads[part] = in_part, out_part
    in_grad = line_scatter(first_grads, places)
    out_expert_grad = line_scatter(second_grads, places)

    def collect(values, dims_in_order):
        shaped = values.reshape(local_experts, 2, len(keys), capacity, width)
        other = swap(shaped[:, 1], core)
        raw = jnp.einsum("bjst,jbsd->btd", hot_own, shaped[:, 0], preferred_element_type=FULL)
        raw = raw + jnp.einsum("bjst,jbsd->btd", hot_other, other, preferred_element_type=FULL)
        held = {key: raw[number] for number, key in enumerate(keys)}
        return scatter_blocks(held, dims_in_order)

    token_y = collect(y_rows, list(reversed(dims)))
    grad_rows = collect(back_rows, dims)

    mixed = (hidden_one + gate_value[:, None] * token_y).astype(LOW)
    grad_gate = jnp.sum(upstream * token_y, axis=1)
    grad_logits = router_soft * (
        jnp.where(chosen_hot, grad_gate[:, None], 0.0) - (gate_value * grad_gate)[:, None]
    )
    router_local = jnp.dot(normed_two_low.astype(FULL).T, grad_logits, precision=HIGH)
    grad_normed_two = grad_rows + jnp.dot(
        grad_logits, router_full.astype(FULL).T, precision=HIGH
    )
    grad_from_two, gain_grad_two = norm_back(
        hidden_one, inverse_two, gains_float[1], grad_normed_two
    )
    grad_hidden_one = upstream + grad_from_two
    grad_attn_low = grad_hidden_one.astype(LOW)
    out_local = jnp.einsum("td,te->de", attended, grad_attn_low, preferred_element_type=FULL)
    grad_attended = mm(grad_attn_low, out_full, ((1,), (1,)), LOW)
    grad_query, grad_key, grad_value, diagonals = attend_back(projected, grad_attended, probs)
    grad_projected = jnp.concatenate((grad_query, grad_key, grad_value), axis=1)
    qkv_local = jnp.einsum("td,te->de", normed_low, grad_projected, preferred_element_type=FULL)
    grad_normed_one = mm(grad_projected, qkv_full, ((1,), (1,)))
    grad_from_one, gain_grad_one = norm_back(inputs, inverse_one, gains_float[0], grad_normed_one)
    tokens_grad = grad_hidden_one + grad_from_one
    bias_local = jnp.einsum("hrj,rjb->bh", diagonals, bucket_hot, precision=HIGH)
    bias_grad = sum_everywhere(bias_local)
    gains_local = jnp.stack((gain_grad_one, gain_grad_two), axis=1)
    packed_grad = jnp.concatenate(
        (
            qkv_local.astype(LOW),
            out_local.astype(LOW),
            router_local.astype(LOW),
            gains_local.astype(LOW),
            jnp.zeros((width, spare), LOW),
        ),
        axis=1,
    )
    dense_grad = dense_scatter(packed_grad, places, place, dims, core, shard_rows)
    qkv_grad = dense_grad[:, : 3 * width]
    out_grad = dense_grad[:, 3 * width : 4 * width]
    router_grad = dense_grad[:, 4 * width : 4 * width + experts_all]
    gains_grad = dense_grad[:, 4 * width + experts_all : 4 * width + experts_all + 2].T
    return (
        mixed,
        tokens_grad,
        gains_grad,
        qkv_grad,
        out_grad,
        router_grad,
        bias_grad,
        in_grad,
        out_expert_grad,
    )


def solution(mesh):
    rows = P(("fsdp", "dp"), None)
    columns = P(None, ("fsdp", "dp"))
    experts = (P("dp", None, "fsdp"), P("dp", "fsdp", None))
    return jax.shard_map(
        body,
        mesh=mesh,
        in_specs=(rows, rows, rows, rows, columns, rows, rows, rows, P()) + experts,
        out_specs=(rows, rows, columns, rows, rows, rows, P()) + experts,
        check_vma=False,
    )
```

time: 1180 us -> 520 us (0.44)
  waiting for transfers between devices: 589 us -> 205 us
  matrix products: 226 us -> 39.2 us
  blocking collectives: 134 us -> 0 us
  starting transfers between devices: 16.4 us -> 98.2 us
  Pallas kernels: 0 us -> 81.3 us
  other arithmetic: 111 us -> 48.5 us
  local copies, waits for them, and re-layouts: 67.9 us -> 35.3 us
  loops' own time: 12.6 us -> 0 us
  between operations: 15.1 us -> 2.6 us
    reduce_scatter x4 -> x0, waiting for transfers between devices: 278 us -> none  [the longest x2 192 us: expert_backward(): lax.psum_scatter(grad_second.astype(jnp.bfloat16), 'fsdp', scatter_dimens...]
    ppermute x0 -> x67, waiting for transfers between devices: none -> 205 us  [the longest x24 89.3 us: line_shift(): return lax.ppermute(value, 'fsdp', pairs)]
    dot_general x60 -> x16, matrix products: 215 us -> 30.9 us  [the longest x4 11.2 us: pick(): jnp.einsum('bjst,btd->jbsd', hot, blocks, preferred_element_type=FULL)]
    while x6 -> x0, waiting for transfers between devices: 140 us -> none
    all_gather x4 -> x0, waiting for transfers between devices: 138 us -> none  [the longest x1 138 us: body(): lax.all_gather(expert_out, 'fsdp', axis=1, tiled=True)]
    ppermute x0 -> x67, starting transfers between devices: none -> 98.2 us  [the longest x24 54.8 us: line_shift(): return lax.ppermute(value, 'fsdp', pairs)]
    all_gather x2 -> x0, blocking collectives: 93.3 us -> none  [the longest x1 50 us: body(): lax.all_gather(router_weight, ('fsdp', 'dp'), axis=0, tiled=True)]
    pallas_call x0 -> x4, Pallas kernels: none -> 81.3 us  [the longest x2 49.4 us: run_experts(): pl.pallas_call(partial(expert_kernel, chunks, len(old) > 0), grid=(expert...]
  transfers between devices with their start and end apart: 14 -> 67, of which waited for: 8 -> 27; matrix products, arithmetic and copies ran while one was open for 29% -> 22% of each run, Pallas kernels for 0% -> 11%
where the time goes in v1:
time: 520 us; the launch traced here: 510 us
  waiting for transfers between devices  205 us (39%)
  starting transfers between devices  98.2 us (19%)
  Pallas kernels  81.3 us (16%)
  other arithmetic  48.5 us (9%)
  matrix products  39.2 us (8%)
  local copies, waits for them, and re-layouts  35.3 us (7%)
    ppermute x24, waiting for transfers between devices, line_shift(): return lax.ppermute(value, 'fsdp', pairs)  89.3 us
    ppermute x31, waiting for transfers between devices, swap(): return lax.ppermute(value, axis, [(i, i ^ mask) for i in range(count)])  67.8 us
    ppermute x24, starting transfers between devices, line_shift(): return lax.ppermute(value, 'fsdp', pairs)  54.8 us
    pallas_call x2, Pallas kernels, run_experts(): pl.pallas_call(partial(expert_kernel, chunks, len(old) > 0), grid=(expert...  49.4 us
    ppermute x12, waiting for transfers between devices, ring_shift(): lax.ppermute(value, 'fsdp', [(i, (i - 2 * by) % count) for i in range(cou...  47.8 us
    ppermute x31, starting transfers between devices, swap(): return lax.ppermute(value, axis, [(i, i ^ mask) for i in range(count)])  27.9 us
    pallas_call x1, Pallas kernels, attend_back(): pl.pallas_call(attend_back_kernel, grid=(pairs,), in_specs=[column, pl.Bl...  16.6 us
    ppermute x12, starting transfers between devices, ring_shift(): lax.ppermute(value, 'fsdp', [(i, (i - 2 * by) % count) for i in range(cou...  15.5 us
  transfers between devices with their start and end apart: 67, of which 27 were waited for; matrix products, arithmetic and copies ran while one was open for 22% of the time, Pallas kernels for 11%

profile of v1, /device:TPU:0, one launch (start us, length us, event | category | flops | bytes accessed | tf_op | source)
XLA Modules:
  0.0 510.0 jit_solution(5992070445985380578)
XLA Ops:
  1.7 5.0 collective-permute-start.6
  10.9 5.4 %collective-permute-start.26 = (bf16[2,384,768]{2,1,0:T(8,128)(2,1)}, bf16[2,384,768]{2,1,0:T(8,128)(2,1)}, u32[]{:S(2)}, u32[]{:S(2)}) collective-permute-start(bf16[2,384,768]{2,1,0:T(8,128)(2,1)} %refs_5_.1), channel_id=1, source_target_pairs={{0,8},{4,12},{8,16},{12,20},{16,24},{20,28},{1,9},{5,13},{9,17},{1... | collective-permute-start | bytes 3538952 | tf_op jit(solution)/shard_map/ppermute | solution.py:84
  24.2 5.6 %collective-permute-start.22 = (bf16[2,768,384]{2,1,0:T(8,128)(2,1)}, bf16[2,768,384]{2,1,0:T(8,128)(2,1)}, u32[]{:S(2)}, u32[]{:S(2)}) collective-permute-start(bf16[2,768,384]{2,1,0:T(8,128)(2,1)} %refs_3_.1), channel_id=1, source_target_pairs={{0,8},{4,12},{8,16},{12,20},{16,24},{20,28},{1,9},{5,13},{9,17},{1... | collective-permute-start | bytes 3538952 | tf_op jit(solution)/shard_map/ppermute | solution.py:84
  32.3 7.7 %collective-permute-done.1 = bf16[2,24,1664]{2,1,0:T(8,128)(2,1)S(1)} collective-permute-done((bf16[2,24,1664]{2,1,0:T(8,128)(2,1)S(1)}, bf16[2,24,1664]{2,1,0:T(8,128)(2,1)S(1)}, u32[]{:S(2)}, u32[]{:S(2)}) %collective-permute-start.1) | collective-permute-done | bytes 159776 | tf_op jit(solution)/shard_map/ppermute | solution.py:66
  41.2 32.9 %collective-permute-done.2 = bf16[2,2,24,1664]{3,2,1,0:T(8,128)(2,1)S(1)} collective-permute-done((bf16[2,2,24,1664]{3,2,1,0:T(8,128)(2,1)S(1)}, bf16[2,2,24,1664]{3,2,1,0:T(8,128)(2,1)S(1)}, u32[]{:S(2)}, u32[]{:S(2)}) %collective-permute-start.2) | collective-permute-done | bytes 319520 | tf_op jit(solution)/shard_map/ppermute | solution.py:89
  74.1 6.8 %collective-permute-done.3 = bf16[2,2,24,1664]{3,2,1,0:T(8,128)(2,1)S(1)} collective-permute-done((bf16[2,2,24,1664]{3,2,1,0:T(8,128)(2,1)S(1)}, bf16[2,2,24,1664]{3,2,1,0:T(8,128)(2,1)S(1)}, u32[]{:S(2)}, u32[]{:S(2)}) %collective-permute-start.3) | collective-permute-done | bytes 319520 | tf_op jit(solution)/shard_map/ppermute | solution.py:89
  86.0 5.7 %collective-permute-done.10 = bf16[2,4,24,1536]{3,2,0,1:T(8,128)(2,1)S(1)} collective-permute-done((bf16[2,4,24,1536]{3,2,0,1:T(8,128)(2,1)S(1)}, bf16[2,4,24,1536]{3,2,0,1:T(8,128)(2,1)S(1)}, u32[]{:S(2)}, u32[]{:S(2)}) %collective-permute-start.10) | collective-permute-done | bytes 589856 | tf_op jit(solution)/shard_map/ppermute | solution.py:66
  100.4 3.5 convolution_convert_fusion.1.query.key.value
  103.9 15.3 %attend_forward.1 = (bf16[512,768]{1,0:T(8,128)(2,1)S(1)}, bf16[12,512,512]{2,1,0:T(8,128)(2,1)}) custom-call(bf16[512,2304]{1,0:T(8,128)(2,1)} %convolution_convert_fusion.1.query.key.value, bf16[512,2304]{1,0:T(8,128)(2,1)} %convolution_convert_fusion.1.query.key.value, bf16[512,2304]{1,0:T(8,128)(2,1)} %convolution_convert_fusion.1.query.key.value, ...), custom_call_target="tpu_custom_call" | custom-call | flops 3221225472 | bytes 9437184 | tf_op jit(solution)/shard_map/attend_forward/pallas_call | solution.py:252
  122.1 6.5 %collective-permute-done.20 = bf16[2,768,384]{2,1,0:T(8,128)(2,1)} collective-permute-done((bf16[2,768,384]{2,1,0:T(8,128)(2,1)}, bf16[2,768,384]{2,1,0:T(8,128)(2,1)}, u32[]{:S(2)}, u32[]{:S(2)}) %collective-permute-start.20) | collective-permute-done | bytes 1179680 | tf_op jit(solution)/shard_map/ppermute | solution.py:84
  131.6 9.6 %collective-permute-done.17 = bf16[512,768]{1,0:T(8,128)(2,1)S(1)} collective-permute-done((bf16[512,768]{1,0:T(8,128)(2,1)S(1)}, bf16[512,768]{1,0:T(8,128)(2,1)S(1)}, u32[]{:S(2)}, u32[]{:S(2)}) %collective-permute-start.17) | collective-permute-done | bytes 786464 | tf_op jit(solution)/shard_map/ppermute | solution.py:66
  142.3 11.6 %collective-permute-done.25 = bf16[2,384,768]{2,1,0:T(8,128)(2,1)} collective-permute-done((bf16[2,384,768]{2,1,0:T(8,128)(2,1)}, bf16[2,384,768]{2,1,0:T(8,128)(2,1)}, u32[]{:S(2)}, u32[]{:S(2)}) %collective-permute-start.25) | collective-permute-done | bytes 1179680 | tf_op jit(solution)/shard_map/ppermute | solution.py:84
  158.6 20.5 %collective-permute-done.21 = bf16[2,768,384]{2,1,0:T(8,128)(2,1)S(1)} collective-permute-done((bf16[2,768,384]{2,1,0:T(8,128)(2,1)}, bf16[2,768,384]{2,1,0:T(8,128)(2,1)S(1)}, u32[]{:S(2)}, u32[]{:S(2)}) %collective-permute-start.21) | collective-permute-done | bytes 1179680 | tf_op jit(solution)/shard_map/ppermute | solution.py:84
  193.3 21.8 %collective-permute-done.15 = bf16[2,512,768]{2,1,0:T(8,128)(2,1)S(1)} collective-permute-done((bf16[2,512,768]{2,1,0:T(8,128)(2,1)S(1)}, bf16[2,512,768]{2,1,0:T(8,128)(2,1)S(1)}, u32[]{:S(2)}, u32[]{:S(2)}) %collective-permute-start.15) | collective-permute-done | bytes 1572896 | tf_op jit(solution)/shard_map/ppermute | solution.py:66
  219.0 10.5 %collective-permute-done.28 = bf16[2,768,384]{2,1,0:T(8,128)(2,1)S(1)} collective-permute-done((bf16[2,768,384]{2,1,0:T(8,128)(2,1)S(1)}, bf16[2,768,384]{2,1,0:T(8,128)(2,1)S(1)}, u32[]{:S(2)}, u32[]{:S(2)}) %collective-permute-start.28) | collective-permute-done | bytes 1179680 | tf_op jit(solution)/shard_map/ppermute | solution.py:84
  240.8 24.7 %expert_pass.2 = (bf16[2,1024,768]{2,1,0:T(8,128)(2,1)}, bf16[2,1024,768]{2,1,0:T(8,128)(2,1)}, bf16[2,768,384]{2,1,0:T(8,128)(2,1)S(1)}, bf16[2,768,384]{2,1,0:...) custom-call(bf16[2,1024,768]{2,1,0:T(8,128)(2,1)} %bitcast.244, ...), custom_call_target="tpu_custom_call" | custom-call | flops 14495514624 | bytes 22020096 | tf_op jit(solution)/shard_map/expert_pass/pallas_call | solution.py:412
  265.5 3.7 collective-permute-start.61
  274.0 24.7 %expert_pass.3 = (bf16[2,1024,768]{2,1,0:T(8,128)(2,1)}, bf16[2,1024,768]{2,1,0:T(8,128)(2,1)}, bf16[2,768,384]{2,1,0:T(8,128)(2,1)S(1)}, bf16[2,768,384]{2,1,0:...) custom-call(bf16[2,1024,768]{2,1,0:T(8,128)(2,1)} %bitcast.245, ...), custom_call_target="tpu_custom_call" | custom-call | flops 14495514624 | bytes 22020096 | tf_op jit(solution)/shard_map/expert_pass/pallas_call | solution.py:412
  306.0 3.6 fusion.23
  312.0 8.1 %collective-permute-done.55 = bf16[2,768,384]{2,1,0:T(8,128)(2,1)S(1)} collective-permute-done((bf16[2,768,384]{2,1,0:T(8,128)(2,1)S(1)}, bf16[2,768,384]{2,1,0:T(8,128)(2,1)S(1)}, u32[]{:S(2)}, u32[]{:S(2)}) %collective-permute-start.55) | collective-permute-done | bytes 1179680 | tf_op jit(solution)/shard_map/ppermute | solution.py:84
  325.1 4.9 collective-permute-start.56
  339.4 6.0 %collective-permute-done.62 = bf16[2,384,768]{2,1,0:T(8,128)(2,1)} collective-permute-done((bf16[2,384,768]{2,1,0:T(8,128)(2,1)}, bf16[2,384,768]{2,1,0:T(8,128)(2,1)}, u32[]{:S(2)}, u32[]{:S(2)}) %collective-permute-start.62) | collective-permute-done | bytes 1179680 | tf_op jit(solution)/shard_map/ppermute | solution.py:84
  348.3 5.0 collective-permute-start.63
  355.1 15.6 %collective-permute-done.56 = bf16[2,768,384]{2,1,0:T(8,128)(2,1)} collective-permute-done((bf16[2,768,384]{2,1,0:T(8,128)(2,1)}, bf16[2,768,384]{2,1,0:T(8,128)(2,1)}, u32[]{:S(2)}, u32[]{:S(2)}) %collective-permute-start.56) | collective-permute-done | bytes 1179680 | tf_op jit(solution)/shard_map/ppermute | solution.py:84
  374.6 6.1 %collective-permute-start.57 = (bf16[2,768,384]{2,1,0:T(8,128)(2,1)}, bf16[2,768,384]{2,1,0:T(8,128)(2,1)}, u32[]{:S(2)}, u32[]{:S(2)}) collective-permute-start(bf16[2,768,384]{2,1,0:T(8,128)(2,1)} %add_convert_fusion.3), channel_id=1, source_target_pairs={{0,8},{4,12},{8,16},{12,20},{16,24},{20,28},{1,9},{5,13},{9,17},{1... | collective-permute-start | bytes 3538952 | tf_op jit(solution)/shard_map/ppermute | solution.py:84
  387.4 8.5 %collective-permute-done.63 = bf16[2,384,768]{2,1,0:T(8,128)(2,1)S(1)} collective-permute-done((bf16[2,384,768]{2,1,0:T(8,128)(2,1)S(1)}, bf16[2,384,768]{2,1,0:T(8,128)(2,1)S(1)}, u32[]{:S(2)}, u32[]{:S(2)}) %collective-permute-start.63) | collective-permute-done | bytes 1179680 | tf_op jit(solution)/shard_map/ppermute | solution.py:84
  409.3 16.6 %attend_back.1 = (bf16[512,768]{1,0:T(8,128)(2,1)S(1)}, bf16[512,768]{1,0:T(8,128)(2,1)S(1)}, bf16[512,768]{1,0:T(8,128)(2,1)}, f32[12,8,1024]{2,1,0:T(8,128)S(1)}) custom-call(bf16[512,2304]{1,0:T(8,128)(2,1)} %convolution_convert_fusion.1.query.key.value, bf16[512,2304]{1,0:T(8,128)(2,1)} %convolution_convert_fusion.1.query.key.value, ...), custom_call_target="tpu_custom_call" | custom-call | flops 6442450944 | bytes 11796480 | tf_op jit(solution)/shard_map/attend_back/pallas_call | solution.py:329
  429.6 3.9 fusion.51
  438.4 4.0 convolution_convert_fusion
  442.5 8.2 %concatenate.121 = bf16[768,3200]{1,0:T(8,128)(2,1)} concatenate(bf16[768,2304]{1,0:T(8,128)(2,1)} %convolution_convert_fusion, bf16[768,768]{1,0:T(8,128)(2,1)S(1)} %convolution_convert_fusion.2, bf16[768,8]{1,0:T(8,128)(2,1)S(1)} %copy-done.27, bf16[768,1]{1,0:T(8,128)(2,1)S(1)} %copy-done.28, bf16[768,1]{1,0:T(8,128)(2,1)S(1)} %copy-done.29, bf16[768,118]{1,0:T(8,128)(2,1)S(1)} %broadcast_in_dim.29), dimensions={1} | concatenate | bytes 9830400 | tf_op jit(solution)/shard_map/concatenate | solution.py:594
  474.2 10.4 %collective-permute-done.45 = bf16[4,2,24,1536]{3,2,1,0:T(8,128)(2,1)S(1)} collective-permute-done((bf16[4,2,24,1536]{3,2,1,0:T(8,128)(2,1)S(1)}, bf16[4,2,24,1536]{3,2,1,0:T(8,128)(2,1)S(1)}, u32[]{:S(2)}, u32[]{:S(2)}) %collective-permute-start.45) | collective-permute-done | bytes 589856 | tf_op jit(solution)/shard_map/ppermute | solution.py:66
  485.4 4.2 collective-permute-done.39
  (369 shorter events, 180.7 us)
Async XLA Ops:
  10.9 83.8 %collective-permute-start.26 = (bf16[2,384,768]{2,1,0:T(8,128)(2,1)}, bf16[2,384,768]{2,1,0:T(8,128)(2,1)}, u32[]{:S(2)}, u32[]{:S(2)}) collective-permute-start(bf16[2,384,768]{2,1,0:T(8,128)(2,1)} %refs_5_.1), channel_id=1, source_target_pairs={{0,8},{4,12},{8,16},{12,20},{16,24},{20,28},{1,9},{5,13},{9,17},{1... | collective-permute-start | bytes 3538952 | tf_op jit(solution)/shard_map/ppermute | solution.py:84
  21.3 75.0 %collective-permute-start.24 = (bf16[2,384,768]{2,1,0:T(8,128)(2,1)}, bf16[2,384,768]{2,1,0:T(8,128)(2,1)}, u32[]{:S(2)}, u32[]{:S(2)}) collective-permute-start(bf16[2,384,768]{2,1,0:T(8,128)(2,1)} %refs_5_.1), channel_id=1, source_target_pairs={{8,0},{12,4},{16,8},{20,12},{24,16},{28,20},{9,1},{13,5},{17,9},{2... | collective-permute-start | bytes 3538952 | tf_op jit(solution)/shard_map/ppermute | solution.py:84
  24.2 73.8 %collective-permute-start.22 = (bf16[2,768,384]{2,1,0:T(8,128)(2,1)}, bf16[2,768,384]{2,1,0:T(8,128)(2,1)}, u32[]{:S(2)}, u32[]{:S(2)}) collective-permute-start(bf16[2,768,384]{2,1,0:T(8,128)(2,1)} %refs_3_.1), channel_id=1, source_target_pairs={{0,8},{4,12},{8,16},{12,20},{16,24},{20,28},{1,9},{5,13},{9,17},{1... | collective-permute-start | bytes 3538952 | tf_op jit(solution)/shard_map/ppermute | solution.py:84
  40.1 34.0 %collective-permute-start.2 = (bf16[2,2,24,1664]{3,2,1,0:T(8,128)(2,1)S(1)}, bf16[2,2,24,1664]{3,2,1,0:T(8,128)(2,1)S(1)}, u32[]{:S(2)}, u32[]{:S(2)}) collective-permute-start(bf16[2,2,24,1664]{3,2,1,0:T(8,128)(2,1)S(1)} %maximum_select_fusion.6), channel_id=1, source_target_pairs={{0,24},{4,28},{8,0},{12,4},{16,8},{20,12},{24,16},{28,20},{1,25},{... | collective-permute-start | bytes 958472 | tf_op jit(solution)/shard_map/ppermute | solution.py:89
  40.2 40.7 %collective-permute-start.3 = (bf16[2,2,24,1664]{3,2,1,0:T(8,128)(2,1)S(1)}, bf16[2,2,24,1664]{3,2,1,0:T(8,128)(2,1)S(1)}, u32[]{:S(2)}, u32[]{:S(2)}) collective-permute-start(bf16[2,2,24,1664]{3,2,1,0:T(8,128)(2,1)S(1)} %maximum_select_fusion.6), channel_id=1, source_target_pairs={{0,16},{4,20},{8,24},{12,28},{16,0},{20,4},{24,8},{28,12},{1,17},{... | collective-permute-start | bytes 958472 | tf_op jit(solution)/shard_map/ppermute | solution.py:89
  92.2 36.5 %collective-permute-start.20 = (bf16[2,768,384]{2,1,0:T(8,128)(2,1)}, bf16[2,768,384]{2,1,0:T(8,128)(2,1)}, u32[]{:S(2)}, u32[]{:S(2)}) collective-permute-start(bf16[2,768,384]{2,1,0:T(8,128)(2,1)} %refs_3_.1), channel_id=1, source_target_pairs={{8,0},{12,4},{16,8},{20,12},{24,16},{28,20},{9,1},{13,5},{17,9},{2... | collective-permute-start | bytes 3538952 | tf_op jit(solution)/shard_map/ppermute | solution.py:84
  96.3 33.6 %collective-permute-start.27 = (bf16[2,384,768]{2,1,0:T(8,128)(2,1)}, bf16[2,384,768]{2,1,0:T(8,128)(2,1)}, u32[]{:S(2)}, u32[]{:S(2)}) collective-permute-start(bf16[2,384,768]{2,1,0:T(8,128)(2,1)} %collective-permute-done.26), channel_id=1, source_target_pairs={{8,16},{12,20},{16,24},{20,28},{9,17},{13,21},{17,25},{21,29},{10,... | collective-permute-start | bytes 3538952 | tf_op jit(solution)/shard_map/ppermute | solution.py:84
  98.0 55.9 %collective-permute-start.25 = (bf16[2,384,768]{2,1,0:T(8,128)(2,1)}, bf16[2,384,768]{2,1,0:T(8,128)(2,1)}, u32[]{:S(2)}, u32[]{:S(2)}) collective-permute-start(bf16[2,384,768]{2,1,0:T(8,128)(2,1)} %collective-permute-done.24), channel_id=1, source_target_pairs={{8,0},{12,4},{16,8},{20,12},{9,1},{13,5},{17,9},{21,13},{10,2},{14... | collective-permute-start | bytes 3538952 | tf_op jit(solution)/shard_map/ppermute | solution.py:84
  99.3 31.6 %collective-permute-start.23 = (bf16[2,768,384]{2,1,0:T(8,128)(2,1)}, bf16[2,768,384]{2,1,0:T(8,128)(2,1)S(1)}, u32[]{:S(2)}, u32[]{:S(2)}) collective-permute-start(bf16[2,768,384]{2,1,0:T(8,128)(2,1)} %collective-permute-done.22), channel_id=1, source_target_pairs={{8,16},{12,20},{16,24},{20,28},{9,17},{13,21},{17,25},{21,29},{10,... | collective-permute-start | bytes 3538952 | tf_op jit(solution)/shard_map/ppermute | solution.py:84
  128.6 50.5 %collective-permute-start.21 = (bf16[2,768,384]{2,1,0:T(8,128)(2,1)}, bf16[2,768,384]{2,1,0:T(8,128)(2,1)S(1)}, u32[]{:S(2)}, u32[]{:S(2)}) collective-permute-start(bf16[2,768,384]{2,1,0:T(8,128)(2,1)} %collective-permute-done.20), channel_id=1, source_target_pairs={{8,0},{12,4},{16,8},{20,12},{9,1},{13,5},{17,9},{21,13},{10,2},{14... | collective-permute-start | bytes 3538952 | tf_op jit(solution)/shard_map/ppermute | solution.py:84
  130.9 50.9 %collective-permute-start.31 = (bf16[2,384,768]{2,1,0:T(8,128)(2,1)}, bf16[2,384,768]{2,1,0:T(8,128)(2,1)S(1)}, u32[]{:S(2)}, u32[]{:S(2)}) collective-permute-start(bf16[2,384,768]{2,1,0:T(8,128)(2,1)} %collective-permute-done.27), channel_id=1, source_target_pairs={{16,24},{20,28},{17,25},{21,29},{18,26},{22,30},{19,27},{23,31}} | collective-permute-start | bytes 3538952 | tf_op jit(solution)/shard_map/ppermute | solution.py:84
  141.2 44.3 %collective-permute-start.29 = (bf16[2,768,384]{2,1,0:T(8,128)(2,1)S(1)}, bf16[2,768,384]{2,1,0:T(8,128)(2,1)S(1)}, u32[]{:S(2)}, u32[]{:S(2)}) collective-permute-start(bf16[2,768,384]{2,1,0:T(8,128)(2,1)S(1)} %collective-permute-done.23), channel_id=1, source_target_pairs={{16,24},{20,28},{17,25},{21,29},{18,26},{22,30},{19,27},{23,31}} | collective-permute-start | bytes 3538952 | tf_op jit(solution)/shard_map/ppermute | solution.py:84
  153.9 36.0 %collective-permute-start.18 = (bf16[2,512,768]{2,1,0:T(8,128)(2,1)S(1)}, bf16[2,512,768]{2,1,0:T(8,128)(2,1)S(1)}, u32[]{:S(2)}, u32[]{:S(2)}) collective-permute-start(bf16[2,512,768]{2,1,0:T(8,128)(2,1)S(1)} %pad_maximum_fusion.6), channel_id=1, source_target_pairs={{0,4},{4,0},{8,12},{12,8},{16,20},{20,16},{24,28},{28,24},{1,5},{5... | collective-permute-start | bytes 4718600 | tf_op jit(solution)/shard_map/ppermute | solution.py:66
  157.2 60.5 %collective-permute-start.30 = (bf16[2,384,768]{2,1,0:T(8,128)(2,1)}, bf16[2,384,768]{2,1,0:T(8,128)(2,1)S(1)}, u32[]{:S(2)}, u32[]{:S(2)}) collective-permute-start(bf16[2,384,768]{2,1,0:T(8,128)(2,1)} %collective-permute-done.25), channel_id=1, source_target_pairs={{8,0},{12,4},{9,1},{13,5},{10,2},{14,6},{11,3},{15,7}} | collective-permute-start | bytes 3538952 | tf_op jit(solution)/shard_map/ppermute | solution.py:84
  179.1 36.0 %collective-permute-start.15 = (bf16[2,512,768]{2,1,0:T(8,128)(2,1)S(1)}, bf16[2,512,768]{2,1,0:T(8,128)(2,1)S(1)}, u32[]{:S(2)}, u32[]{:S(2)}) collective-permute-start(bf16[2,512,768]{2,1,0:T(8,128)(2,1)S(1)} %pad_maximum_fusion.5), channel_id=1, source_target_pairs={{0,2},{1,3},{2,0},{3,1},{4,6},{5,7},{6,4},{7,5},{8,10},{9,11},{10,... | collective-permute-start | bytes 4718600 | tf_op jit(solution)/shard_map/ppermute | solution.py:66
  181.8 47.6 %collective-permute-start.28 = (bf16[2,768,384]{2,1,0:T(8,128)(2,1)S(1)}, bf16[2,768,384]{2,1,0:T(8,128)(2,1)S(1)}, u32[]{:S(2)}, u32[]{:S(2)}) collective-permute-start(bf16[2,768,384]{2,1,0:T(8,128)(2,1)S(1)} %collective-permute-done.21), channel_id=1, source_target_pairs={{8,0},{12,4},{9,1},{13,5},{10,2},{14,6},{11,3},{15,7}} | collective-permute-start | bytes 3538952 | tf_op jit(solution)/shard_map/ppermute | solution.py:84
  193.2 43.1 %collective-permute-start.19 = (bf16[2,4,128,768]{3,2,0,1:T(8,128)(2,1)S(1)}, bf16[2,4,128,768]{3,2,0,1:T(8,128)(2,1)S(1)}, u32[]{:S(2)}, u32[]{:S(2)}) collective-permute-start(bf16[2,4,128,768]{3,2,0,1:T(8,128)(2,1)S(1)} %fusion.65), channel_id=1, source_target_pairs={{0,1},{1,0},{2,3},{3,2},{4,5},{5,4},{6,7},{7,6},{8,9},{9,8},{10,11... | collective-permute-start | bytes 4718600 | tf_op jit(solution)/shard_map/ppermute | solution.py:66
  265.5 38.7 %collective-permute-start.61 = (bf16[2,384,768]{2,1,0:T(8,128)(2,1)}, bf16[2,384,768]{2,1,0:T(8,128)(2,1)}, u32[]{:S(2)}, u32[]{:S(2)}) collective-permute-start(bf16[2,384,768]{2,1,0:T(8,128)(2,1)} %get-tuple-element.44), channel_id=1, source_target_pairs={{0,8},{4,12},{1,9},{5,13},{2,10},{6,14},{3,11},{7,15}} | collective-permute-start | bytes 3538952 | tf_op jit(solution)/shard_map/ppermute | solution.py:84
  269.3 36.6 %collective-permute-start.64 = (bf16[2,384,768]{2,1,0:T(8,128)(2,1)}, bf16[2,384,768]{2,1,0:T(8,128)(2,1)}, u32[]{:S(2)}, u32[]{:S(2)}) collective-permute-start(bf16[2,384,768]{2,1,0:T(8,128)(2,1)} %get-tuple-element.42), channel_id=1, source_target_pairs={{24,16},{28,20},{25,17},{29,21},{26,18},{30,22},{27,19},{31,23}} | collective-permute-start | bytes 3538952 | tf_op jit(solution)/shard_map/ppermute | solution.py:84
  271.0 49.1 %collective-permute-start.55 = (bf16[2,768,384]{2,1,0:T(8,128)(2,1)S(1)}, bf16[2,768,384]{2,1,0:T(8,128)(2,1)S(1)}, u32[]{:S(2)}, u32[]{:S(2)}) collective-permute-start(bf16[2,768,384]{2,1,0:T(8,128)(2,1)S(1)} %get-tuple-element.40), channel_id=1, source_target_pairs={{0,8},{4,12},{1,9},{5,13},{2,10},{6,14},{3,11},{7,15}} | collective-permute-start | bytes 3538952 | tf_op jit(solution)/shard_map/ppermute | solution.py:84
  272.3 49.5 %collective-permute-start.58 = (bf16[2,768,384]{2,1,0:T(8,128)(2,1)}, bf16[2,768,384]{2,1,0:T(8,128)(2,1)}, u32[]{:S(2)}, u32[]{:S(2)}) collective-permute-start(bf16[2,768,384]{2,1,0:T(8,128)(2,1)} %get-tuple-element.38), channel_id=1, source_target_pairs={{24,16},{28,20},{25,17},{29,21},{26,18},{30,22},{27,19},{31,23}} | collective-permute-start | bytes 3538952 | tf_op jit(solution)/shard_map/ppermute | solution.py:84
  304.2 29.9 %collective-permute-start.35 = (bf16[2,4,128,768]{3,2,0,1:T(8,128)(2,1)S(1)}, bf16[2,4,128,768]{3,2,0,1:T(8,128)(2,1)S(1)}, u32[]{:S(2)}, u32[]{:S(2)}) collective-permute-start(bf16[2,4,128,768]{3,2,0,1:T(8,128)(2,1)S(1)} %bitcast.252), channel_id=1, source_target_pairs={{0,1},{1,0},{2,3},{3,2},{4,5},{5,4},{6,7},{7,6},{8,9},{9,8},{10,11... | collective-permute-start | bytes 4718600 | tf_op jit(solution)/shard_map/ppermute | solution.py:66
  309.7 35.8 %collective-permute-start.62 = (bf16[2,384,768]{2,1,0:T(8,128)(2,1)}, bf16[2,384,768]{2,1,0:T(8,128)(2,1)}, u32[]{:S(2)}, u32[]{:S(2)}) collective-permute-start(bf16[2,384,768]{2,1,0:T(8,128)(2,1)} %get-tuple-element.110), channel_id=1, source_target_pairs={{0,8},{4,12},{8,16},{12,20},{1,9},{5,13},{9,17},{13,21},{2,10},{6,... | collective-permute-start | bytes 3538952 | tf_op jit(solution)/shard_map/ppermute | solution.py:84
  320.1 28.3 %collective-permute-start.65 = (bf16[2,384,768]{2,1,0:T(8,128)(2,1)}, bf16[2,384,768]{2,1,0:T(8,128)(2,1)}, u32[]{:S(2)}, u32[]{:S(2)}) collective-permute-start(bf16[2,384,768]{2,1,0:T(8,128)(2,1)} %get-tuple-element.111), channel_id=1, source_target_pairs={{16,8},{20,12},{24,16},{28,20},{17,9},{21,13},{25,17},{29,21},{18,... | collective-permute-start | bytes 3538952 | tf_op jit(solution)/shard_map/ppermute | solution.py:84
  325.1 45.7 %collective-permute-start.56 = (bf16[2,768,384]{2,1,0:T(8,128)(2,1)}, bf16[2,768,384]{2,1,0:T(8,128)(2,1)}, u32[]{:S(2)}, u32[]{:S(2)}) collective-permute-start(bf16[2,768,384]{2,1,0:T(8,128)(2,1)} %get-tuple-element.112), channel_id=1, source_target_pairs={{0,8},{4,12},{8,16},{12,20},{1,9},{5,13},{9,17},{13,21},{2,10},{6,... | collective-permute-start | bytes 3538952 | tf_op jit(solution)/shard_map/ppermute | solution.py:84
  332.6 42.1 %collective-permute-start.33 = (bf16[2,512,768]{2,1,0:T(8,128)(2,1)}, bf16[2,512,768]{2,1,0:T(8,128)(2,1)}, u32[]{:S(2)}, u32[]{:S(2)}) collective-permute-start(bf16[2,512,768]{2,1,0:T(8,128)(2,1)} %slice.227), channel_id=1, source_target_pairs={{0,2},{1,3},{2,0},{3,1},{4,6},{5,7},{6,4},{7,5},{8,10},{9,11},{10,... | collective-permute-start | bytes 4718600 | tf_op jit(solution)/shard_map/ppermute | solution.py:66
  338.8 43.3 %collective-permute-start.36 = (bf16[2,512,768]{2,1,0:T(8,128)(2,1)}, bf16[2,512,768]{2,1,0:T(8,128)(2,1)}, u32[]{:S(2)}, u32[]{:S(2)}) collective-permute-start(bf16[2,512,768]{2,1,0:T(8,128)(2,1)} %pad_maximum_fusion.7), channel_id=1, source_target_pairs={{0,4},{4,0},{8,12},{12,8},{16,20},{20,16},{24,28},{28,24},{1,5},{5... | collective-permute-start | bytes 4718600 | tf_op jit(solution)/shard_map/ppermute | solution.py:66
  345.4 39.1 %collective-permute-start.59 = (bf16[2,768,384]{2,1,0:T(8,128)(2,1)}, bf16[2,768,384]{2,1,0:T(8,128)(2,1)S(1)}, u32[]{:S(2)}, u32[]{:S(2)}) collective-permute-start(bf16[2,768,384]{2,1,0:T(8,128)(2,1)} %get-tuple-element.113), channel_id=1, source_target_pairs={{16,8},{20,12},{24,16},{28,20},{17,9},{21,13},{25,17},{29,21},{18,... | collective-permute-start | bytes 3538952 | tf_op jit(solution)/shard_map/ppermute | solution.py:84
  348.3 47.6 %collective-permute-start.63 = (bf16[2,384,768]{2,1,0:T(8,128)(2,1)S(1)}, bf16[2,384,768]{2,1,0:T(8,128)(2,1)S(1)}, u32[]{:S(2)}, u32[]{:S(2)}) collective-permute-start(bf16[2,384,768]{2,1,0:T(8,128)(2,1)S(1)} %add_convert_fusion.1), channel_id=1, source_target_pairs={{0,8},{4,12},{8,16},{12,20},{16,24},{20,28},{1,9},{5,13},{9,17},{1... | collective-permute-start | bytes 3538952 | tf_op jit(solution)/shard_map/ppermute | solution.py:84
  370.7 28.5 %collective-permute-start.66 = (bf16[2,384,768]{2,1,0:T(8,128)(2,1)S(1)}, bf16[2,384,768]{2,1,0:T(8,128)(2,1)S(1)}, u32[]{:S(2)}, u32[]{:S(2)}) collective-permute-start(bf16[2,384,768]{2,1,0:T(8,128)(2,1)S(1)} %add_convert_fusion), channel_id=1, source_target_pairs={{8,0},{12,4},{16,8},{20,12},{24,16},{28,20},{9,1},{13,5},{17,9},{2... | collective-permute-start | bytes 3538952 | tf_op jit(solution)/shard_map/ppermute | solution.py:84
  374.6 81.0 %collective-permute-start.57 = (bf16[2,768,384]{2,1,0:T(8,128)(2,1)}, bf16[2,768,384]{2,1,0:T(8,128)(2,1)}, u32[]{:S(2)}, u32[]{:S(2)}) collective-permute-start(bf16[2,768,384]{2,1,0:T(8,128)(2,1)} %add_convert_fusion.3), channel_id=1, source_target_pairs={{0,8},{4,12},{8,16},{12,20},{16,24},{20,28},{1,9},{5,13},{9,17},{1... | collective-permute-start | bytes 3538952 | tf_op jit(solution)/shard_map/ppermute | solution.py:84
  395.9 59.7 %collective-permute-start.60 = (bf16[2,768,384]{2,1,0:T(8,128)(2,1)}, bf16[2,768,384]{2,1,0:T(8,128)(2,1)}, u32[]{:S(2)}, u32[]{:S(2)}) collective-permute-start(bf16[2,768,384]{2,1,0:T(8,128)(2,1)} %add_convert_fusion.2), channel_id=1, source_target_pairs={{8,0},{12,4},{16,8},{20,12},{24,16},{28,20},{9,1},{13,5},{17,9},{2... | collective-permute-start | bytes 3538952 | tf_op jit(solution)/shard_map/ppermute | solution.py:84
  (88 other events, 979.8 us)

commit v2 on v1

v2 whole, which is shorter than its diff:
```python
from functools import partial, reduce

import jax
import jax.numpy as jnp
from jax import lax
from jax.experimental import pallas as pl
from jax.experimental.pallas import tpu as pltpu
from jax.sharding import PartitionSpec as P

HEADS = 12
HEAD_DIM = 64
EPS = 1e-06
LIMITS = (12, 16, 23, 32, 46, 64, 91)
SCALE = 0.125
HIGH = lax.Precision.HIGHEST
LOW = jnp.bfloat16
FULL = jnp.float32
ROWS = 128
VMEM_BYTES = 52 * 1024 * 1024


def bucket_index(relative):
    distance = jnp.abs(relative)
    far_bucket = reduce(
        lambda counted, boundary: counted + (distance >= boundary).astype(jnp.int32),
        LIMITS,
        jnp.full_like(distance, 8),
    )
    return jnp.where(distance < 8, distance, far_bucket) + 16 * (relative > 0).astype(jnp.int32)


def segment_ids(lengths, slots):
    ending = jnp.cumsum(lengths)
    places = jnp.arange(slots, dtype=jnp.int32)
    return jnp.sum((places[:, None] >= ending[None, :]).astype(jnp.int32), axis=1)


def rms_parts(values, gain):
    inverse = lax.rsqrt(jnp.mean(values * values, axis=-1, keepdims=True) + EPS)
    return (values * inverse * gain, inverse)


def norm_back(values, inverse, gain, upstream):
    scaled = upstream * gain
    grad_values = inverse * scaled - values * inverse * inverse * inverse * jnp.mean(
        values * scaled, axis=-1, keepdims=True
    )
    return (grad_values, jnp.sum(upstream * values * inverse, axis=0))


def softmax_rows(scores):
    highest = jnp.max(scores, axis=-1, keepdims=True)
    raised = jnp.exp(scores - highest)
    return raised / jnp.sum(raised, axis=-1, keepdims=True)


def mm(left, right, contract, out=FULL):
    return lax.dot_general(left, right, (contract, ((), ())), preferred_element_type=FULL).astype(
        out
    )


def small_cost(flops, bytes_accessed, transcendentals):
    return pl.CostEstimate(
        flops=flops // 64,
        bytes_accessed=bytes_accessed // 64,
        transcendentals=transcendentals // 64,
    )


def nothing_kernel(*refs):
    del refs


def after(values, deps):
    values, deps = list(values), list(deps)
    anywhere = pl.BlockSpec(memory_space=pl.ANY)
    return pl.pallas_call(
        nothing_kernel,
        in_specs=[anywhere] * (len(values) + len(deps)),
        out_specs=[anywhere] * len(values),
        out_shape=[jax.ShapeDtypeStruct(value.shape, value.dtype) for value in values],
        input_output_aliases={number: number for number in range(len(values))},
        name="after",
    )(*values, *deps)


def swap(value, dim):
    axis, mask = dim
    count = lax.axis_size(axis)
    return lax.ppermute(value, axis, [(i, i ^ mask) for i in range(count)])


def bit_of(dim):
    axis, mask = dim
    return (lax.axis_index(axis) & mask) != 0


def stage_pair(value, dim):
    other = swap(value, dim)
    return jnp.where(bit_of(dim), jnp.stack((other, value)), jnp.stack((value, other)))


def ring_shift(value, places, by):
    count = 2 * places
    return lax.ppermute(value, "fsdp", [(i, (i - 2 * by) % count) for i in range(count)])


def z_gather(value, places, place):
    parts = jnp.stack([value] + [ring_shift(value, places, by) for by in range(1, places)])
    return lax.dynamic_slice_in_dim(
        jnp.concatenate((parts, parts)), lax.rem(places - place, places), places, 0
    )


def z_groups(places):
    return [[2 * place + side for place in range(places)] for side in (0, 1)]


def gather_step(held, dim):
    keys = list(held)
    value = jnp.stack([held[key] for key in keys]) if len(keys) > 1 else held[keys[0]]
    return swap(value, dim)


def gather_join(held, dim, arrived):
    keys = list(held)
    joined = dict(held)
    for number, key in enumerate(keys):
        joined[tuple(sorted(key + (dim,)))] = arrived[number] if len(keys) > 1 else arrived
    return joined


def gather_blocks(value, dims):
    held = {(): value}
    for dim in dims:
        held = gather_join(held, dim, gather_step(held, dim))
    return held


def gather_halves(value, dims):
    half = value.shape[0] // 2
    held = [{(): value[:half]}, {(): value[half:]}]
    brought = []
    for number in range(len(dims)):
        steps = (dims[number], dims[len(dims) - 1 - number])
        arrived = [gather_step(part, dim) for part, dim in zip(held, steps)]
        brought.append(arrived)
        held = [gather_join(*of) for of in zip(held, steps, arrived)]
    upper, lower = held
    blocks = jnp.stack([jnp.concatenate((upper[key], lower[key])) for key in sorted(upper)])
    return (blocks, brought)


def scatter_step(held, dim):
    stay = [key for key in held if dim not in key]
    leave = [tuple(sorted(key + (dim,))) for key in stay]
    sent = jnp.stack([held[key].astype(LOW) for key in leave])
    arrived = swap(sent, dim)
    return {
        key: held[key].astype(FULL) + arrived[number].astype(FULL)
        for number, key in enumerate(stay)
    }


def scatter_halves(blocks, keys, dims):
    half = blocks.shape[1] // 2
    upper = {key: blocks[number, :half] for number, key in enumerate(keys)}
    lower = {key: blocks[number, half:] for number, key in enumerate(keys)}
    between = ()
    for number in range(len(dims)):
        upper = scatter_step(upper, dims[len(dims) - 1 - number])
        lower = scatter_step(lower, dims[number])
        if number == 0 and len(dims) > 1:
            upper = {key: value.astype(LOW) for key, value in upper.items()}
            lower = {key: value.astype(LOW) for key, value in lower.items()}
            between = list(upper.values()) + list(lower.values())
    return (jnp.concatenate((upper[()], lower[()])), between)


def dense_gather(value, places, place, dims, core):
    columns = value.shape[1]
    half = (columns // 256) * 128
    near = z_gather(value, places, place)
    wanted = ("z", dims[0]) + tuple(sorted(dims[1:], reverse=True)) + ("core", "rows", "columns")

    def run(part, order):
        axes = ("z", "rows", "columns")
        for dim in order:
            part = stage_pair(part, dim)
            axes = (dim,) + axes
        part = stage_pair(part, core)
        axes = ("core",) + axes
        return part.transpose([axes.index(name) for name in wanted]).reshape(-1, part.shape[-1])

    first = run(near[..., :half], dims)
    second = run(near[..., half:], list(reversed(dims)))
    return (jnp.concatenate((first, second), axis=1), near)


def dense_scatter(value, peer_dims, rows):
    bits = len(peer_dims)
    part = value.reshape((-1,) + (2,) * bits + (rows, value.shape[1]))
    for number, dim in enumerate(peer_dims):
        spot = bits - number
        own = bit_of(dim).astype(jnp.int32)
        keep = lax.dynamic_index_in_dim(part, own, spot, keepdims=False)
        send = lax.dynamic_index_in_dim(part, 1 - own, spot, keepdims=False)
        part = (keep.astype(FULL) + swap(send, dim).astype(FULL)).astype(LOW)
    return part


def dense_finish(part):
    arrived = lax.all_to_all(part, "fsdp", split_axis=0, concat_axis=0, tiled=True)
    return jnp.sum(arrived.astype(FULL), axis=0)


def sum_everywhere(value):
    for axis in ("dp", "fsdp"):
        mask = 1
        while mask < lax.axis_size(axis):
            value = value + swap(value, (axis, mask))
            mask *= 2
    return value


def diagonal_hot(slots, bucket_count):
    width = 2 * slots
    lanes = jnp.arange(width, dtype=jnp.int32)[None, :]
    rows = jnp.arange(8, dtype=jnp.int32)[:, None]
    diagonal = (lanes - rows + (ROWS - 1)) % width
    bucket = jnp.where(diagonal < width - 1, bucket_index(diagonal - (slots - 1)), -1)
    return (bucket[:, :, None] == jnp.arange(bucket_count, dtype=jnp.int32)).astype(FULL)


def attend_kernel(query, key, value, base, seg_col, seg_row, out, probs, toeplitz):
    slots = query.shape[0]
    lanes = lax.broadcasted_iota(jnp.int32, (1, 2 * HEAD_DIM), 1)
    total = [None] * (slots // ROWS)
    for head in range(2):
        mine = (lanes >= head * HEAD_DIM) & (lanes < (head + 1) * HEAD_DIM)
        table = base[head]
        size = 8
        while size < ROWS:
            table = jnp.concatenate((table, pltpu.roll(table, size, 1)), axis=0)
            size *= 2
        toeplitz[...] = table
        value_head = jnp.where(mine, value[...], 0).astype(LOW)
        for block in range(slots // ROWS):
            rows = pl.ds(block * ROWS, ROWS)
            query_head = jnp.where(mine, query[rows, :], 0).astype(LOW)
            shift = slots - ROWS - block * ROWS
            scores = mm(query_head, key[...], ((1,), (1,))) * SCALE
            scores = scores + toeplitz[:, shift : shift + slots]
            scores = jnp.where(seg_col[rows, :] == seg_row[...], scores, -1e30)
            highest = jnp.max(scores, axis=-1, keepdims=True)
            raised = jnp.exp(scores - highest)
            low = (raised / jnp.sum(raised, axis=-1, keepdims=True)).astype(LOW)
            probs[head, rows, :] = low
            part = mm(low, value_head, ((1,), (0,)))
            total[block] = part if head == 0 else total[block] + part
    for block in range(slots // ROWS):
        out[pl.ds(block * ROWS, ROWS), :] = total[block].astype(LOW)


def attend_forward(projected, base, seg_col, seg_row):
    slots = projected.shape[0]
    width = projected.shape[1] // 3
    pairs = HEADS // 2
    lanes = 2 * HEAD_DIM
    return pl.pallas_call(
        attend_kernel,
        grid=(pairs,),
        in_specs=[
            pl.BlockSpec((slots, lanes), lambda p: (0, p)),
            pl.BlockSpec((slots, lanes), lambda p: (0, p + pairs)),
            pl.BlockSpec((slots, lanes), lambda p: (0, p + 2 * pairs)),
            pl.BlockSpec((2, 8, 2 * slots), lambda p: (p, 0, 0)),
            pl.BlockSpec((slots, 1), lambda p: (0, 0)),
            pl.BlockSpec((1, slots), lambda p: (0, 0)),
        ],
        out_specs=[
            pl.BlockSpec((slots, lanes), lambda p: (0, p)),
            pl.BlockSpec((2, slots, slots), lambda p: (p, 0, 0)),
        ],
        out_shape=[
            jax.ShapeDtypeStruct((slots, width), LOW),
            jax.ShapeDtypeStruct((HEADS, slots, slots), LOW),
        ],
        scratch_shapes=[pltpu.VMEM((ROWS, 2 * slots), FULL)],
        compiler_params=pltpu.CompilerParams(vmem_limit_bytes=VMEM_BYTES),
        cost_estimate=small_cost(
            flops=HEADS * slots * slots * HEAD_DIM * 16,
            bytes_accessed=HEADS * slots * slots * 2 + 8 * slots * width,
            transcendentals=HEADS * slots * slots,
        ),
        name="attend_forward",
    )(projected, projected, projected, base, seg_col, seg_row)


def attend_back_kernel(
    query, key, value, grad, probs, out_query, out_key, out_value, diagonals, lined, scores_low
):
    slots = query.shape[0]
    lanes = lax.broadcasted_iota(jnp.int32, (1, 2 * HEAD_DIM), 1)
    query_total = [None] * (slots // ROWS)
    key_total = value_total = None
    for head in range(2):
        mine = (lanes >= head * HEAD_DIM) & (lanes < (head + 1) * HEAD_DIM)
        key_head = jnp.where(mine, key[...], 0).astype(LOW)
        grad_head = jnp.where(mine, grad[...], 0).astype(LOW)
        query_head = jnp.where(mine, query[...], 0).astype(LOW)
        lined[...] = jnp.zeros_like(lined)
        for block in range(slots // ROWS):
            rows = pl.ds(block * ROWS, ROWS)
            soft = probs[head, rows, :].astype(FULL)
            grad_rows = jnp.where(mine, grad[rows, :], 0).astype(LOW)
            weighted = soft * mm(grad_rows, value[...], ((1,), (1,)))
            back = weighted - soft * jnp.sum(weighted, axis=-1, keepdims=True)
            low = back.astype(LOW)
            scores_low[rows, :] = low
            shift = slots - ROWS - block * ROWS
            lined[:, shift : shift + slots] += low.astype(FULL)
            part = mm(low, key_head, ((1,), (0,)))
            query_total[block] = part if head == 0 else query_total[block] + part
        key_part = mm(scores_low[...], query_head, ((0,), (0,)))
        value_part = mm(probs[head], grad_head, ((0,), (0,)))
        key_total = key_part if head == 0 else key_total + key_part
        value_total = value_part if head == 0 else value_total + value_part
        table = lined[...]
        size = ROWS
        while size > 8:
            size //= 2
            table = table[:size] + pltpu.roll(table[size:], 2 * slots - size, 1)
        diagonals[head] = table
    out_key[...] = (key_total * SCALE).astype(LOW)
    out_value[...] = value_total.astype(LOW)
    for block in range(slots // ROWS):
        out_query[pl.ds(block * ROWS, ROWS), :] = (query_total[block] * SCALE).astype(LOW)


def attend_back(projected, grad_attended, probs, begin, count):
    slots = projected.shape[0]
    pairs = HEADS // 2
    lanes = 2 * HEAD_DIM
    width = count * lanes
    column = pl.BlockSpec((slots, lanes), lambda p: (0, p))

    def column_from(offset):
        return pl.BlockSpec((slots, lanes), lambda p: (0, p + offset))

    return pl.pallas_call(
        attend_back_kernel,
        grid=(count,),
        in_specs=[
            column_from(begin),
            column_from(begin + pairs),
            column_from(begin + 2 * pairs),
            column_from(begin),
            pl.BlockSpec((2, slots, slots), lambda p: (p + begin, 0, 0)),
        ],
        out_specs=[
            column,
            column,
            column,
            pl.BlockSpec((2, 8, 2 * slots), lambda p: (p, 0, 0)),
        ],
        out_shape=[jax.ShapeDtypeStruct((slots, width), LOW)] * 3
        + [jax.ShapeDtypeStruct((2 * count, 8, 2 * slots), FULL)],
        scratch_shapes=[pltpu.VMEM((ROWS, 2 * slots), FULL), pltpu.VMEM((slots, slots), LOW)],
        compiler_params=pltpu.CompilerParams(vmem_limit_bytes=VMEM_BYTES),
        cost_estimate=small_cost(
            flops=2 * count * slots * slots * HEAD_DIM * 32,
            bytes_accessed=2 * count * slots * slots * 2 + 14 * slots * width,
            transcendentals=0,
        ),
        name="attend_back",
    )(projected, projected, projected, grad_attended, probs)


def expert_forward_kernel(rows, first, second, y_out, hidden_out, slope_out, y_sum):
    chunk = pl.program_id(0)
    count = rows.shape[1]
    step = min(256, count)

    @pl.when(chunk == 0)
    def _():
        y_sum[...] = jnp.zeros_like(y_sum)

    for block in range(count // step):
        some = pl.ds(block * step, step)
        pre = mm(rows[0, some, :], first[0], ((1,), (0,)))
        normal_cdf = 0.5 + 0.5 * lax.erf(pre * 0.7071067811865476)
        slope = normal_cdf + pre * jnp.exp(-0.5 * pre * pre) * 0.3989422804014327
        hidden = (pre * normal_cdf).astype(LOW)
        hidden_out[0, some, :] = hidden
        slope_out[0, some, :] = slope.astype(LOW)
        y_sum[some, :] += mm(hidden, second[0], ((1,), (0,)))

    @pl.when(chunk == pl.num_programs(0) - 1)
    def _():
        y_out[...] = y_sum[...].astype(LOW)


def expert_specs(expert, count, width, units):
    def part(*shape):
        return pl.BlockSpec((1,) + shape, lambda c: (c, 0, 0))

    rows_in = pl.BlockSpec((1, count, width), lambda c: (expert, 0, 0))
    rows_out = pl.BlockSpec((count, width), lambda c: (0, 0))
    return (rows_in, rows_out, part(width, units), part(units, width), part(count, units))


def expert_forward(expert, rows, first, second):
    chunks, width, units = first.shape
    count = rows.shape[1]
    rows_in, rows_out, first_spec, second_spec, unit_spec = expert_specs(expert, count, width, units)
    hidden_shape = jax.ShapeDtypeStruct((chunks, count, units), LOW)
    return pl.pallas_call(
        expert_forward_kernel,
        grid=(chunks,),
        in_specs=[rows_in, first_spec, second_spec],
        out_specs=[rows_out, unit_spec, unit_spec],
        out_shape=[jax.ShapeDtypeStruct((count, width), LOW), hidden_shape, hidden_shape],
        scratch_shapes=[pltpu.VMEM((count, width), FULL)],
        compiler_params=pltpu.CompilerParams(vmem_limit_bytes=VMEM_BYTES),
        cost_estimate=small_cost(
            flops=chunks * 4 * count * width * units,
            bytes_accessed=4 * count * width + 4 * chunks * (width + count) * units,
            transcendentals=2 * chunks * count * units,
        ),
        name="expert_forward",
    )(rows, first, second)


def expert_back_kernel(
    rows, grads, first, second, hidden, slope, back_out, first_out, second_out, back_sum, pre_low
):
    chunk = pl.program_id(0)
    count = rows.shape[1]
    step = min(256, count)

    @pl.when(chunk == 0)
    def _():
        back_sum[...] = jnp.zeros_like(back_sum)

    for block in range(count // step):
        some = pl.ds(block * step, step)
        grad_hidden = mm(grads[0, some, :], second[0], ((1,), (1,)))
        grad_pre = (grad_hidden * slope[0, some, :].astype(FULL)).astype(LOW)
        pre_low[some, :] = grad_pre
        back_sum[some, :] += mm(grad_pre, first[0], ((1,), (1,)))
    first_out[0] = mm(rows[0], pre_low[...], ((0,), (0,)), LOW)
    second_out[0] = mm(hidden[0], grads[0], ((0,), (0,)), LOW)

    @pl.when(chunk == pl.num_programs(0) - 1)
    def _():
        back_out[...] = back_sum[...].astype(LOW)


def expert_back(expert, rows, grads, first, second, hidden, slope):
    chunks, width, units = first.shape
    count = rows.shape[1]
    rows_in, rows_out, first_spec, second_spec, unit_spec = expert_specs(expert, count, width, units)
    return pl.pallas_call(
        expert_back_kernel,
        grid=(chunks,),
        in_specs=[rows_in, rows_in, first_spec, second_spec, unit_spec, unit_spec],
        out_specs=[rows_out, first_spec, second_spec],
        out_shape=[
            jax.ShapeDtypeStruct((count, width), LOW),
            jax.ShapeDtypeStruct(first.shape, LOW),
            jax.ShapeDtypeStruct(second.shape, LOW),
        ],
        scratch_shapes=[pltpu.VMEM((count, width), FULL), pltpu.VMEM((count, units), LOW)],
        compiler_params=pltpu.CompilerParams(vmem_limit_bytes=VMEM_BYTES),
        cost_estimate=small_cost(
            flops=chunks * 8 * count * width * units,
            bytes_accessed=6 * count * width + 4 * chunks * (2 * width + count) * units,
            transcendentals=0,
        ),
        name="expert_back",
    )(rows, grads, first, second, hidden, slope)


def body(
    tokens,
    cotangent,
    seq_lens,
    routes,
    norm_gains,
    qkv_weight,
    out_weight,
    router_weight,
    rel_bias,
    expert_in,
    expert_out,
):
    tok_count, width = tokens.shape
    bucket_count = rel_bias.shape[0]
    shard_rows = qkv_weight.shape[0]
    experts_all = router_weight.shape[1]
    local_experts = expert_in.shape[0]
    capacity = 2 * tok_count // experts_all
    places = lax.axis_size("fsdp") // 2
    place = lax.axis_index("fsdp") // 2
    peer = lax.axis_index("dp")
    peer_count = lax.axis_size("dp")
    core = ("dp", 1)
    dims = [("fsdp", 1)]
    mask = 2
    while mask < peer_count:
        dims.append(("dp", mask))
        mask *= 2

    spare = -(4 * width + experts_all + 2) % 128
    packed = jnp.concatenate(
        (
            qkv_weight,
            out_weight,
            router_weight,
            norm_gains.T,
            jnp.zeros((shard_rows, spare), LOW),
        ),
        axis=1,
    )
    dense, near = dense_gather(packed, places, place, dims, core)
    qkv_full = dense[:, : 3 * width]
    out_full = dense[:, 3 * width : 4 * width]
    router_full = dense[:, 4 * width : 4 * width + experts_all]
    gains_float = dense[:, 4 * width + experts_all : 4 * width + experts_all + 2].T.astype(FULL)

    groups = z_groups(places)
    weights = []
    for expert in range(local_experts):
        own = (expert_in[expert], expert_out[expert])
        if expert > 0:
            own = after(own, (near,))
        weights.append([lax.all_gather(v, "fsdp", axis=0, axis_index_groups=groups) for v in own])

    chosen = routes[:, 0]
    chosen_hot = chosen[:, None] == jnp.arange(experts_all, dtype=jnp.int32)[None, :]
    order = jnp.arange(tok_count, dtype=jnp.int32)
    earlier = (order[:, None] > order[None, :]).astype(LOW)
    rank_all = jnp.dot(earlier, chosen_hot.astype(LOW), preferred_element_type=FULL)
    rank_in = jnp.sum(jnp.where(chosen_hot, rank_all, 0.0), axis=1).astype(jnp.int32)
    slots_of = gather_blocks((chosen * capacity + rank_in)[None, :], dims)
    keys = sorted(slots_of)
    slots_near = jnp.stack([slots_of[key][0] for key in keys])
    local_slots = local_experts * capacity
    slot_ids = jnp.arange(local_slots, dtype=jnp.int32).reshape(local_experts, capacity)

    def hot_of(owner):
        wanted = owner * local_slots + slot_ids
        return (slots_near[:, None, None, :] == wanted[None, :, :, None]).astype(LOW)

    hot_own, hot_other = hot_of(peer), hot_of(peer ^ 1)
    segment = segment_ids(seq_lens[0], tok_count)
    bucket_hot = diagonal_hot(tok_count, bucket_count)
    base = jnp.einsum("rjb,bh->hrj", bucket_hot, rel_bias, precision=HIGH)

    inputs = tokens.astype(FULL)
    normed_one, inverse_one = rms_parts(inputs, gains_float[0])
    normed_low = normed_one.astype(LOW)
    projected = jnp.dot(normed_low, qkv_full, preferred_element_type=FULL).astype(LOW)
    attended, probs = attend_forward(projected, base, segment[:, None], segment[None, :])
    hidden_one = inputs + jnp.dot(attended, out_full, preferred_element_type=FULL)
    normed_two, inverse_two = rms_parts(hidden_one, gains_float[1])
    normed_two_low = normed_two.astype(LOW)
    router_soft = softmax_rows(jnp.dot(normed_two_low, router_full, preferred_element_type=FULL))
    gate_value = jnp.sum(jnp.where(chosen_hot, router_soft, 0.0), axis=1)
    upstream = cotangent.astype(FULL)
    grad_y = (gate_value[:, None] * upstream).astype(LOW)

    def pick(hot, blocks):
        return jnp.einsum("bjst,btd->jbsd", hot, blocks, preferred_element_type=FULL).astype(LOW)

    def to_rows(blocks):
        other = swap(pick(hot_other, blocks), core)
        both = jnp.stack((pick(hot_own, blocks), other), axis=1)
        return both.reshape(local_experts, -1, width)

    hot_all = jnp.concatenate((hot_own, hot_other), axis=1).reshape(
        len(keys), 2 * local_slots, tok_count
    )

    def from_rows(values, ready=()):
        shaped = [value.reshape(2, len(keys), capacity, width) for value in values]
        parts = [part[0] for part in shaped] + [swap(part[1], core) for part in shaped]
        joined = jnp.concatenate(parts, axis=1)
        if ready:
            (joined,) = after((joined,), ready)
        return jnp.einsum("bst,bsd->btd", hot_all, joined, preferred_element_type=FULL).astype(LOW)

    blocks, brought = gather_halves(normed_two_low, dims)
    rows = to_rows(blocks)
    grad_half = tok_count // 2
    grad_parts = after((grad_y[:grad_half], grad_y[grad_half:]), brought[0])
    held = [{(): part} for part in grad_parts]
    grad_brought = []
    forwards = []
    for number in range(len(dims)):
        steps = (dims[number], dims[len(dims) - 1 - number])
        arrived = [gather_step(part, dim) for part, dim in zip(held, steps)]
        if number == len(dims) - 1:
            (tied,) = after((rows,), sum(grad_brought, []))
            forwards.append(expert_forward(0, tied, *weights[0]))
            arrived = after(arrived, (forwards[0][0],))
        grad_brought.append(arrived)
        held = [gather_join(*of) for of in zip(held, steps, arrived)]
    grad_blocks = jnp.stack(
        [jnp.concatenate((held[0][key], held[1][key])) for key in sorted(held[0])]
    )
    grads = to_rows(grad_blocks)
    backs = []
    for expert in range(local_experts):
        if expert > 0:
            (tied,) = after((rows,), (backs[-1][0],))
            forwards.append(expert_forward(expert, tied, *weights[expert]))
        tied = grads
        if expert == local_experts - 1:
            y_raw = from_rows([forward[0] for forward in forwards])
            token_y, y_between = scatter_halves(y_raw, keys, dims)
            (tied,) = after((grads,), (y_raw,))
        backs.append(expert_back(expert, rows, tied, *weights[expert], *forwards[expert][1:]))
    in_grad, out_expert_grad = (
        jnp.stack(
            [
                lax.psum_scatter(
                    back[which], "fsdp", scatter_dimension=0, axis_index_groups=groups, tiled=False
                ).astype(FULL)
                for back in backs
            ]
        )
        for which in (1, 2)
    )
    grad_rows, _ = scatter_halves(
        from_rows([back[0] for back in backs], y_between), keys, dims
    )

    mixed = (hidden_one + gate_value[:, None] * token_y).astype(LOW)
    grad_gate = jnp.sum(upstream * token_y, axis=1)
    grad_logits = router_soft * (
        jnp.where(chosen_hot, grad_gate[:, None], 0.0) - (gate_value * grad_gate)[:, None]
    )
    router_local = jnp.dot(normed_two_low.astype(FULL).T, grad_logits, precision=HIGH)
    grad_normed_two = grad_rows + jnp.dot(
        grad_logits, router_full.astype(FULL).T, precision=HIGH
    )
    grad_from_two, gain_grad_two = norm_back(
        hidden_one, inverse_two, gains_float[1], grad_normed_two
    )
    grad_hidden_one = upstream + grad_from_two
    grad_attn_low = grad_hidden_one.astype(LOW)
    out_local = jnp.einsum("td,te->de", attended, grad_attn_low, preferred_element_type=FULL)
    grad_attended = mm(grad_attn_low, out_full, ((1,), (1,)), LOW)
    peer_dims = [core] + dims[1:]
    spare_out = -(experts_all + 2) % 128
    out_panel = jnp.concatenate(
        (
            out_local.astype(LOW),
            router_local.astype(LOW),
            gain_grad_two[:, None].astype(LOW),
            jnp.zeros((width, spare_out + 1), LOW),
        ),
        axis=1,
    )
    (grad_attended,) = after((grad_attended,), (out_panel,))
    out_part = dense_scatter(out_panel, peer_dims, shard_rows)
    pairs = HEADS // 2
    halves = ((0, pairs // 2), (pairs // 2, pairs - pairs // 2))
    grad_normed_one = 0.0
    diagonals, sums = [], []
    for number, (begin, count) in enumerate(halves):
        if number > 0:
            (grad_attended,) = after((grad_attended,), (panel, out_part))
        *grad_parts, lined = attend_back(projected, grad_attended, probs, begin, count)
        diagonals.append(lined)
        piece = jnp.concatenate(grad_parts, axis=1)
        lanes = count * 2 * HEAD_DIM
        weight = jnp.concatenate(
            [
                qkv_full[:, width * part + begin * 2 * HEAD_DIM :][:, :lanes]
                for part in range(3)
            ],
            axis=1,
        )
        grad_normed_one = grad_normed_one + mm(piece, weight, ((1,), (1,)))
        qkv_local = jnp.einsum("td,te->de", normed_low, piece, preferred_element_type=FULL)
        panel = qkv_local.astype(LOW)
        sums.append(dense_scatter(panel, peer_dims, shard_rows))
    out_sum = dense_finish(out_part)
    last_sum = dense_finish(jnp.concatenate(sums, axis=-1))
    starts = [0] + [3 * count * 2 * HEAD_DIM for _, count in halves][:-1]
    sums = [last_sum[:, start:] for start in starts]
    grad_from_one, gain_grad_one = norm_back(inputs, inverse_one, gains_float[0], grad_normed_one)
    tokens_grad = grad_hidden_one + grad_from_one
    bias_local = jnp.einsum(
        "hrj,rjb->bh", jnp.concatenate(diagonals), bucket_hot, precision=HIGH
    )
    gain_rows = width // 128
    small = jnp.concatenate((bias_local.reshape(-1, 128), gain_grad_one.reshape(-1, 128)))
    small = sum_everywhere(small)
    bias_grad = small[:-gain_rows].reshape(bias_local.shape)
    device = lax.axis_index("fsdp") * peer_count + peer
    gain_one = lax.dynamic_slice_in_dim(
        small[-gain_rows:].reshape(-1), device * shard_rows, shard_rows
    )
    gains_grad = jnp.stack((gain_one, out_sum[:, width + experts_all]))
    router_grad = out_sum[:, width : width + experts_all]
    out_grad = out_sum[:, :width]
    qkv_grad = jnp.concatenate(
        [
            sums[number][:, part * count * 2 * HEAD_DIM :][:, : count * 2 * HEAD_DIM]
            for part in range(3)
            for number, (_, count) in enumerate(halves)
        ],
        axis=1,
    )
    return (
        mixed,
        tokens_grad,
        gains_grad,
        qkv_grad,
        out_grad,
        router_grad,
        bias_grad,
        in_grad,
        out_expert_grad,
    )


def solution(mesh):
    rows = P(("fsdp", "dp"), None)
    columns = P(None, ("fsdp", "dp"))
    experts = (P("dp", None, "fsdp"), P("dp", "fsdp", None))
    return jax.shard_map(
        body,
        mesh=mesh,
        in_specs=(rows, rows, rows, rows, columns, rows, rows, rows, P()) + experts,
        out_specs=(rows, rows, columns, rows, rows, rows, P()) + experts,
        check_vma=False,
    )
```

time: 520 us -> 480 us (0.923)
  starting transfers between devices: 98.2 us -> 51.9 us
  waiting for transfers between devices: 205 us -> 170 us
  local copies, waits for them, and re-layouts: 35.3 us -> 54 us
  Pallas kernels: 81.3 us -> 95.6 us
  between operations: 2.6 us -> 16.3 us
    ppermute x24 -> x0, waiting for transfers between devices: 89.3 us -> none  [line_shift(): return lax.ppermute(value, 'fsdp', pairs)]
    ppermute x31 -> x41, waiting for transfers between devices: 67.8 us -> 135 us  [swap(): return lax.ppermute(value, axis, [(i, i ^ mask) for i in range(count)])]
    ppermute x24 -> x0, starting transfers between devices: 54.8 us -> none  [line_shift(): return lax.ppermute(value, 'fsdp', pairs)]
    ppermute x12 -> x3, waiting for transfers between devices: 47.8 us -> 14.1 us  [ring_shift(): lax.ppermute(value, 'fsdp', [(i, (i - 2 * by) % count) for i in range(cou...]
    all_gather x0 -> x4, waiting for transfers between devices: none -> 18.1 us  [body(): lax.all_gather(v, 'fsdp', axis=0, axis_index_groups=groups)]
    unnamed x126 -> x220, local copies, waits for them, and re-layouts: 10.1 us -> 25.7 us
    pallas_call x3 -> x15, Pallas kernels: 66 us -> 80.2 us  [the longest x2 38 us: expert_back(): pl.pallas_call(expert_back_kernel, grid=(chunks,), in_specs=[rows_in, row...]
    another operation x9 -> x21, other arithmetic: 2.72 us -> 15.9 us  [the longest x2 5.62 us: body(): jnp.stack([lax.psum_scatter(back[which], 'fsdp', scatter_dimension=0, axi...]
  transfers between devices with their start and end apart: 67 -> 54, of which waited for: 27 -> 26; matrix products, arithmetic and copies ran while one was open for 22% -> 26% of each run, Pallas kernels for 11% -> 20%
where the time goes in v2:
time: 480 us; the launch traced here: 471 us
  waiting for transfers between devices  170 us (35%)
  Pallas kernels  95.6 us (20%)
  local copies, waits for them, and re-layouts  54 us (11%)
  starting transfers between devices  51.9 us (11%)
  other arithmetic  44.3 us (9%)
  matrix products  39 us (8%)
  between operations  16.3 us (3%)
    ppermute x41, waiting for transfers between devices, swap(): return lax.ppermute(value, axis, [(i, i ^ mask) for i in range(count)])  135 us
    pallas_call x2, Pallas kernels, expert_back(): pl.pallas_call(expert_back_kernel, grid=(chunks,), in_specs=[rows_in, row...  38 us
    ppermute x41, starting transfers between devices, swap(): return lax.ppermute(value, axis, [(i, i ^ mask) for i in range(count)])  37.1 us
    unnamed x220, local copies, waits for them, and re-layouts  25.7 us
    pallas_call x2, Pallas kernels, expert_forward(): pl.pallas_call(expert_forward_kernel, grid=(chunks,), in_specs=[rows_in,...  24.4 us
    all_gather x4, waiting for transfers between devices, body(): lax.all_gather(v, 'fsdp', axis=0, axis_index_groups=groups)  18.1 us
    pallas_call x2, Pallas kernels, attend_back(): pl.pallas_call(attend_back_kernel, grid=(count,), in_specs=[column_from(b...  17.9 us
    pallas_call x1, Pallas kernels, attend_forward(): pl.pallas_call(attend_kernel, grid=(pairs,), in_specs=[pl.BlockSpec((slot...  15.4 us
  transfers between devices with their start and end apart: 54, of which 26 were waited for; matrix products, arithmetic and copies ran while one was open for 26% of the time, Pallas kernels for 20%

profile of v2, /device:TPU:0, one launch (start us, length us, event | category | flops | bytes accessed | tf_op | source)
XLA Modules:
  0.0 470.9 jit_solution(18159821680766745491)
XLA Ops:
  10.2 5.1 %collective-permute-start = (bf16[24,3200]{1,0:T(8,128)(2,1)S(1)}, bf16[24,3200]{1,0:T(8,128)(2,1)S(1)}, u32[]{:S(2)}, u32[]{:S(2)}) collective-permute-start(bf16[24,3200]{1,0:T(8,128)(2,1)S(1)} %concatenate.174), channel_id=1, source_target_pairs={{0,24},{4,28},{8,0},{12,4},{16,8},{20,12},{24,16},{28,20},{1,25},{... | collective-permute-start | bytes 460808 | tf_op jit(solution)/shard_map/ppermute | solution.py:106
  23.6 14.1 %collective-permute-done.1 = bf16[24,3200]{1,0:T(8,128)(2,1)} collective-permute-done((bf16[24,3200]{1,0:T(8,128)(2,1)S(1)}, bf16[24,3200]{1,0:T(8,128)(2,1)}, u32[]{:S(2)}, u32[]{:S(2)}) %collective-permute-start.1) | collective-permute-done | bytes 153632 | tf_op jit(solution)/shard_map/ppermute | solution.py:106
  44.9 5.0 %collective-permute-done.6 = bf16[4,24,1536]{2,1,0:T(8,128)(2,1)S(1)} collective-permute-done((bf16[4,24,1536]{2,1,0:T(8,128)(2,1)S(1)}, bf16[4,24,1536]{2,1,0:T(8,128)(2,1)S(1)}, u32[]{:S(2)}, u32[]{:S(2)}) %collective-permute-start.6) | collective-permute-done | bytes 294944 | tf_op jit(solution)/shard_map/ppermute | solution.py:91
  54.7 6.7 %collective-permute-done.7 = bf16[2,4,24,1536]{3,2,1,0:T(8,128)(2,1)S(1)} collective-permute-done((bf16[2,4,24,1536]{3,2,1,0:T(8,128)(2,1)S(1)}, bf16[2,4,24,1536]{3,2,1,0:T(8,128)(2,1)S(1)}, u32[]{:S(2)}, u32[]{:S(2)}) %collective-permute-start.7) | collective-permute-done | bytes 589856 | tf_op jit(solution)/shard_map/ppermute | solution.py:91
  69.0 3.5 convolution_convert_fusion.query.key.value
  72.5 15.4 %attend_forward.1 = (bf16[512,768]{1,0:T(8,128)(2,1)S(1)}, bf16[12,512,512]{2,1,0:T(8,128)(2,1)}) custom-call(bf16[512,2304]{1,0:T(8,128)(2,1)} %convolution_convert_fusion.query.key.value, bf16[512,2304]{1,0:T(8,128)(2,1)} %convolution_convert_fusion.query.key.value, bf16[512,2304]{1,0:T(8,128)(2,1)} %convolution_convert_fusion.query.key.value, ...), custom_call_target="tpu_custom_call" | custom-call | flops 50331648 | bytes 147456 | tf_op jit(solution)/shard_map/attend_forward/pallas_call | solution.py:271
  95.7 5.9 %collective-permute-done.11.refs_2_ = bf16[256,768]{1,0:T(8,128)(2,1)S(1)} collective-permute-done((bf16[256,768]{1,0:T(8,128)(2,1)}, bf16[256,768]{1,0:T(8,128)(2,1)S(1)}, u32[]{:S(2)}, u32[]{:S(2)}) %collective-permute-start.11) | collective-permute-done | bytes 393248 | tf_op jit(solution)/shard_map/ppermute | solution.py:91
  107.7 14.0 %collective-permute-done.12 = bf16[2,256,768]{2,1,0:T(8,128)(2,1)S(1)} collective-permute-done((bf16[2,256,768]{2,1,0:T(8,128)(2,1)S(1)}, bf16[2,256,768]{2,1,0:T(8,128)(2,1)S(1)}, u32[]{:S(2)}, u32[]{:S(2)}) %collective-permute-start.12) | collective-permute-done | bytes 786464 | tf_op jit(solution)/shard_map/ppermute | solution.py:91
  130.2 9.2 %collective-permute-done.17.refs_2_ = bf16[256,768]{1,0:T(8,128)(2,1)S(1)} collective-permute-done((bf16[256,768]{1,0:T(8,128)(2,1)}, bf16[256,768]{1,0:T(8,128)(2,1)S(1)}, u32[]{:S(2)}, u32[]{:S(2)}) %collective-permute-start.17) | collective-permute-done | bytes 393248 | tf_op jit(solution)/shard_map/ppermute | solution.py:91
  152.5 12.2 %expert_forward.2 = (bf16[1024,768]{1,0:T(8,128)(2,1)S(1)}, bf16[4,1024,384]{2,1,0:T(8,128)(2,1)}, bf16[4,1024,384]{2,1,0:T(8,128)(2,1)}) custom-call(bf16[2,1024,768]{2,1,0:T(8,128)(2,1)} %after.10.rows, bf16[4,768,384]{2,1,0:T(8,128)(2,1)} %all-gather.7.cloned.1.call-done.first, bf16[4,384,768]{2,1,0:T(8,128)(2,1)} %all-gather.9.cloned.1.call-done.second), custom_call_target="tpu_custom_call" | custom-call | flops 75497472 | bytes 221184 | tf_op jit(solution)/shard_map/expert_forward/pallas_call | solution.py:419
  177.7 19.2 %expert_back.2 = (bf16[1024,768]{1,0:T(8,128)(2,1)S(1)}, bf16[4,768,384]{2,1,0:T(8,128)(2,1)}, bf16[4,384,768]{2,1,0:T(8,128)(2,1)}) custom-call(bf16[2,1024,768]{2,1,0:T(8,128)(2,1)} %bitcast.235, bf16[2,1024,768]{2,1,0:T(8,128)(2,1)} %bitcast.238, bf16[4,768,384]{2,1,0:T(8,128)(2,1)} %all-gather.7.cloned.1.call-done.first, ...), custom_call_target="tpu_custom_call" | custom-call | flops 150994944 | bytes 319488 | tf_op jit(solution)/shard_map/expert_back/pallas_call | solution.py:465
  198.4 3.8 copy.208.refs_0_
  203.6 18.1 %all-gather.13.cloned.1.call-done = bf16[1536,768]{1,0:T(8,128)(2,1)} async-done(((bf16[384,768]{1,0:T(8,128)(2,1)}), bf16[1536,768]{1,0:T(8,128)(2,1)}) %all-gather.13.cloned.1.call-update) | async-done | bytes 2359312 | tf_op jit(solution)/shard_map/all_gather | solution.py:539
  221.8 12.2 %expert_forward.3 = (bf16[1024,768]{1,0:T(8,128)(2,1)S(1)}, bf16[4,1024,384]{2,1,0:T(8,128)(2,1)}, bf16[4,1024,384]{2,1,0:T(8,128)(2,1)}) custom-call(bf16[2,1024,768]{2,1,0:T(8,128)(2,1)} %after.12.rows, bf16[4,768,384]{2,1,0:T(8,128)(2,1)} %bitcast.243, bf16[4,384,768]{2,1,0:T(8,128)(2,1)} %bitcast.245), custom_call_target="tpu_custom_call" | custom-call | flops 75497472 | bytes 221184 | tf_op jit(solution)/shard_map/expert_forward/pallas_call | solution.py:419
  236.4 3.3 fusion.11.refs_1_
  239.7 18.8 %expert_back.3 = (bf16[1024,768]{1,0:T(8,128)(2,1)S(1)}, bf16[4,768,384]{2,1,0:T(8,128)(2,1)}, bf16[4,384,768]{2,1,0:T(8,128)(2,1)}) custom-call(bf16[2,1024,768]{2,1,0:T(8,128)(2,1)} %bitcast.237, bf16[2,1024,768]{2,1,0:T(8,128)(2,1)} %after.14.grads, bf16[4,768,384]{2,1,0:T(8,128)(2,1)} %bitcast.244, bf16[4,384,768]{2,1,0:T(8,128)(2,1)} %bitcast.246, ...), custom_call_target="tpu_custom_call" | custom-call | flops 150994944 | bytes 319488 | tf_op jit(solution)/shard_map/expert_back/pallas_call | solution.py:465
  265.9 15.8 %collective-permute-done.25 = bf16[2,256,768]{2,1,0:T(8,128)(2,1)S(1)} collective-permute-done((bf16[2,256,768]{2,1,0:T(8,128)(2,1)S(1)}, bf16[2,256,768]{2,1,0:T(8,128)(2,1)S(1)}, u32[]{:S(2)}, u32[]{:S(2)}) %collective-permute-start.25) | collective-permute-done | bytes 786464 | tf_op jit(solution)/shard_map/ppermute | solution.py:91
  287.1 6.3 %collective-permute-done.24 = bf16[1,256,768]{2,1,0:T(8,128)(2,1)S(1)} collective-permute-done((bf16[1,256,768]{2,1,0:T(8,128)(2,1)S(1)}, bf16[1,256,768]{2,1,0:T(8,128)(2,1)S(1)}, u32[]{:S(2)}, u32[]{:S(2)}) %collective-permute-start.24) | collective-permute-done | bytes 393248 | tf_op jit(solution)/shard_map/ppermute | solution.py:91
  294.7 4.6 convolution_convert_fusion.3
  303.5 13.5 %collective-permute-done.29 = bf16[2,256,768]{2,1,0:T(8,128)(2,1)S(1)} collective-permute-done((bf16[2,256,768]{2,1,0:T(8,128)(2,1)S(1)}, bf16[2,256,768]{2,1,0:T(8,128)(2,1)S(1)}, u32[]{:S(2)}, u32[]{:S(2)}) %collective-permute-start.29) | collective-permute-done | bytes 786464 | tf_op jit(solution)/shard_map/ppermute | solution.py:91
  320.1 3.8 fusion.118
  324.0 3.9 collective-permute-done.30
  332.7 6.9 %collective-permute-done.32 = bf16[1,256,768]{2,1,0:T(8,128)(2,1)} collective-permute-done((bf16[1,256,768]{2,1,0:T(8,128)(2,1)}, bf16[1,256,768]{2,1,0:T(8,128)(2,1)}, u32[]{:S(2)}, u32[]{:S(2)}) %collective-permute-start.32) | collective-permute-done | bytes 393248 | tf_op jit(solution)/shard_map/ppermute | solution.py:91
  352.0 8.9 %attend_back.2 = (bf16[512,384]{1,0:T(8,128)(2,1)S(1)}, bf16[512,384]{1,0:T(8,128)(2,1)S(1)}, bf16[512,384]{1,0:T(8,128)(2,1)S(1)}, f32[6,8,1024]{2,1,0:T(8,128)S(1)}) custom-call(bf16[512,2304]{1,0:T(8,128)(2,1)} %convolution_convert_fusion.query.key.value, bf16[512,2304]{1,0:T(8,128)(2,1)} %convolution_convert_fusion.query.key.value, ...), custom_call_target="tpu_custom_call" | custom-call | flops 50331648 | bytes 92160 | tf_op jit(solution)/shard_map/attend_back/pallas_call | solution.py:352
  369.9 7.0 %collective-permute-done.34 = bf16[8,24,896]{2,1,0:T(8,128)(2,1)S(1)} collective-permute-done((bf16[8,24,896]{2,1,0:T(8,128)(2,1)S(1)}, bf16[8,24,896]{2,1,0:T(8,128)(2,1)S(1)}, u32[]{:S(2)}, u32[]{:S(2)}) %collective-permute-start.34) | collective-permute-done | bytes 344096 | tf_op jit(solution)/shard_map/ppermute | solution.py:91
  377.7 9.0 %attend_back.3 = (bf16[512,384]{1,0:T(8,128)(2,1)S(1)}, bf16[512,384]{1,0:T(8,128)(2,1)S(1)}, bf16[512,384]{1,0:T(8,128)(2,1)S(1)}, f32[6,8,1024]{2,1,0:T(8,128)S(1)}) custom-call(bf16[512,2304]{1,0:T(8,128)(2,1)} %convolution_convert_fusion.query.key.value, bf16[512,2304]{1,0:T(8,128)(2,1)} %convolution_convert_fusion.query.key.value, ...), custom_call_target="tpu_custom_call" | custom-call | flops 50331648 | bytes 92160 | tf_op jit(solution)/shard_map/attend_back/pallas_call | solution.py:352
  390.1 5.0 %fusion.40 = (f32[768]{0:T(1024)S(1)}, f32[512]{0:T(512)}, f32[512,768]{1,0:T(8,128)}) fusion(bf16[512,768]{1,0:T(8,128)(2,1)S(1)} %copy-done.37, f32[512]{0:T(512)S(1)} %copy-done.86, f32[768]{0:T(1024)S(1)} %copy-done.84, f32[512,768]{1,0:T(8,128)} %fusion.16, bf16[512,1152]{1,0:T(8,128)(2,1)} %constant_dynamic-update-slice_fusion.3, ...), kind=kOutput, calls=%fused_computation.66 | convolution fusion | flops 914422528 | bytes 6891520 | tf_op jit(solution)/shard_map/dot_general | solution.py:58
  403.4 4.1 all-to-all-start
  412.8 3.8 collective-permute-done.41
  417.7 6.2 %collective-permute-done.43 = bf16[8,24,1152]{2,1,0:T(8,128)(2,1)S(1)} collective-permute-done((bf16[8,24,1152]{2,1,0:T(8,128)(2,1)S(1)}, bf16[8,24,1152]{2,1,0:T(8,128)(2,1)S(1)}, u32[]{:S(2)}, u32[]{:S(2)}) %collective-permute-start.43) | collective-permute-done | bytes 442400 | tf_op jit(solution)/shard_map/ppermute | solution.py:91
  427.1 3.6 all-to-all-start.1
  436.7 16.4 %collective-permute-done.39 = f32[9,128]{1,0:T(8,128)S(1)} collective-permute-done((f32[9,128]{1,0:T(8,128)S(1)}, f32[9,128]{1,0:T(8,128)S(1)}, u32[]{:S(2)}, u32[]{:S(2)}) %collective-permute-start.39) | collective-permute-done | bytes 4640 | tf_op jit(solution)/shard_map/ppermute | solution.py:91
  (481 shorter events, 169.4 us)
Async XLA Ops:
  7.3 145.2 %all-gather.7.cloned.1.call-start = ((), (), s32[]{:S(2)}) async-start(), calls=%async_computation.6 | async-start | bytes 2949120 | tf_op jit(solution)/shard_map/all_gather | solution.py:539
  9.8 142.7 %all-gather.9.cloned.1.call-start = ((), (), s32[]{:S(2)}) async-start(), calls=%async_computation.7 | async-start | bytes 2949120 | tf_op jit(solution)/shard_map/all_gather | solution.py:539
  10.2 13.4 %collective-permute-start = (bf16[24,3200]{1,0:T(8,128)(2,1)S(1)}, bf16[24,3200]{1,0:T(8,128)(2,1)S(1)}, u32[]{:S(2)}, u32[]{:S(2)}) collective-permute-start(bf16[24,3200]{1,0:T(8,128)(2,1)S(1)} %concatenate.174), channel_id=1, source_target_pairs={{0,24},{4,28},{8,0},{12,4},{16,8},{20,12},{24,16},{28,20},{1,25},{... | collective-permute-start | bytes 460808 | tf_op jit(solution)/shard_map/ppermute | solution.py:106
  15.3 22.5 %collective-permute-start.1 = (bf16[24,3200]{1,0:T(8,128)(2,1)S(1)}, bf16[24,3200]{1,0:T(8,128)(2,1)}, u32[]{:S(2)}, u32[]{:S(2)}) collective-permute-start(bf16[24,3200]{1,0:T(8,128)(2,1)S(1)} %concatenate.174), channel_id=1, source_target_pairs={{0,16},{4,20},{8,24},{12,28},{16,0},{20,4},{24,8},{28,12},{1,17},{... | collective-permute-start | bytes 460808 | tf_op jit(solution)/shard_map/ppermute | solution.py:106
  15.3 23.4 %collective-permute-start.2 = (bf16[24,3200]{1,0:T(8,128)(2,1)S(1)}, bf16[24,3200]{1,0:T(8,128)(2,1)}, u32[]{:S(2)}, u32[]{:S(2)}) collective-permute-start(bf16[24,3200]{1,0:T(8,128)(2,1)S(1)} %concatenate.174), channel_id=1, source_target_pairs={{0,8},{4,12},{8,16},{12,20},{16,24},{20,28},{24,0},{28,4},{1,9},{5... | collective-permute-start | bytes 460808 | tf_op jit(solution)/shard_map/ppermute | solution.py:106
  19.3 184.3 %all-gather.11.cloned.1.call-start = ((), (), s32[]{:S(2)}) async-start(), calls=%async_computation.12 | async-start | bytes 2949120 | tf_op jit(solution)/shard_map/all_gather | solution.py:539
  22.1 72.2 %collective-permute-start.10 = (s32[2,1,512]{2,1,0:T(1,128)}, s32[2,1,512]{2,1,0:T(1,128)}, u32[]{:S(2)}, u32[]{:S(2)}) collective-permute-start(s32[2,1,512]{2,1,0:T(1,128)} %pad_add_fusion.2), channel_id=1, source_target_pairs={{0,2},{1,3},{2,0},{3,1},{4,6},{5,7},{6,4},{7,5},{8,10},{9,11},{10,... | collective-permute-start | bytes 12296 | tf_op jit(solution)/shard_map/ppermute | solution.py:91
  92.1 129.6 %all-gather.13.cloned.1.call-start = ((), (), s32[]{:S(2)}) async-start(), calls=%async_computation.13 | async-start | bytes 2949120 | tf_op jit(solution)/shard_map/all_gather | solution.py:539
  102.8 18.9 %collective-permute-start.12 = (bf16[2,256,768]{2,1,0:T(8,128)(2,1)S(1)}, bf16[2,256,768]{2,1,0:T(8,128)(2,1)S(1)}, u32[]{:S(2)}, u32[]{:S(2)}) collective-permute-start(bf16[2,256,768]{2,1,0:T(8,128)(2,1)S(1)} %pad_maximum_fusion.7), channel_id=1, source_target_pairs={{0,2},{1,3},{2,0},{3,1},{4,6},{5,7},{6,4},{7,5},{8,10},{9,11},{10,... | collective-permute-start | bytes 2359304 | tf_op jit(solution)/shard_map/ppermute | solution.py:91
  104.5 18.6 %collective-permute-start.14 = (bf16[2,256,768]{2,1,0:T(8,128)(2,1)S(1)}, bf16[2,256,768]{2,1,0:T(8,128)(2,1)S(1)}, u32[]{:S(2)}, u32[]{:S(2)}) collective-permute-start(bf16[2,256,768]{2,1,0:T(8,128)(2,1)S(1)} %pad_maximum_fusion.8), channel_id=1, source_target_pairs={{0,4},{4,0},{8,12},{12,8},{16,20},{20,16},{24,28},{28,24},{1,5},{5... | collective-permute-start | bytes 2359304 | tf_op jit(solution)/shard_map/ppermute | solution.py:91
  126.5 20.5 %collective-permute-start.15 = (bf16[2,4,128,768]{3,2,0,1:T(8,128)(2,1)}, bf16[2,4,128,768]{3,2,0,1:T(8,128)(2,1)}, u32[]{:S(2)}, u32[]{:S(2)}) collective-permute-start(bf16[2,4,128,768]{3,2,0,1:T(8,128)(2,1)} %fusion.42), channel_id=1, source_target_pairs={{0,1},{1,0},{2,3},{3,2},{4,5},{5,4},{6,7},{7,6},{8,9},{9,8},{10,11... | collective-permute-start | bytes 4718600 | tf_op jit(solution)/shard_map/ppermute | solution.py:91
  129.2 12.9 %collective-permute-start.16 = (bf16[256,768]{1,0:T(8,128)(2,1)}, bf16[256,768]{1,0:T(8,128)(2,1)S(1)}, u32[]{:S(2)}, u32[]{:S(2)}) collective-permute-start(bf16[256,768]{1,0:T(8,128)(2,1)} %get-tuple-element.38), channel_id=1, source_target_pairs={{0,4},{4,0},{8,12},{12,8},{16,20},{20,16},{24,28},{28,24},{1,5},{5... | collective-permute-start | bytes 1179656 | tf_op jit(solution)/shard_map/ppermute | solution.py:91
  130.2 326.9 %reduce-scatter.9.cloned.1.call-start = ((), (), s32[]{:S(2)}) async-start(), calls=%async_computation.10 | async-start | bytes 2949120 | tf_op jit(solution)/shard_map/reduce_scatter | solution.py:629
  141.6 24.3 %collective-permute-start.19 = (bf16[2,256,768]{2,1,0:T(8,128)(2,1)}, bf16[2,256,768]{2,1,0:T(8,128)(2,1)S(1)}, u32[]{:S(2)}, u32[]{:S(2)}) collective-permute-start(bf16[2,256,768]{2,1,0:T(8,128)(2,1)} %pad_maximum_fusion.10), channel_id=1, source_target_pairs={{0,4},{4,0},{8,12},{12,8},{16,20},{20,16},{24,28},{28,24},{1,5},{5... | collective-permute-start | bytes 2359304 | tf_op jit(solution)/shard_map/ppermute | solution.py:91
  143.1 22.7 %collective-permute-start.18 = (bf16[2,256,768]{2,1,0:T(8,128)(2,1)}, bf16[2,256,768]{2,1,0:T(8,128)(2,1)}, u32[]{:S(2)}, u32[]{:S(2)}) collective-permute-start(bf16[2,256,768]{2,1,0:T(8,128)(2,1)} %pad_maximum_fusion.9), channel_id=1, source_target_pairs={{0,2},{1,3},{2,0},{3,1},{4,6},{5,7},{6,4},{7,5},{8,10},{9,11},{10,... | collective-permute-start | bytes 2359304 | tf_op jit(solution)/shard_map/ppermute | solution.py:91
  198.1 259.0 %reduce-scatter.11.cloned.1.call-start = ((), (), s32[]{:S(2)}) async-start(), calls=%async_computation.11 | async-start | bytes 2949120 | tf_op jit(solution)/shard_map/reduce_scatter | solution.py:629
  203.4 31.4 %collective-permute-start.21 = (bf16[4,128,768]{2,1,0:T(8,128)(2,1)}, bf16[4,128,768]{2,1,0:T(8,128)(2,1)S(1)}, u32[]{:S(2)}, u32[]{:S(2)}) collective-permute-start(bf16[4,128,768]{2,1,0:T(8,128)(2,1)} %bitcast.87), channel_id=1, source_target_pairs={{0,1},{1,0},{2,3},{3,2},{4,5},{5,4},{6,7},{7,6},{8,9},{9,8},{10,11... | collective-permute-start | bytes 2359304 | tf_op jit(solution)/shard_map/ppermute | solution.py:91
  258.5 201.5 %reduce-scatter.5.cloned.1.call-start = ((), (), s32[]{:S(2)}) async-start(), calls=%async_computation.8 | async-start | bytes 2949120 | tf_op jit(solution)/shard_map/reduce_scatter | solution.py:629
  259.2 200.7 %reduce-scatter.7.cloned.1.call-start = ((), (), s32[]{:S(2)}) async-start(), calls=%async_computation.9 | async-start | bytes 2949120 | tf_op jit(solution)/shard_map/reduce_scatter | solution.py:629
  262.1 19.7 %collective-permute-start.25 = (bf16[2,256,768]{2,1,0:T(8,128)(2,1)S(1)}, bf16[2,256,768]{2,1,0:T(8,128)(2,1)S(1)}, u32[]{:S(2)}, u32[]{:S(2)}) collective-permute-start(bf16[2,256,768]{2,1,0:T(8,128)(2,1)S(1)} %pad_maximum_fusion.11), channel_id=1, source_target_pairs={{0,4},{4,0},{8,12},{12,8},{16,20},{20,16},{24,28},{28,24},{1,5},{5... | collective-permute-start | bytes 2359304 | tf_op jit(solution)/shard_map/ppermute | solution.py:91
  263.6 19.3 %collective-permute-start.23 = (bf16[2,256,768]{2,1,0:T(8,128)(2,1)S(1)}, bf16[2,256,768]{2,1,0:T(8,128)(2,1)S(1)}, u32[]{:S(2)}, u32[]{:S(2)}) collective-permute-start(bf16[2,256,768]{2,1,0:T(8,128)(2,1)S(1)} %stack.333), channel_id=1, source_target_pairs={{0,2},{1,3},{2,0},{3,1},{4,6},{5,7},{6,4},{7,5},{8,10},{9,11},{10,... | collective-permute-start | bytes 2359304 | tf_op jit(solution)/shard_map/ppermute | solution.py:91
  265.2 20.0 %collective-permute-start.27 = (bf16[4,128,768]{2,1,0:T(8,128)(2,1)S(1)}, bf16[4,128,768]{2,1,0:T(8,128)(2,1)S(1)}, u32[]{:S(2)}, u32[]{:S(2)}) collective-permute-start(bf16[4,128,768]{2,1,0:T(8,128)(2,1)S(1)} %bitcast.284), channel_id=1, source_target_pairs={{0,1},{1,0},{2,3},{3,2},{4,5},{5,4},{6,7},{7,6},{8,9},{9,8},{10,11... | collective-permute-start | bytes 2359304 | tf_op jit(solution)/shard_map/ppermute | solution.py:91
  265.4 19.8 %collective-permute-start.28 = (bf16[4,128,768]{2,1,0:T(8,128)(2,1)S(1)}, bf16[4,128,768]{2,1,0:T(8,128)(2,1)S(1)}, u32[]{:S(2)}, u32[]{:S(2)}) collective-permute-start(bf16[4,128,768]{2,1,0:T(8,128)(2,1)S(1)} %bitcast.285), channel_id=1, source_target_pairs={{0,1},{1,0},{2,3},{3,2},{4,5},{5,4},{6,7},{7,6},{8,9},{9,8},{10,11... | collective-permute-start | bytes 2359304 | tf_op jit(solution)/shard_map/ppermute | solution.py:91
  299.4 17.6 %collective-permute-start.29 = (bf16[2,256,768]{2,1,0:T(8,128)(2,1)S(1)}, bf16[2,256,768]{2,1,0:T(8,128)(2,1)S(1)}, u32[]{:S(2)}, u32[]{:S(2)}) collective-permute-start(bf16[2,256,768]{2,1,0:T(8,128)(2,1)S(1)} %stack.334), channel_id=1, source_target_pairs={{0,2},{1,3},{2,0},{3,1},{4,6},{5,7},{6,4},{7,5},{8,10},{9,11},{10,... | collective-permute-start | bytes 2359304 | tf_op jit(solution)/shard_map/ppermute | solution.py:91
  302.0 22.0 %collective-permute-start.31 = (bf16[2,256,768]{2,1,0:T(8,128)(2,1)}, bf16[2,256,768]{2,1,0:T(8,128)(2,1)}, u32[]{:S(2)}, u32[]{:S(2)}) collective-permute-start(bf16[2,256,768]{2,1,0:T(8,128)(2,1)} %pad_maximum_fusion.12), channel_id=1, source_target_pairs={{0,4},{4,0},{8,12},{12,8},{16,20},{20,16},{24,28},{28,24},{1,5},{5... | collective-permute-start | bytes 2359304 | tf_op jit(solution)/shard_map/ppermute | solution.py:91
  366.1 31.4 %collective-permute-start.40 = (bf16[8,2,24,1152]{3,2,1,0:T(8,128)(2,1)}, bf16[8,2,24,1152]{3,2,1,0:T(8,128)(2,1)}, u32[]{:S(2)}, u32[]{:S(2)}) collective-permute-start(bf16[8,2,24,1152]{3,2,1,0:T(8,128)(2,1)} %dynamic-slice_bitcast_fusion), channel_id=1, source_target_pairs={{0,1},{1,0},{2,3},{3,2},{4,5},{5,4},{6,7},{7,6},{8,9},{9,8},{10,11... | collective-permute-start | bytes 2654216 | tf_op jit(solution)/shard_map/ppermute | solution.py:91
  403.2 13.4 %collective-permute-start.41 = (bf16[8,24,1152]{2,1,0:T(8,128)(2,1)}, bf16[8,24,1152]{2,1,0:T(8,128)(2,1)}, u32[]{:S(2)}, u32[]{:S(2)}) collective-permute-start(bf16[8,24,1152]{2,1,0:T(8,128)(2,1)} %dynamic-slice_bitcast_fusion.3), channel_id=1, source_target_pairs={{0,2},{1,3},{2,0},{3,1},{4,6},{5,7},{6,4},{7,5},{8,10},{9,11},{10,... | collective-permute-start | bytes 1327112 | tf_op jit(solution)/shard_map/ppermute | solution.py:91
  403.4 23.7 %all-to-all-start = ((bf16[8,24,896]{2,1,0:T(8,128)(2,1)}), bf16[8,24,896]{2,1,0:T(8,128)(2,1)}, u32[]{:S(2)}, u32[]{:S(2)}) async-start(bf16[8,24,896]{2,1,0:T(8,128)(2,1)} %fusion.67.refs_2_), calls=%async_computation | async-start | bytes 688128 | tf_op jit(solution)/shard_map/all_to_all | solution.py:214
  407.5 23.2 %collective-permute-start.38 = (f32[9,128]{1,0:T(8,128)S(1)}, f32[9,128]{1,0:T(8,128)S(1)}, u32[]{:S(2)}, u32[]{:S(2)}) collective-permute-start(f32[9,128]{1,0:T(8,128)S(1)} %add.341), channel_id=1, source_target_pairs={{0,8},{4,12},{8,0},{12,4},{16,24},{20,28},{24,16},{28,20},{1,9},{5... | collective-permute-start | bytes 13832 | tf_op jit(solution)/shard_map/ppermute | solution.py:91
  410.9 13.0 %collective-permute-start.43 = (bf16[8,24,1152]{2,1,0:T(8,128)(2,1)S(1)}, bf16[8,24,1152]{2,1,0:T(8,128)(2,1)S(1)}, u32[]{:S(2)}, u32[]{:S(2)}) collective-permute-start(bf16[8,24,1152]{2,1,0:T(8,128)(2,1)S(1)} %dynamic-slice_bitcast_fusion.2), channel_id=1, source_target_pairs={{0,2},{1,3},{2,0},{3,1},{4,6},{5,7},{6,4},{7,5},{8,10},{9,11},{10,... | collective-permute-start | bytes 1327112 | tf_op jit(solution)/shard_map/ppermute | solution.py:91
  427.1 35.7 %all-to-all-start.1 = ((bf16[8,24,2304]{2,1,0:T(8,128)(2,1)}), bf16[8,24,2304]{2,1,0:T(8,128)(2,1)S(1)}, u32[]{:S(2)}, u32[]{:S(2)}) async-start(bf16[8,24,2304]{2,1,0:T(8,128)(2,1)} %pad_maximum_fusion.6), calls=%async_computation.1 | async-start | bytes 1769472 | tf_op jit(solution)/shard_map/all_to_all | solution.py:214
  430.7 22.5 %collective-permute-start.39 = (f32[9,128]{1,0:T(8,128)S(1)}, f32[9,128]{1,0:T(8,128)S(1)}, u32[]{:S(2)}, u32[]{:S(2)}) collective-permute-start(f32[9,128]{1,0:T(8,128)S(1)} %add.342), channel_id=1, source_target_pairs={{0,16},{4,20},{8,24},{12,28},{16,0},{20,4},{24,8},{28,12},{1,17},{... | collective-permute-start | bytes 13832 | tf_op jit(solution)/shard_map/ppermute | solution.py:91
  (121 other events, 787.9 us)
Sparse Core Ops, SparseCore 0:
  9.9 57.0 all-gather.6
  68.6 51.4 all-gather.8
  121.7 49.2 all-gather.10
  172.5 49.2 all-gather.12
  223.9 46.8 reduce-scatter.8
  273.0 47.5 reduce-scatter.10
  323.4 47.4 reduce-scatter.4
  373.3 53.1 reduce-scatter.6

commit v3 on v2

--- a/solution.py
+++ b/solution.py
@@ -144,7 +144,7 @@
     brought = []
     for number in range(len(dims)):
         steps = (dims[number], dims[len(dims) - 1 - number])
-        arrived = [gather_step(part, dim) for part, dim in zip(held, steps)]
+        arrived = after([gather_step(part, dim) for part, dim in zip(held, steps)], ())
         brought.append(arrived)
         held = [gather_join(*of) for of in zip(held, steps, arrived)]
     upper, lower = held
@@ -152,30 +152,28 @@
     return (blocks, brought)
 
 
-def scatter_step(held, dim):
-    stay = [key for key in held if dim not in key]
-    leave = [tuple(sorted(key + (dim,))) for key in stay]
-    sent = jnp.stack([held[key].astype(LOW) for key in leave])
-    arrived = swap(sent, dim)
-    return {
-        key: held[key].astype(FULL) + arrived[number].astype(FULL)
-        for number, key in enumerate(stay)
-    }
-
-
 def scatter_halves(blocks, keys, dims):
     half = blocks.shape[1] // 2
-    upper = {key: blocks[number, :half] for number, key in enumerate(keys)}
-    lower = {key: blocks[number, half:] for number, key in enumerate(keys)}
-    between = ()
+    parts = [
+        {key: blocks[number, :half] for number, key in enumerate(keys)},
+        {key: blocks[number, half:] for number, key in enumerate(keys)},
+    ]
     for number in range(len(dims)):
-        upper = scatter_step(upper, dims[len(dims) - 1 - number])
-        lower = scatter_step(lower, dims[number])
-        if number == 0 and len(dims) > 1:
-            upper = {key: value.astype(LOW) for key, value in upper.items()}
-            lower = {key: value.astype(LOW) for key, value in lower.items()}
-            between = list(upper.values()) + list(lower.values())
-    return (jnp.concatenate((upper[()], lower[()])), between)
+        steps = (dims[len(dims) - 1 - number], dims[number])
+        stay = [[key for key in held if dim not in key] for held, dim in zip(parts, steps)]
+        sent = [
+            jnp.stack([held[tuple(sorted(key + (dim,)))].astype(LOW) for key in some])
+            for held, dim, some in zip(parts, steps, stay)
+        ]
+        arrived = after([swap(value, dim) for value, dim in zip(sent, steps)], ())
+        parts = [
+            {
+                key: held[key].astype(FULL) + value[place].astype(FULL)
+                for place, key in enumerate(some)
+            }
+            for held, value, some in zip(parts, arrived, stay)
+        ]
+    return jnp.concatenate((parts[0][()], parts[1][()]))
 
 
 def dense_gather(value, places, place, dims, core):
@@ -198,30 +196,45 @@
     return (jnp.concatenate((first, second), axis=1), near)
 
 
-def dense_scatter(value, peer_dims, rows):
-    bits = len(peer_dims)
-    part = value.reshape((-1,) + (2,) * bits + (rows, value.shape[1]))
-    for number, dim in enumerate(peer_dims):
-        spot = bits - number
+def halve(parts, all_names, dims, beside=()):
+    kept, sent, left = [], [], []
+    for part, names, dim in zip(parts, all_names, dims):
+        spot = names.index(dim)
         own = bit_of(dim).astype(jnp.int32)
-        keep = lax.dynamic_index_in_dim(part, own, spot, keepdims=False)
+        kept.append(lax.dynamic_index_in_dim(part, own, spot, keepdims=False))
         send = lax.dynamic_index_in_dim(part, 1 - own, spot, keepdims=False)
-        part = (keep.astype(FULL) + swap(send, dim).astype(FULL)).astype(LOW)
-    return part
-
-
-def dense_finish(part):
-    arrived = lax.all_to_all(part, "fsdp", split_axis=0, concat_axis=0, tiled=True)
-    return jnp.sum(arrived.astype(FULL), axis=0)
-
-
-def sum_everywhere(value):
-    for axis in ("dp", "fsdp"):
-        mask = 1
-        while mask < lax.axis_size(axis):
-            value = value + swap(value, (axis, mask))
-            mask *= 2
-    return value
+        sent.append(swap(send, dim))
+        left.append(names[:spot] + names[spot + 1 :])
+    arrived = after(sent + list(beside), ())
+    sums = [(a.astype(FULL) + b.astype(FULL)).astype(LOW) for a, b in zip(kept, arrived)]
+    return (sums, left, arrived[len(sent) :])
+
+
+def dense_scatter(parts, names, orders, places, place, small, small_dims):
+    all_names = [names] * len(parts)
+    for dims, dim in zip(zip(*orders), small_dims):
+        parts, all_names, (other,) = halve(parts, all_names, dims, (swap(small, dim),))
+        small = small + other
+    moved = []
+    for part in parts:
+        for by in range(1, places):
+            send = lax.dynamic_index_in_dim(part, lax.rem(place + by, places), 0, keepdims=False)
+            moved.append(ring_shift(send, places, places - by))
+    *moved, other = after(moved + [swap(small, small_dims[-1])], ())
+    small = small + other
+    small = reduce(
+        lambda total, by: total + ring_shift(small, places, by), range(1, places), small
+    )
+    count = places - 1
+    sums = [
+        reduce(
+            lambda total, value: total + value.astype(FULL),
+            moved[number * count : (number + 1) * count],
+            lax.dynamic_index_in_dim(part, place, 0, keepdims=False).astype(FULL),
+        )
+        for number, part in enumerate(parts)
+    ]
+    return (sums, small)
 
 
 def diagonal_hot(slots, bucket_count):
@@ -483,6 +496,38 @@
     )(rows, grads, first, second, hidden, slope)
 
 
+def place_kernel(groups, hot, *refs):
+    *parts, out = refs
+    size = len(parts) // groups
+    width = parts[0].shape[1]
+    for group in range(groups):
+        some = [part[...] for part in parts[group * size : (group + 1) * size]]
+        values = jnp.concatenate(some, axis=0)
+        out[0, :, group * width : (group + 1) * width] = mm(hot[0], values, ((1,), (0,)), LOW)
+
+
+def place_rows(hot, groups, capacity):
+    blocks, count, slots = hot.shape
+    parts = sum(groups, [])
+    width = parts[0].shape[1]
+    wide = width * len(groups)
+    return pl.pallas_call(
+        partial(place_kernel, len(groups)),
+        grid=(blocks,),
+        in_specs=[pl.BlockSpec((1, count, slots), lambda b: (b, 0, 0))]
+        + [pl.BlockSpec((capacity, width), lambda b: (b, 0))] * len(parts),
+        out_specs=pl.BlockSpec((1, count, wide), lambda b: (b, 0, 0)),
+        out_shape=jax.ShapeDtypeStruct((blocks, count, wide), LOW),
+        compiler_params=pltpu.CompilerParams(vmem_limit_bytes=VMEM_BYTES),
+        cost_estimate=small_cost(
+            flops=2 * blocks * count * slots * wide,
+            bytes_accessed=4 * blocks * count * wide,
+            transcendentals=0,
+        ),
+        name="place_rows",
+    )(hot, *parts)
+
+
 def body(
     tokens,
     cotangent,
@@ -580,17 +625,15 @@
         both = jnp.stack((pick(hot_own, blocks), other), axis=1)
         return both.reshape(local_experts, -1, width)
 
-    hot_all = jnp.concatenate((hot_own, hot_other), axis=1).reshape(
-        len(keys), 2 * local_slots, tok_count
-    )
-
-    def from_rows(values, ready=()):
-        shaped = [value.reshape(2, len(keys), capacity, width) for value in values]
-        parts = [part[0] for part in shaped] + [swap(part[1], core) for part in shaped]
-        joined = jnp.concatenate(parts, axis=1)
-        if ready:
-            (joined,) = after((joined,), ready)
-        return jnp.einsum("bst,bsd->btd", hot_all, joined, preferred_element_type=FULL).astype(LOW)
+    token_ids = jnp.concatenate((peer * local_slots + slot_ids, (peer ^ 1) * local_slots + slot_ids))
+    hot_back = (slots_near[:, :, None] == token_ids.reshape(-1)[None, None, :]).astype(LOW)
+
+    def from_rows(*groups):
+        near_rows = len(keys) * capacity
+        parts = [
+            list(values) + [swap(value[near_rows:], core) for value in values] for values in groups
+        ]
+        return place_rows(hot_back, parts, capacity)
 
     blocks, brought = gather_halves(normed_two_low, dims)
     rows = to_rows(blocks)
@@ -617,26 +660,20 @@
         if expert > 0:
             (tied,) = after((rows,), (backs[-1][0],))
             forwards.append(expert_forward(expert, tied, *weights[expert]))
-        tied = grads
-        if expert == local_experts - 1:
-            y_raw = from_rows([forward[0] for forward in forwards])
-            token_y, y_between = scatter_halves(y_raw, keys, dims)
-            (tied,) = after((grads,), (y_raw,))
-        backs.append(expert_back(expert, rows, tied, *weights[expert], *forwards[expert][1:]))
-    in_grad, out_expert_grad = (
-        jnp.stack(
-            [
-                lax.psum_scatter(
-                    back[which], "fsdp", scatter_dimension=0, axis_index_groups=groups, tiled=False
-                ).astype(FULL)
-                for back in backs
-            ]
-        )
-        for which in (1, 2)
-    )
-    grad_rows, _ = scatter_halves(
-        from_rows([back[0] for back in backs], y_between), keys, dims
-    )
+        backs.append(expert_back(expert, rows, grads, *weights[expert], *forwards[expert][1:]))
+    summed = [
+        [
+            lax.psum_scatter(
+                value, "fsdp", scatter_dimension=0, axis_index_groups=groups, tiled=False
+            )
+            for value in back[1:]
+        ]
+        for back in backs
+    ]
+    returned = scatter_halves(
+        from_rows([forward[0] for forward in forwards], [back[0] for back in backs]), keys, dims
+    )
+    token_y, grad_rows = returned[:, :width], returned[:, width:]
 
     mixed = (hidden_one + gate_value[:, None] * token_y).astype(LOW)
     grad_gate = jnp.sum(upstream * token_y, axis=1)
@@ -654,7 +691,13 @@
     grad_attn_low = grad_hidden_one.astype(LOW)
     out_local = jnp.einsum("td,te->de", attended, grad_attn_low, preferred_element_type=FULL)
     grad_attended = mm(grad_attn_low, out_full, ((1,), (1,)), LOW)
-    peer_dims = [core] + dims[1:]
+    names = ["z", dims[0]] + sorted(dims[1:], reverse=True) + [core]
+
+    def split_rows(panel):
+        shape = (places,) + (2,) * (len(names) - 1) + (shard_rows, panel.shape[1])
+        parts, left, _ = halve([panel.reshape(shape)], [names], [core])
+        return (parts[0], left[0])
+
     spare_out = -(experts_all + 2) % 128
     out_panel = jnp.concatenate(
         (
@@ -665,42 +708,34 @@
         ),
         axis=1,
     )
-    (grad_attended,) = after((grad_attended,), (out_panel,))
-    out_part = dense_scatter(out_panel, peer_dims, shard_rows)
-    pairs = HEADS // 2
-    halves = ((0, pairs // 2), (pairs // 2, pairs - pairs // 2))
-    grad_normed_one = 0.0
-    diagonals, sums = [], []
-    for number, (begin, count) in enumerate(halves):
-        if number > 0:
-            (grad_attended,) = after((grad_attended,), (panel, out_part))
-        *grad_parts, lined = attend_back(projected, grad_attended, probs, begin, count)
-        diagonals.append(lined)
-        piece = jnp.concatenate(grad_parts, axis=1)
-        lanes = count * 2 * HEAD_DIM
-        weight = jnp.concatenate(
-            [
-                qkv_full[:, width * part + begin * 2 * HEAD_DIM :][:, :lanes]
-                for part in range(3)
-            ],
-            axis=1,
-        )
-        grad_normed_one = grad_normed_one + mm(piece, weight, ((1,), (1,)))
-        qkv_local = jnp.einsum("td,te->de", normed_low, piece, preferred_element_type=FULL)
-        panel = qkv_local.astype(LOW)
-        sums.append(dense_scatter(panel, peer_dims, shard_rows))
-    out_sum = dense_finish(out_part)
-    last_sum = dense_finish(jnp.concatenate(sums, axis=-1))
-    starts = [0] + [3 * count * 2 * HEAD_DIM for _, count in halves][:-1]
-    sums = [last_sum[:, start:] for start in starts]
+    out_half, half_names = split_rows(out_panel)
+    early = [value for back in summed[:-1] for value in back]
+    (grad_attended,) = after((grad_attended,), early)
+    *grad_parts, diagonals = attend_back(projected, grad_attended, probs, 0, HEADS // 2)
+    grad_projected = jnp.concatenate(grad_parts, axis=1)
+    qkv_local = mm(normed_low, grad_projected, ((0,), (0,)), LOW)
+    qkv_half, _ = split_rows(qkv_local)
+    half = 3 * width // 2
+    grad_normed_one = mm(grad_projected, qkv_full, ((1,), (1,)))
     grad_from_one, gain_grad_one = norm_back(inputs, inverse_one, gains_float[0], grad_normed_one)
     tokens_grad = grad_hidden_one + grad_from_one
-    bias_local = jnp.einsum(
-        "hrj,rjb->bh", jnp.concatenate(diagonals), bucket_hot, precision=HIGH
-    )
+    bias_local = jnp.einsum("hrj,rjb->bh", diagonals, bucket_hot, precision=HIGH)
     gain_rows = width // 128
     small = jnp.concatenate((bias_local.reshape(-1, 128), gain_grad_one.reshape(-1, 128)))
-    small = sum_everywhere(small)
+    (first_sum, second_sum, out_sum), small = dense_scatter(
+        [qkv_half[..., :half], qkv_half[..., half:], out_half],
+        half_names,
+        [dims, dims[::-1], dims[::-1]],
+        places,
+        place,
+        small,
+        [core] + dims,
+    )
+    summed[-1] = after(summed[-1], (first_sum, second_sum))
+    in_grad, out_expert_grad = (
+        jnp.stack([back[which].astype(FULL) for back in summed]) for which in (0, 1)
+    )
+    qkv_grad = jnp.concatenate((first_sum, second_sum), axis=1)
     bias_grad = small[:-gain_rows].reshape(bias_local.shape)
     device = lax.axis_index("fsdp") * peer_count + peer
     gain_one = lax.dynamic_slice_in_dim(
@@ -709,14 +744,6 @@
     gains_grad = jnp.stack((gain_one, out_sum[:, width + experts_all]))
     router_grad = out_sum[:, width : width + experts_all]
     out_grad = out_sum[:, :width]
-    qkv_grad = jnp.concatenate(
-        [
-            sums[number][:, part * count * 2 * HEAD_DIM :][:, : count * 2 * HEAD_DIM]
-            for part in range(3)
-            for number, (_, count) in enumerate(halves)
-        ],
-        axis=1,
-    )
     return (
         mixed,
         tokens_grad,

time: 480 us -> 474 us (0.988)
  waiting for transfers between devices: 170 us -> 146 us
  starting transfers between devices: 51.9 us -> 71.8 us
  matrix products: 39 us -> 24.4 us
  Pallas kernels: 95.6 us -> 103 us
    ppermute x3 -> x15, starting transfers between devices: 6.08 us -> 27.9 us  [ring_shift(): lax.ppermute(value, 'fsdp', [(i, (i - 2 * by) % count) for i in range(cou...]
    ppermute x41 -> x37, waiting for transfers between devices: 135 us -> 115 us  [swap(): return lax.ppermute(value, axis, [(i, i ^ mask) for i in range(count)])]
    all_gather x4, waiting for transfers between devices: 18.1 us -> 5.99 us  [body(): lax.all_gather(v, 'fsdp', axis=0, axis_index_groups=groups)]
    dot_general x5 -> x1, matrix products: 11.3 us -> 0.77 us  [body(): jnp.einsum('hrj,rjb->bh', diagonals, bucket_hot, precision=HIGH)]
    ppermute x3 -> x15, waiting for transfers between devices: 14.1 us -> 23.9 us  [ring_shift(): lax.ppermute(value, 'fsdp', [(i, (i - 2 * by) % count) for i in range(cou...]
    convert_element_type x8 -> x10, other arithmetic: 6.22 us -> 15.3 us  [the longest x8 10.4 us: halve(): (a.astype(FULL) + b.astype(FULL)).astype(LOW)]
    reduce_scatter x4, starting transfers between devices: 0.55 us -> 9.41 us  [body(): lax.psum_scatter(value, 'fsdp', scatter_dimension=0, axis_index_groups=gr...]
    pallas_call x0 -> x1, Pallas kernels: none -> 8.11 us  [place_rows(): pl.pallas_call(partial(place_kernel, len(groups)), grid=(blocks,), in_spe...]
  transfers between devices with their start and end apart: 54 -> 60, of which waited for: 26 -> 27; matrix products, arithmetic and copies ran while one was open for 26% -> 23% of each run, Pallas kernels for 20% -> 22%
where the time goes in v3:
time: 474 us; the launch traced here: 465 us
  waiting for transfers between devices  146 us (31%)
  Pallas kernels  103 us (22%)
  starting transfers between devices  71.8 us (15%)
  local copies, waits for them, and re-layouts  56.5 us (12%)
  other arithmetic  47.5 us (10%)
  matrix products  24.4 us (5%)
  between operations  16.2 us (3%)
    ppermute x37, waiting for transfers between devices, swap(): return lax.ppermute(value, axis, [(i, i ^ mask) for i in range(count)])  115 us
    pallas_call x2, Pallas kernels, expert_back(): pl.pallas_call(expert_back_kernel, grid=(chunks,), in_specs=[rows_in, row...  38 us
    ppermute x37, starting transfers between devices, swap(): return lax.ppermute(value, axis, [(i, i ^ mask) for i in range(count)])  34.1 us
    unnamed x269, local copies, waits for them, and re-layouts  28.6 us
    ppermute x15, starting transfers between devices, ring_shift(): lax.ppermute(value, 'fsdp', [(i, (i - 2 * by) % count) for i in range(cou...  27.9 us
    pallas_call x2, Pallas kernels, expert_forward(): pl.pallas_call(expert_forward_kernel, grid=(chunks,), in_specs=[rows_in,...  24.5 us
    ppermute x15, waiting for transfers between devices, ring_shift(): lax.ppermute(value, 'fsdp', [(i, (i - 2 * by) % count) for i in range(cou...  23.9 us
    pallas_call x1, Pallas kernels, attend_back(): pl.pallas_call(attend_back_kernel, grid=(count,), in_specs=[column_from(b...  16.5 us
  transfers between devices with their start and end apart: 60, of which 27 were waited for; matrix products, arithmetic and copies ran while one was open for 23% of the time, Pallas kernels for 22%

profile of v3, /device:TPU:0, one launch (start us, length us, event | category | flops | bytes accessed | tf_op | source)
XLA Modules:
  0.0 464.7 jit_solution(4675639344344599272)
XLA Ops:
  10.2 5.1 %collective-permute-start = (bf16[24,3200]{1,0:T(8,128)(2,1)S(1)}, bf16[24,3200]{1,0:T(8,128)(2,1)S(1)}, u32[]{:S(2)}, u32[]{:S(2)}) collective-permute-start(bf16[24,3200]{1,0:T(8,128)(2,1)S(1)} %concatenate.147), channel_id=1, source_target_pairs={{0,24},{4,28},{8,0},{12,4},{16,8},{20,12},{24,16},{28,20},{1,25},{... | collective-permute-start | bytes 460808 | tf_op jit(solution)/shard_map/ppermute | solution.py:106
  23.6 14.2 %collective-permute-done.1 = bf16[24,3200]{1,0:T(8,128)(2,1)} collective-permute-done((bf16[24,3200]{1,0:T(8,128)(2,1)S(1)}, bf16[24,3200]{1,0:T(8,128)(2,1)}, u32[]{:S(2)}, u32[]{:S(2)}) %collective-permute-start.1) | collective-permute-done | bytes 153632 | tf_op jit(solution)/shard_map/ppermute | solution.py:106
  44.9 5.0 %collective-permute-done.6 = bf16[4,24,1536]{2,1,0:T(8,128)(2,1)S(1)} collective-permute-done((bf16[4,24,1536]{2,1,0:T(8,128)(2,1)S(1)}, bf16[4,24,1536]{2,1,0:T(8,128)(2,1)S(1)}, u32[]{:S(2)}, u32[]{:S(2)}) %collective-permute-start.6) | collective-permute-done | bytes 294944 | tf_op jit(solution)/shard_map/ppermute | solution.py:91
  54.6 6.7 %collective-permute-done.7 = bf16[2,4,24,1536]{3,2,1,0:T(8,128)(2,1)S(1)} collective-permute-done((bf16[2,4,24,1536]{3,2,1,0:T(8,128)(2,1)S(1)}, bf16[2,4,24,1536]{3,2,1,0:T(8,128)(2,1)S(1)}, u32[]{:S(2)}, u32[]{:S(2)}) %collective-permute-start.7) | collective-permute-done | bytes 589856 | tf_op jit(solution)/shard_map/ppermute | solution.py:91
  61.6 2.8 collective-permute-done.4
  68.9 3.5 convolution_convert_fusion.1.query.key.value
  72.5 15.4 %attend_forward.1 = (bf16[512,768]{1,0:T(8,128)(2,1)S(1)}, bf16[12,512,512]{2,1,0:T(8,128)(2,1)}) custom-call(bf16[512,2304]{1,0:T(8,128)(2,1)} %convolution_convert_fusion.1.query.key.value, bf16[512,2304]{1,0:T(8,128)(2,1)} %convolution_convert_fusion.1.query.key.value, bf16[512,2304]{1,0:T(8,128)(2,1)} %convolution_convert_fusion.1.query.key.value, ...), custom_call_target="tpu_custom_call" | custom-call | flops 50331648 | bytes 147456 | tf_op jit(solution)/shard_map/attend_forward/pallas_call | solution.py:284
  94.5 6.9 %collective-permute-done.11.refs_0_ = bf16[256,768]{1,0:T(8,128)(2,1)S(1)} collective-permute-done((bf16[256,768]{1,0:T(8,128)(2,1)}, bf16[256,768]{1,0:T(8,128)(2,1)S(1)}, u32[]{:S(2)}, u32[]{:S(2)}) %collective-permute-start.11) | collective-permute-done | bytes 393248 | tf_op jit(solution)/shard_map/ppermute | solution.py:91
  111.7 11.3 %collective-permute-done.14.refs_1_ = bf16[2,256,768]{2,1,0:T(8,128)(2,1)S(1)} collective-permute-done((bf16[2,256,768]{2,1,0:T(8,128)(2,1)S(1)}, bf16[2,256,768]{2,1,0:T(8,128)(2,1)S(1)}, u32[]{:S(2)}, u32[]{:S(2)}) %collective-permute-start.14) | collective-permute-done | bytes 786464 | tf_op jit(solution)/shard_map/ppermute | solution.py:91
  134.8 8.3 %collective-permute-done.17.refs_2_ = bf16[256,768]{1,0:T(8,128)(2,1)S(1)} collective-permute-done((bf16[256,768]{1,0:T(8,128)(2,1)}, bf16[256,768]{1,0:T(8,128)(2,1)S(1)}, u32[]{:S(2)}, u32[]{:S(2)}) %collective-permute-start.17) | collective-permute-done | bytes 393248 | tf_op jit(solution)/shard_map/ppermute | solution.py:91
  156.9 12.3 %expert_forward.2 = (bf16[1024,768]{1,0:T(8,128)(2,1)S(1)}, bf16[4,1024,384]{2,1,0:T(8,128)(2,1)}, bf16[4,1024,384]{2,1,0:T(8,128)(2,1)}) custom-call(bf16[2,1024,768]{2,1,0:T(8,128)(2,1)} %after.19.rows, bf16[4,768,384]{2,1,0:T(8,128)(2,1)} %all-gather.7.cloned.1.call-done.first, bf16[4,384,768]{2,1,0:T(8,128)(2,1)} %all-gather.9.cloned.1.call-done.second), custom_call_target="tpu_custom_call" | custom-call | flops 75497472 | bytes 221184 | tf_op jit(solution)/shard_map/expert_forward/pallas_call | solution.py:432
  182.2 18.8 %expert_back.2 = (bf16[1024,768]{1,0:T(8,128)(2,1)S(1)}, bf16[4,768,384]{2,1,0:T(8,128)(2,1)}, bf16[4,384,768]{2,1,0:T(8,128)(2,1)}) custom-call(bf16[2,1024,768]{2,1,0:T(8,128)(2,1)} %bitcast.250, bf16[2,1024,768]{2,1,0:T(8,128)(2,1)} %bitcast.253, bf16[4,768,384]{2,1,0:T(8,128)(2,1)} %all-gather.7.cloned.1.call-done.first, ...), custom_call_target="tpu_custom_call" | custom-call | flops 150994944 | bytes 319488 | tf_op jit(solution)/shard_map/expert_back/pallas_call | solution.py:478
  201.7 9.3 %reduce-scatter.9.cloned.1.call-start = ((), (), s32[]{:S(2)}) async-start(), calls=%async_computation.8 | async-start | bytes 2949120 | tf_op jit(solution)/shard_map/reduce_scatter | solution.py:666
  210.9 3.7 copy.211.refs_0_
  215.8 6.0 %all-gather.13.cloned.1.call-done = bf16[1536,768]{1,0:T(8,128)(2,1)} async-done(((bf16[384,768]{1,0:T(8,128)(2,1)}), bf16[1536,768]{1,0:T(8,128)(2,1)}) %all-gather.13.cloned.1.call-update) | async-done | bytes 2359312 | tf_op jit(solution)/shard_map/all_gather | solution.py:584
  221.8 12.2 %expert_forward.3 = (bf16[1024,768]{1,0:T(8,128)(2,1)S(1)}, bf16[4,1024,384]{2,1,0:T(8,128)(2,1)}, bf16[4,1024,384]{2,1,0:T(8,128)(2,1)}) custom-call(bf16[2,1024,768]{2,1,0:T(8,128)(2,1)} %after.21.rows, bf16[4,768,384]{2,1,0:T(8,128)(2,1)} %bitcast.255, bf16[4,384,768]{2,1,0:T(8,128)(2,1)} %bitcast.257), custom_call_target="tpu_custom_call" | custom-call | flops 75497472 | bytes 221184 | tf_op jit(solution)/shard_map/expert_forward/pallas_call | solution.py:432
  234.0 19.2 %expert_back.3 = (bf16[1024,768]{1,0:T(8,128)(2,1)S(1)}, bf16[4,768,384]{2,1,0:T(8,128)(2,1)}, bf16[4,384,768]{2,1,0:T(8,128)(2,1)}) custom-call(bf16[2,1024,768]{2,1,0:T(8,128)(2,1)} %bitcast.252, bf16[2,1024,768]{2,1,0:T(8,128)(2,1)} %bitcast.254, bf16[4,768,384]{2,1,0:T(8,128)(2,1)} %bitcast.256, bf16[4,384,768]{2,1,0:T(8,128)(2,1)} %bitcast.258, ...), custom_call_target="tpu_custom_call" | custom-call | flops 150994944 | bytes 319488 | tf_op jit(solution)/shard_map/expert_back/pallas_call | solution.py:478
  258.8 8.1 %place_rows.1 = bf16[4,512,1536]{2,1,0:T(8,128)(2,1)} custom-call(bf16[4,512,512]{2,1,0:T(8,128)(2,1)} %compare_convert_fusion.hot, bf16[1024,768]{1,0:T(8,128)(2,1)} %copy-done.2, bf16[1024,768]{1,0:T(8,128)(2,1)} %copy-done.5, bf16[512,768]{1,0:T(8,128)(2,1)S(1)} %collective-permute-done.21.refs_2_, bf16[512,768]{1,0:T(8,128)(2,1)S(1)} %collective-permute-done.22.refs_3_, ...), custom_call_target="tpu_custom_call" | custom-call | flops 50331648 | bytes 196608 | tf_op jit(solution)/shard_map/place_rows/pallas_call | solution.py:514
  273.1 33.5 %collective-permute-done.26.refs_1_ = bf16[2,256,1536]{2,1,0:T(8,128)(2,1)S(1)} collective-permute-done((bf16[2,256,1536]{2,1,0:T(8,128)(2,1)S(1)}, bf16[2,256,1536]{2,1,0:T(8,128)(2,1)S(1)}, u32[]{:S(2)}, u32[]{:S(2)}) %collective-permute-start.26) | collective-permute-done | bytes 1572896 | tf_op jit(solution)/shard_map/ppermute | solution.py:91
  309.0 3.4 add_convert_fusion.1
  316.0 15.5 %collective-permute-done.27.refs_0_ = bf16[1,256,1536]{2,1,0:T(8,128)(2,1)} collective-permute-done((bf16[1,256,1536]{2,1,0:T(8,128)(2,1)}, bf16[1,256,1536]{2,1,0:T(8,128)(2,1)}, u32[]{:S(2)}, u32[]{:S(2)}) %collective-permute-start.27) | collective-permute-done | bytes 786464 | tf_op jit(solution)/shard_map/ppermute | solution.py:91
  342.8 16.5 %attend_back.1 = (bf16[512,768]{1,0:T(8,128)(2,1)S(1)}, bf16[512,768]{1,0:T(8,128)(2,1)S(1)}, bf16[512,768]{1,0:T(8,128)(2,1)}, f32[12,8,1024]{2,1,0:T(8,128)S(1)}) custom-call(bf16[512,2304]{1,0:T(8,128)(2,1)} %convolution_convert_fusion.1.query.key.value, bf16[512,2304]{1,0:T(8,128)(2,1)} %convolution_convert_fusion.1.query.key.value, ...), custom_call_target="tpu_custom_call" | custom-call | flops 100663296 | bytes 184320 | tf_op jit(solution)/shard_map/attend_back/pallas_call | solution.py:365
  374.3 2.6 fusion
  380.7 3.9 fusion.36
  386.7 6.0 %collective-permute-done.31.refs_1_ = bf16[4,2,24,1152]{3,2,1,0:T(8,128)(2,1)} collective-permute-done((bf16[4,2,24,1152]{3,2,1,0:T(8,128)(2,1)}, bf16[4,2,24,1152]{3,2,1,0:T(8,128)(2,1)}, u32[]{:S(2)}, u32[]{:S(2)}) %collective-permute-start.31) | collective-permute-done | bytes 442400 | tf_op jit(solution)/shard_map/ppermute | solution.py:91
  401.8 3.5 collective-permute-done.36.refs_1_
  411.3 2.8 collective-permute-start.47
  417.6 2.9 collective-permute-start.44
  423.8 3.8 collective-permute-start.41
  430.7 8.4 %collective-permute-done.40.refs_1_ = bf16[24,1152]{1,0:T(8,128)(2,1)S(1)} collective-permute-done((bf16[24,1152]{1,0:T(8,128)(2,1)S(1)}, bf16[24,1152]{1,0:T(8,128)(2,1)S(1)}, u32[]{:S(2)}, u32[]{:S(2)}) %collective-permute-start.40) | collective-permute-done | bytes 55328 | tf_op jit(solution)/shard_map/ppermute | solution.py:106
  441.0 5.2 %collective-permute-start.49 = (f32[9,128]{1,0:T(8,128)S(1)}, f32[9,128]{1,0:T(8,128)S(1)}, u32[]{:S(2)}, u32[]{:S(2)}) collective-permute-start(f32[9,128]{1,0:T(8,128)S(1)} %add.418), channel_id=1, source_target_pairs={{0,24},{4,28},{8,0},{12,4},{16,8},{20,12},{24,16},{28,20},{1,25},{... | collective-permute-start | bytes 13832 | tf_op jit(solution)/shard_map/ppermute | solution.py:106
  450.2 2.7 maximum_convert_fusion.1
  (538 shorter events, 169.0 us)
Async XLA Ops:
  7.3 149.6 %all-gather.7.cloned.1.call-start = ((), (), s32[]{:S(2)}) async-start(), calls=%async_computation.4 | async-start | bytes 2949120 | tf_op jit(solution)/shard_map/all_gather | solution.py:584
  9.8 147.1 %all-gather.9.cloned.1.call-start = ((), (), s32[]{:S(2)}) async-start(), calls=%async_computation.5 | async-start | bytes 2949120 | tf_op jit(solution)/shard_map/all_gather | solution.py:584
  10.2 13.4 %collective-permute-start = (bf16[24,3200]{1,0:T(8,128)(2,1)S(1)}, bf16[24,3200]{1,0:T(8,128)(2,1)S(1)}, u32[]{:S(2)}, u32[]{:S(2)}) collective-permute-start(bf16[24,3200]{1,0:T(8,128)(2,1)S(1)} %concatenate.147), channel_id=1, source_target_pairs={{0,24},{4,28},{8,0},{12,4},{16,8},{20,12},{24,16},{28,20},{1,25},{... | collective-permute-start | bytes 460808 | tf_op jit(solution)/shard_map/ppermute | solution.py:106
  15.2 22.5 %collective-permute-start.1 = (bf16[24,3200]{1,0:T(8,128)(2,1)S(1)}, bf16[24,3200]{1,0:T(8,128)(2,1)}, u32[]{:S(2)}, u32[]{:S(2)}) collective-permute-start(bf16[24,3200]{1,0:T(8,128)(2,1)S(1)} %concatenate.147), channel_id=1, source_target_pairs={{0,16},{4,20},{8,24},{12,28},{16,0},{20,4},{24,8},{28,12},{1,17},{... | collective-permute-start | bytes 460808 | tf_op jit(solution)/shard_map/ppermute | solution.py:106
  15.2 23.4 %collective-permute-start.2 = (bf16[24,3200]{1,0:T(8,128)(2,1)S(1)}, bf16[24,3200]{1,0:T(8,128)(2,1)}, u32[]{:S(2)}, u32[]{:S(2)}) collective-permute-start(bf16[24,3200]{1,0:T(8,128)(2,1)S(1)} %concatenate.147), channel_id=1, source_target_pairs={{0,8},{4,12},{8,16},{12,20},{16,24},{20,28},{24,0},{28,4},{1,9},{5... | collective-permute-start | bytes 460808 | tf_op jit(solution)/shard_map/ppermute | solution.py:106
  19.3 196.5 %all-gather.11.cloned.1.call-start = ((), (), s32[]{:S(2)}) async-start(), calls=%async_computation.10 | async-start | bytes 2949120 | tf_op jit(solution)/shard_map/all_gather | solution.py:584
  22.0 71.2 %collective-permute-start.10 = (s32[2,1,512]{2,1,0:T(1,128)}, s32[2,1,512]{2,1,0:T(1,128)}, u32[]{:S(2)}, u32[]{:S(2)}) collective-permute-start(s32[2,1,512]{2,1,0:T(1,128)} %pad_add_fusion.1), channel_id=1, source_target_pairs={{0,2},{1,3},{2,0},{3,1},{4,6},{5,7},{6,4},{7,5},{8,10},{9,11},{10,... | collective-permute-start | bytes 12296 | tf_op jit(solution)/shard_map/ppermute | solution.py:91
  92.9 128.9 %all-gather.13.cloned.1.call-start = ((), (), s32[]{:S(2)}) async-start(), calls=%async_computation.11 | async-start | bytes 2949120 | tf_op jit(solution)/shard_map/all_gather | solution.py:584
  104.1 18.9 %collective-permute-start.14 = (bf16[2,256,768]{2,1,0:T(8,128)(2,1)S(1)}, bf16[2,256,768]{2,1,0:T(8,128)(2,1)S(1)}, u32[]{:S(2)}, u32[]{:S(2)}) collective-permute-start(bf16[2,256,768]{2,1,0:T(8,128)(2,1)S(1)} %pad_maximum_fusion.8), channel_id=1, source_target_pairs={{0,4},{4,0},{8,12},{12,8},{16,20},{20,16},{24,28},{28,24},{1,5},{5... | collective-permute-start | bytes 2359304 | tf_op jit(solution)/shard_map/ppermute | solution.py:91
  106.2 18.4 %collective-permute-start.13 = (bf16[2,256,768]{2,1,0:T(8,128)(2,1)S(1)}, bf16[2,256,768]{2,1,0:T(8,128)(2,1)}, u32[]{:S(2)}, u32[]{:S(2)}) collective-permute-start(bf16[2,256,768]{2,1,0:T(8,128)(2,1)S(1)} %pad_maximum_fusion.7), channel_id=1, source_target_pairs={{0,2},{1,3},{2,0},{3,1},{4,6},{5,7},{6,4},{7,5},{8,10},{9,11},{10,... | collective-permute-start | bytes 2359304 | tf_op jit(solution)/shard_map/ppermute | solution.py:91
  130.2 21.4 %collective-permute-start.15 = (bf16[2,4,128,768]{3,2,0,1:T(8,128)(2,1)}, bf16[2,4,128,768]{3,2,0,1:T(8,128)(2,1)}, u32[]{:S(2)}, u32[]{:S(2)}) collective-permute-start(bf16[2,4,128,768]{3,2,0,1:T(8,128)(2,1)} %fusion.42), channel_id=1, source_target_pairs={{0,1},{1,0},{2,3},{3,2},{4,5},{5,4},{6,7},{7,6},{8,9},{9,8},{10,11... | collective-permute-start | bytes 4718600 | tf_op jit(solution)/shard_map/ppermute | solution.py:91
  131.4 11.7 %collective-permute-start.17 = (bf16[256,768]{1,0:T(8,128)(2,1)}, bf16[256,768]{1,0:T(8,128)(2,1)S(1)}, u32[]{:S(2)}, u32[]{:S(2)}) collective-permute-start(bf16[256,768]{1,0:T(8,128)(2,1)} %get-tuple-element.67), channel_id=1, source_target_pairs={{0,2},{1,3},{2,0},{3,1},{4,6},{5,7},{6,4},{7,5},{8,10},{9,11},{10,... | collective-permute-start | bytes 1179656 | tf_op jit(solution)/shard_map/ppermute | solution.py:91
  132.8 13.7 %collective-permute-start.16 = (bf16[256,768]{1,0:T(8,128)(2,1)}, bf16[256,768]{1,0:T(8,128)(2,1)S(1)}, u32[]{:S(2)}, u32[]{:S(2)}) collective-permute-start(bf16[256,768]{1,0:T(8,128)(2,1)} %get-tuple-element.66), channel_id=1, source_target_pairs={{0,4},{4,0},{8,12},{12,8},{16,20},{20,16},{24,28},{28,24},{1,5},{5... | collective-permute-start | bytes 1179656 | tf_op jit(solution)/shard_map/ppermute | solution.py:91
  134.7 208.0 %reduce-scatter.5.cloned.1.call-start = ((), (), s32[]{:S(2)}) async-start(), calls=%async_computation.6 | async-start | bytes 2949120 | tf_op jit(solution)/shard_map/reduce_scatter | solution.py:666
  145.2 25.1 %collective-permute-start.19 = (bf16[2,256,768]{2,1,0:T(8,128)(2,1)}, bf16[2,256,768]{2,1,0:T(8,128)(2,1)S(1)}, u32[]{:S(2)}, u32[]{:S(2)}) collective-permute-start(bf16[2,256,768]{2,1,0:T(8,128)(2,1)} %pad_maximum_fusion.10), channel_id=1, source_target_pairs={{0,4},{4,0},{8,12},{12,8},{16,20},{20,16},{24,28},{28,24},{1,5},{5... | collective-permute-start | bytes 2359304 | tf_op jit(solution)/shard_map/ppermute | solution.py:91
  147.6 22.7 %collective-permute-start.18 = (bf16[2,256,768]{2,1,0:T(8,128)(2,1)}, bf16[2,256,768]{2,1,0:T(8,128)(2,1)S(1)}, u32[]{:S(2)}, u32[]{:S(2)}) collective-permute-start(bf16[2,256,768]{2,1,0:T(8,128)(2,1)} %pad_maximum_fusion.9), channel_id=1, source_target_pairs={{0,2},{1,3},{2,0},{3,1},{4,6},{5,7},{6,4},{7,5},{8,10},{9,11},{10,... | collective-permute-start | bytes 2359304 | tf_op jit(solution)/shard_map/ppermute | solution.py:91
  201.1 141.7 %reduce-scatter.7.cloned.1.call-start = ((), (), s32[]{:S(2)}) async-start(), calls=%async_computation.7 | async-start | bytes 2949120 | tf_op jit(solution)/shard_map/reduce_scatter | solution.py:666
  201.7 247.7 %reduce-scatter.9.cloned.1.call-start = ((), (), s32[]{:S(2)}) async-start(), calls=%async_computation.8 | async-start | bytes 2949120 | tf_op jit(solution)/shard_map/reduce_scatter | solution.py:666
  215.6 41.0 %collective-permute-start.21 = (bf16[512,768]{1,0:T(8,128)(2,1)}, bf16[512,768]{1,0:T(8,128)(2,1)S(1)}, u32[]{:S(2)}, u32[]{:S(2)}) collective-permute-start(bf16[512,768]{1,0:T(8,128)(2,1)} %slice.179), channel_id=1, source_target_pairs={{0,1},{1,0},{2,3},{3,2},{4,5},{5,4},{6,7},{7,6},{8,9},{9,8},{10,11... | collective-permute-start | bytes 2359304 | tf_op jit(solution)/shard_map/ppermute | solution.py:91
  270.1 36.5 %collective-permute-start.26 = (bf16[2,256,1536]{2,1,0:T(8,128)(2,1)S(1)}, bf16[2,256,1536]{2,1,0:T(8,128)(2,1)S(1)}, u32[]{:S(2)}, u32[]{:S(2)}) collective-permute-start(bf16[2,256,1536]{2,1,0:T(8,128)(2,1)S(1)} %pad_maximum_fusion.6), channel_id=1, source_target_pairs={{0,4},{4,0},{8,12},{12,8},{16,20},{20,16},{24,28},{28,24},{1,5},{5... | collective-permute-start | bytes 4718600 | tf_op jit(solution)/shard_map/ppermute | solution.py:91
  271.7 36.2 %collective-permute-start.25 = (bf16[2,256,1536]{2,1,0:T(8,128)(2,1)S(1)}, bf16[2,256,1536]{2,1,0:T(8,128)(2,1)S(1)}, u32[]{:S(2)}, u32[]{:S(2)}) collective-permute-start(bf16[2,256,1536]{2,1,0:T(8,128)(2,1)S(1)} %stack.331), channel_id=1, source_target_pairs={{0,2},{1,3},{2,0},{3,1},{4,6},{5,7},{6,4},{7,5},{8,10},{9,11},{10,... | collective-permute-start | bytes 4718600 | tf_op jit(solution)/shard_map/ppermute | solution.py:91
  312.4 19.1 %collective-permute-start.27 = (bf16[1,256,1536]{2,1,0:T(8,128)(2,1)}, bf16[1,256,1536]{2,1,0:T(8,128)(2,1)}, u32[]{:S(2)}, u32[]{:S(2)}) collective-permute-start(bf16[1,256,1536]{2,1,0:T(8,128)(2,1)} %get-tuple-element.158), channel_id=1, source_target_pairs={{0,4},{4,0},{8,12},{12,8},{16,20},{20,16},{24,28},{28,24},{1,5},{5... | collective-permute-start | bytes 2359304 | tf_op jit(solution)/shard_map/ppermute | solution.py:91
  313.8 18.9 %collective-permute-start.28 = (bf16[1,256,1536]{2,1,0:T(8,128)(2,1)}, bf16[1,256,1536]{2,1,0:T(8,128)(2,1)}, u32[]{:S(2)}, u32[]{:S(2)}) collective-permute-start(bf16[1,256,1536]{2,1,0:T(8,128)(2,1)} %get-tuple-element.157), channel_id=1, source_target_pairs={{0,2},{1,3},{2,0},{3,1},{4,6},{5,7},{6,4},{7,5},{8,10},{9,11},{10,... | collective-permute-start | bytes 2359304 | tf_op jit(solution)/shard_map/ppermute | solution.py:91
  316.0 133.4 %reduce-scatter.11.cloned.1.call-start = ((), (), s32[]{:S(2)}) async-start(), calls=%async_computation.9 | async-start | bytes 2949120 | tf_op jit(solution)/shard_map/reduce_scatter | solution.py:666
  372.8 12.8 %collective-permute-start.33 = (bf16[4,2,24,896]{3,2,1,0:T(8,128)(2,1)}, bf16[4,2,24,896]{3,2,1,0:T(8,128)(2,1)}, u32[]{:S(2)}, u32[]{:S(2)}) collective-permute-start(bf16[4,2,24,896]{3,2,1,0:T(8,128)(2,1)} %copy_bitcast_fusion.5), channel_id=1, source_target_pairs={{0,2},{1,3},{2,0},{3,1},{4,6},{5,7},{6,4},{7,5},{8,10},{9,11},{10,... | collective-permute-start | bytes 1032200 | tf_op jit(solution)/shard_map/ppermute | solution.py:91
  378.7 14.0 %collective-permute-start.31 = (bf16[4,2,24,1152]{3,2,1,0:T(8,128)(2,1)}, bf16[4,2,24,1152]{3,2,1,0:T(8,128)(2,1)}, u32[]{:S(2)}, u32[]{:S(2)}) collective-permute-start(bf16[4,2,24,1152]{3,2,1,0:T(8,128)(2,1)} %copy_bitcast_fusion.2), channel_id=1, source_target_pairs={{0,2},{1,3},{2,0},{3,1},{4,6},{5,7},{6,4},{7,5},{8,10},{9,11},{10,... | collective-permute-start | bytes 1327112 | tf_op jit(solution)/shard_map/ppermute | solution.py:91
  380.1 12.6 %collective-permute-start.30 = (bf16[4,2,24,1152]{3,2,1,0:T(8,128)(2,1)}, bf16[4,2,24,1152]{3,2,1,0:T(8,128)(2,1)}, u32[]{:S(2)}, u32[]{:S(2)}) collective-permute-start(bf16[4,2,24,1152]{3,2,1,0:T(8,128)(2,1)} %copy_bitcast_fusion.3), channel_id=1, source_target_pairs={{0,4},{4,0},{8,12},{12,8},{16,20},{20,16},{24,28},{28,24},{1,5},{5... | collective-permute-start | bytes 1327112 | tf_op jit(solution)/shard_map/ppermute | solution.py:91
  416.3 14.3 %collective-permute-start.43 = (bf16[24,1152]{1,0:T(8,128)(2,1)S(1)}, bf16[24,1152]{1,0:T(8,128)(2,1)S(1)}, u32[]{:S(2)}, u32[]{:S(2)}) collective-permute-start(bf16[24,1152]{1,0:T(8,128)(2,1)S(1)} %get-tuple-element.186), channel_id=1, source_target_pairs={{0,16},{4,20},{8,24},{12,28},{16,0},{20,4},{24,8},{28,12},{1,17},{... | collective-permute-start | bytes 165896 | tf_op jit(solution)/shard_map/ppermute | solution.py:106
  417.6 13.1 %collective-permute-start.44 = (bf16[24,1152]{1,0:T(8,128)(2,1)S(1)}, bf16[24,1152]{1,0:T(8,128)(2,1)S(1)}, u32[]{:S(2)}, u32[]{:S(2)}) collective-permute-start(bf16[24,1152]{1,0:T(8,128)(2,1)S(1)} %get-tuple-element.185), channel_id=1, source_target_pairs={{0,24},{4,28},{8,0},{12,4},{16,8},{20,12},{24,16},{28,20},{1,25},{... | collective-permute-start | bytes 165896 | tf_op jit(solution)/shard_map/ppermute | solution.py:106
  421.4 17.6 %collective-permute-start.40 = (bf16[24,1152]{1,0:T(8,128)(2,1)S(1)}, bf16[24,1152]{1,0:T(8,128)(2,1)S(1)}, u32[]{:S(2)}, u32[]{:S(2)}) collective-permute-start(bf16[24,1152]{1,0:T(8,128)(2,1)S(1)} %get-tuple-element.189), channel_id=1, source_target_pairs={{0,16},{4,20},{8,24},{12,28},{16,0},{20,4},{24,8},{28,12},{1,17},{... | collective-permute-start | bytes 165896 | tf_op jit(solution)/shard_map/ppermute | solution.py:106
  423.8 15.2 %collective-permute-start.41 = (bf16[24,1152]{1,0:T(8,128)(2,1)S(1)}, bf16[24,1152]{1,0:T(8,128)(2,1)S(1)}, u32[]{:S(2)}, u32[]{:S(2)}) collective-permute-start(bf16[24,1152]{1,0:T(8,128)(2,1)S(1)} %get-tuple-element.188), channel_id=1, source_target_pairs={{0,24},{4,28},{8,0},{12,4},{16,8},{20,12},{24,16},{28,20},{1,25},{... | collective-permute-start | bytes 165896 | tf_op jit(solution)/shard_map/ppermute | solution.py:106
  441.0 15.0 %collective-permute-start.49 = (f32[9,128]{1,0:T(8,128)S(1)}, f32[9,128]{1,0:T(8,128)S(1)}, u32[]{:S(2)}, u32[]{:S(2)}) collective-permute-start(f32[9,128]{1,0:T(8,128)S(1)} %add.418), channel_id=1, source_target_pairs={{0,24},{4,28},{8,0},{12,4},{16,8},{20,12},{24,16},{28,20},{1,25},{... | collective-permute-start | bytes 13832 | tf_op jit(solution)/shard_map/ppermute | solution.py:106
  (155 other events, 946.2 us)
Sparse Core Ops, SparseCore 0:
  9.9 57.0 all-gather.6
  68.6 51.4 all-gather.8
  121.7 49.2 all-gather.10
  172.4 49.3 all-gather.12
  224.5 46.8 reduce-scatter.4
  273.6 47.5 reduce-scatter.6
  323.4 47.5 reduce-scatter.8
  385.8 56.6 reduce-scatter.10
